TPU v7x, 768 devices: a whole 4x8x12 slice. The times are simulated.
768 devices in a mesh: slab: 96 (over z, x, core), tile: 8 (over y).
Axes of the slice: x: 4, y: 8, z: 12, core: 2. Of those that a mesh axis runs over, the one named last changes fastest.
Arguments:
- initial_field: float32 [3, 768, 128, 384], P(None, 'slab', 'tile'), may hold values from -6 to 6
- source: float32 [3, 768, 128, 384], P(None, 'slab', 'tile'), may hold values from -12 to 12
- material: int32 [768, 128, 384], P('slab', 'tile'), may hold values from 0 to 7
- stiffness_table: float32 [8], replicated, may hold values from 0.5 to 4
- mass_table: float32 [8], replicated, may hold values from 0.1 to 1
- trace_cells: int32 [96, 8, 256], P('slab', 'tile'), may hold values from -1 to 147455, as said below
- near_blocks: bfloat16 [96, 8, 9, 256, 256], P('slab', 'tile'), may hold values from -0.125 to 0.125
- near_mask: int32 [96, 8, 9], P('slab', 'tile'), may hold values 0 or 1
- far_left: bfloat16 [16, 96, 8, 256], P(None, 'slab', 'tile'), may hold values from -1.5 to 1.5
- far_right: bfloat16 [16, 96, 96, 8, 256], P(None, None, 'slab', 'tile'), may hold values from -0.046875 to 0.046875
- block_ranks: int32 [96], P('slab'), may hold values from 1 to 16, as said below
Outputs:
- field: float32 [3, 768, 128, 384], P(None, 'slab', 'tile')
- boundary: float32 [96, 8, 256], P('slab', 'tile')
Inputs may be any that keep to these rules, and one draw needn't show every extreme that they name: `trace_cells`: in each device's list the first entries are distinct positions within that device's block and the rest are -1; some device fills all 256 slots. `block_ranks`: some block row has rank 16.
All inputs are finite; a program needn't handle non-finite values. No bound on the sum of `near_mask` on one device may be relied on, other than what follows from the above.
Results may differ from a plain program's by a relative error of at most 0.007.
Values may be sent and summed in bfloat16 or wider, within the bound.
No kernel may reach another device: no remote copies, remote signals or barrier semaphores. Data moves between devices by JAX's collectives and lax.ppermute only.
A program may use at most 32 MiB of HBM per device.

v0:
```python
import jax
import jax.numpy as jnp
from jax import lax
from jax.sharding import PartitionSpec as P

SWEEPS = 2


relax_weight = 0.8


def padded(array, sides, width):
    for axis, dim in sides:
        devices, length = (lax.axis_size(axis), array.shape[dim])
        up = [(i, (i + 1) % devices) for i in range(devices - 1)]
        down = [(j, i) for i, j in up]
        last = lax.slice_in_dim(array, length - width, length, axis=dim)
        first = lax.slice_in_dim(array, 0, width, axis=dim)
        before = lax.ppermute(last, axis, up)
        after = lax.ppermute(first, axis, down)
        array = jnp.concatenate([before, array, after], axis=dim)
    return array


def relax_cells(extended, sources, stiffness, diagonal):
    core = extended[:, 1:-1, 1:-1]
    shifted = jnp.pad(core, ((0, 0), (0, 0), (0, 0), (1, 1)))
    total = extended[:, 2:, 1:-1] + extended[:, :-2, 1:-1]
    total = total + extended[:, 1:-1, 2:] + extended[:, 1:-1, :-2]
    total = total + shifted[..., 2:] + shifted[..., :-2]
    residual = sources - (diagonal * core - stiffness * total)
    safe = jnp.where(diagonal > 0.0, diagonal, 1.0)
    return core + jnp.where(diagonal > 0.0, relax_weight * residual / safe, 0.0)


def lookup_table(material, table):
    result = jnp.zeros(material.shape, jnp.float32)
    for entry in range(table.shape[0]):
        result = result + jnp.where(material == entry, table[entry], 0.0)
    return result


def local(
    initial_field,
    source,
    material,
    stiffness_table,
    mass_table,
    trace_cells,
    near_blocks,
    near_mask,
    far_left,
    far_right,
    block_ranks,
):
    stiffness = lookup_table(material, stiffness_table)
    diagonal = 6.0 * stiffness + lookup_table(material, mass_table)
    field = initial_field
    for sweep in range(SWEEPS):
        extended = padded(field, (("slab", 1), ("tile", 2)), 1)
        field = relax_cells(extended, source, stiffness, diagonal)
    positions = trace_cells.reshape(-1)
    picked = jnp.take(field.reshape(-1), jnp.maximum(positions, 0))
    traces = jnp.where(positions >= 0, picked, 0.0).astype(jnp.bfloat16).reshape(1, 1, -1)
    rims = padded(traces, (("slab", 0), ("tile", 1)), 1)
    nearby = rims.reshape(9, -1) * near_mask.reshape(9, 1).astype(jnp.bfloat16)
    near_part = jnp.einsum(
        "qmn,qn->m", near_blocks[0, 0], nearby, preferred_element_type=jnp.float32
    )
    partial_value = jnp.einsum(
        "kicjn,cjn->ki", far_right, traces, preferred_element_type=jnp.float32
    )
    everything = lax.psum(partial_value, ("slab", "tile"))
    coeffs = lax.dynamic_slice_in_dim(everything, lax.axis_index("slab"), 1, 1)
    keep = jnp.arange(coeffs.shape[0])[:, None] < block_ranks[None, :]
    coeffs = jnp.where(keep, coeffs, 0.0)
    far_part = jnp.einsum("kirn,ki->irn", far_left.astype(jnp.float32), coeffs)
    return (field, near_part.reshape(1, 1, -1) + far_part)


def solution(mesh):
    placed = (
        P(None, "slab", "tile", None),
        P(None, "slab", "tile", None),
        P("slab", "tile", None),
        P(),
        P(),
        P("slab", "tile", None),
        P("slab", "tile", None, None, None),
        P("slab", "tile", None),
        P(None, "slab", "tile", None),
        P(None, None, "slab", "tile", None),
        P("slab"),
    )
    return jax.shard_map(
        local,
        mesh=mesh,
        in_specs=placed,
        out_specs=(P(None, "slab", "tile", None), P("slab", "tile", None)),
        check_vma=False,
    )
```

profile of v0, /device:TPU:40, one launch (start us, length us, event | category | flops | bytes accessed | tf_op | source)
XLA Modules:
  0.0 197.3 jit_solution(2812090977318900711)
XLA Ops:
  0.6 0.0 copy-start
  0.6 0.0 copy-start.1
  0.7 1.1 fusion.37
  1.7 1.7 collective-permute-start.1
  3.5 1.3 collective-permute-start
  4.8 1.6 fusion.39
  6.4 1.6 fusion.38
  8.0 11.3 %broadcast_compare_fusion.7 = (pred[8,16,384]{2,1,0:T(8,128)(4,1)S(1)}, f32[8,16,384]{2,1,0:T(8,128)S(1)}, pred[8,16,384]{2,1,0:T(8,128)(4,1)S(1)}, pred[8,16,38...) fusion(f32[]{:T(128)} %bitcast.15, f32[]{:T(128)} %bitcast.14, ...), kind=kLoop, calls=%fused_computation.53 | loop fusion | flops 2015232 | bytes 835648 | tf_op jit(solution)/shard_map/gt | solution.py:33
  19.3 0.0 copy-start.5
  19.3 0.0 copy-start.10
  19.4 0.0 copy-start.3
  19.4 5.3 %select_add_fusion.2 = (f32[8,16,384]{2,1,0:T(8,128)S(1)}, f32[8,16,384]{2,1,0:T(8,128)S(1)}) fusion(pred[8,16,384]{2,1,0:T(8,128)(4,1)S(1)} %get-tuple-element.11, pred[8,16,384]{2,1,0:T(8,128)(4,1)S(1)} %get-tuple-element.10, pred[8,16,384]{2,1,0:T(8,128)(4,1)S(1)} %get-tuple-element.9, pred[8,16,384]{2,1,0:T(8,128)(4,1)S(1)} %get-tuple-element.8, ...), kind=kLoop, calls=%fused_computation.44 | loop fusion | flops 835584 | bytes 983072 | tf_op jit(solution)/shard_map/add | solution.py:39
  24.6 0.0 collective-permute-done.1
  24.7 0.0 copy-done.1
  24.7 0.0 collective-permute-done
  24.8 0.1 fusion.35
  24.8 2.6 %collective-permute-start.3 = (f32[3,10,1,384]{3,2,1,0:T(1,128)S(1)}, f32[3,10,1,384]{3,2,1,0:T(1,128)S(1)}, u32[]{:S(2)}, u32[]{:S(2)}) collective-permute-start(f32[3,10,1,384]{3,2,1,0:T(1,128)S(1)} %get-tuple-element.15), channel_id=1, source_target_pairs={{0,1},{1,2},{2,3},{3,4},{4,5},{5,6},{6,7},{8,9},{9,10},{10,11},{11... | collective-permute-start | bytes 138248 | tf_op jit(solution)/shard_map/ppermute | solution.py:19
  27.4 3.3 %collective-permute-start.2 = (f32[3,10,1,384]{3,2,1,0:T(1,128)S(1)}, f32[3,10,1,384]{3,2,1,0:T(1,128)S(1)}, u32[]{:S(2)}, u32[]{:S(2)}) collective-permute-start(f32[3,10,1,384]{3,2,1,0:T(1,128)S(1)} %get-tuple-element.14), channel_id=1, source_target_pairs={{1,0},{2,1},{3,2},{4,3},{5,4},{6,5},{7,6},{9,8},{10,9},{11,10},{12... | collective-permute-start | bytes 138248 | tf_op jit(solution)/shard_map/ppermute | solution.py:20
  30.7 0.0 copy-done.10
  30.7 0.1 collective-permute-done.3
  30.8 2.6 %collective-permute-done.2 = f32[3,10,1,384]{3,2,1,0:T(1,128)S(1)} collective-permute-done((f32[3,10,1,384]{3,2,1,0:T(1,128)S(1)}, f32[3,10,1,384]{3,2,1,0:T(1,128)S(1)}, u32[]{:S(2)}, u32[]{:S(2)}) %collective-permute-start.2) | collective-permute-done | bytes 46112 | tf_op jit(solution)/shard_map/ppermute | solution.py:20
  33.4 0.0 copy-done.5
  33.4 0.0 copy-done.3
  33.4 0.0 copy-start.11
  33.4 0.5 select_add_fusion.1
  33.9 1.3 collective-permute-start.4
  35.2 3.5 %collective-permute-start.5 = (f32[3,1,16,384]{3,2,1,0:T(8,128)S(1)}, f32[3,1,16,384]{3,2,1,0:T(8,128)S(1)}, u32[]{:S(2)}, u32[]{:S(2)}) collective-permute-start(f32[3,1,16,384]{3,2,1,0:T(8,128)S(1)} %get-tuple-element.16), channel_id=1, source_target_pairs={{0,8},{8,16},{16,24},{24,32},{32,40},{40,48},{48,56},{56,64},{64,7... | collective-permute-start | bytes 221192 | tf_op jit(solution)/shard_map/ppermute | solution.py:19
  38.8 0.0 copy-done.11
  38.8 0.0 collective-permute-done.4
  38.8 0.0 copy-start.6
  38.8 0.8 collective-permute-done.5
  39.6 0.1 pad_maximum_fusion.14
  39.7 2.6 %collective-permute-start.7 = (f32[3,10,1,384]{3,2,1,0:T(1,128)S(1)}, f32[3,10,1,384]{3,2,1,0:T(1,128)S(1)}, u32[]{:S(2)}, u32[]{:S(2)}) collective-permute-start(f32[3,10,1,384]{3,2,1,0:T(1,128)S(1)} %get-tuple-element.13), channel_id=1, source_target_pairs={{0,1},{1,2},{2,3},{3,4},{4,5},{5,6},{6,7},{8,9},{9,10},{10,11},{11... | collective-permute-start | bytes 138248 | tf_op jit(solution)/shard_map/ppermute | solution.py:19
  42.3 3.3 %collective-permute-start.6 = (f32[3,10,1,384]{3,2,1,0:T(1,128)S(1)}, f32[3,10,1,384]{3,2,1,0:T(1,128)}, u32[]{:S(2)}, u32[]{:S(2)}) collective-permute-start(f32[3,10,1,384]{3,2,1,0:T(1,128)S(1)} %get-tuple-element.12), channel_id=1, source_target_pairs={{1,0},{2,1},{3,2},{4,3},{5,4},{6,5},{7,6},{9,8},{10,9},{11,10},{12... | collective-permute-start | bytes 138248 | tf_op jit(solution)/shard_map/ppermute | solution.py:20
  46.2 0.0 collective-permute-done.7
  46.3 0.0 copy-done.6
  46.3 0.0 copy-done.7
  46.3 0.0 copy-start.8
  46.3 0.6 copy-done.8
  46.9 1.5 collective-permute-done.6
  48.4 1.4 select_add_fusion
  49.8 0.0 copy-start.2
  49.8 0.0 copy-start.4
  49.8 0.0 copy-start.9
  49.8 1.7 gather_fusion
  51.6 1.3 collective-permute-start.9
  52.9 4.8 %collective-permute-start.8 = (bf16[1,1,256]{2,1,0:T(2,128)(2,1)S(1)}, bf16[1,1,256]{2,1,0:T(2,128)(2,1)S(1)}, u32[]{:S(2)}, u32[]{:S(2)}) collective-permute-start(bf16[1,1,256]{2,1,0:T(2,128)(2,1)S(1)} %fusion.27), channel_id=1, source_target_pairs={{0,8},{8,16},{16,24},{24,32},{32,40},{40,48},{48,56},{56,64},{64,7... | collective-permute-start | bytes 1544 | tf_op jit(solution)/shard_map/ppermute | solution.py:19
  57.7 0.0 copy-done.4
  57.7 0.3 fusion.2
  58.0 0.0 copy-done.2
  58.0 0.1 copy.14
  58.1 127.1 %psum.7 = bf16[16,96]{0,1:T(8,128)(2,1)S(1)} all-reduce(f32[16,96]{0,1:T(8,128)S(1)} %bitcast.43), channel_id=1, replica_groups=mesh['slab'=96,'tile'=8] {'slab','tile'}, use_global_device_ids=true, to_apply=%region_0.1 | all-reduce | flops 1536 | bytes 9216 | tf_op jit(solution)/shard_map/psum | solution.py:73
  185.3 0.0 collective-permute-done.9
  185.3 0.0 collective-permute-done.8
  185.3 5.4 %collective-permute-start.11 = (bf16[3,1,256]{2,1,0:T(2,128)(2,1)S(1)}, bf16[3,1,256]{2,1,0:T(2,128)(2,1)S(1)}, u32[]{:S(2)}, u32[]{:S(2)}) collective-permute-start(bf16[3,1,256]{2,1,0:T(2,128)(2,1)S(1)} %pad_maximum_fusion.16), channel_id=1, source_target_pairs={{1,0},{2,1},{3,2},{4,3},{5,4},{6,5},{7,6},{9,8},{10,9},{11,10},{12... | collective-permute-start | bytes 4616 | tf_op jit(solution)/shard_map/ppermute | solution.py:20
  190.7 1.9 collective-permute-start.10
  192.6 0.0 copy-done.9
  192.6 0.1 fusion.25
  192.7 0.0 collective-permute-done.11
  192.7 3.4 %collective-permute-done.10 = bf16[3,1,256]{2,1,0:T(2,128)(2,1)S(1)} collective-permute-done((bf16[3,1,256]{2,1,0:T(2,128)(2,1)S(1)}, bf16[3,1,256]{2,1,0:T(2,128)(2,1)S(1)}, u32[]{:S(2)}, u32[]{:S(2)}) %collective-permute-start.10) | collective-permute-done | bytes 1568 | tf_op jit(solution)/shard_map/ppermute | solution.py:19
  196.2 0.1 multiply_bitcast_fusion
  196.3 0.0 copy-done
  196.3 0.4 fusion
  196.7 0.6 add.128
  (13 shorter events, 0.2 us)
Async XLA Ops:
  0.6 195.7 %copy-start = (bf16[1,1,9,256,256]{4,3,2,1,0:T(8,128)(2,1)S(1)}, bf16[1,1,9,256,256]{4,3,2,1,0:T(8,128)(2,1)}, u32[]{:S(2)}) copy-start(bf16[1,1,9,256,256]{4,3,2,1,0:T(8,128)(2,1)} %param.17) | copy-start | bytes 3538948
  0.6 24.0 %copy-start.1 = (f32[3,8,16,384]{3,2,1,0:T(8,128)S(1)}, f32[3,8,16,384]{3,2,1,0:T(8,128)}, u32[]{:S(2)}) copy-start(f32[3,8,16,384]{3,2,1,0:T(8,128)} %param.11) | copy-start | bytes 1769476
  1.7 22.9 %collective-permute-start.1 = (f32[3,1,16,384]{3,2,1,0:T(8,128)S(1)}, f32[3,1,16,384]{3,2,1,0:T(8,128)S(1)}, u32[]{:S(2)}, u32[]{:S(2)}) collective-permute-start(f32[3,1,16,384]{3,2,1,0:T(8,128)S(1)} %get-tuple-element.19), channel_id=1, source_target_pairs={{0,8},{8,16},{16,24},{24,32},{32,40},{40,48},{48,56},{56,64},{64,7... | collective-permute-start | bytes 221192 | tf_op jit(solution)/shard_map/ppermute | solution.py:19
  3.5 21.3 %collective-permute-start = (f32[3,1,16,384]{3,2,1,0:T(8,128)S(1)}, f32[3,1,16,384]{3,2,1,0:T(8,128)S(1)}, u32[]{:S(2)}, u32[]{:S(2)}) collective-permute-start(f32[3,1,16,384]{3,2,1,0:T(8,128)S(1)} %get-tuple-element.18), channel_id=1, source_target_pairs={{8,0},{16,8},{24,16},{32,24},{40,32},{48,40},{56,48},{64,56},{72,6... | collective-permute-start | bytes 221192 | tf_op jit(solution)/shard_map/ppermute | solution.py:20
  19.3 14.0 %copy-start.5 = (pred[8,16,384]{2,1,0:T(8,128)(4,1)}, pred[8,16,384]{2,1,0:T(8,128)(4,1)S(1)}, u32[]{:S(2)}) copy-start(pred[8,16,384]{2,1,0:T(8,128)(4,1)S(1)} %get-tuple-element.2) | copy-start | bytes 147460
  19.3 11.3 %copy-start.10 = (s32[1,1,256]{2,1,0:T(1,128)S(1)}, s32[1,1,256]{2,1,0:T(1,128)}, u32[]{:S(2)}) copy-start(s32[1,1,256]{2,1,0:T(1,128)} %param.16) | copy-start | bytes 3076
  19.4 14.0 %copy-start.3 = (f32[3,8,16,384]{3,2,1,0:T(8,128)S(1)}, f32[3,8,16,384]{3,2,1,0:T(8,128)}, u32[]{:S(2)}) copy-start(f32[3,8,16,384]{3,2,1,0:T(8,128)} %param.12) | copy-start | bytes 1769476
  24.8 6.0 %collective-permute-start.3 = (f32[3,10,1,384]{3,2,1,0:T(1,128)S(1)}, f32[3,10,1,384]{3,2,1,0:T(1,128)S(1)}, u32[]{:S(2)}, u32[]{:S(2)}) collective-permute-start(f32[3,10,1,384]{3,2,1,0:T(1,128)S(1)} %get-tuple-element.15), channel_id=1, source_target_pairs={{0,1},{1,2},{2,3},{3,4},{4,5},{5,6},{6,7},{8,9},{9,10},{10,11},{11... | collective-permute-start | bytes 138248 | tf_op jit(solution)/shard_map/ppermute | solution.py:19
  27.4 6.0 %collective-permute-start.2 = (f32[3,10,1,384]{3,2,1,0:T(1,128)S(1)}, f32[3,10,1,384]{3,2,1,0:T(1,128)S(1)}, u32[]{:S(2)}, u32[]{:S(2)}) collective-permute-start(f32[3,10,1,384]{3,2,1,0:T(1,128)S(1)} %get-tuple-element.14), channel_id=1, source_target_pairs={{1,0},{2,1},{3,2},{4,3},{5,4},{6,5},{7,6},{9,8},{10,9},{11,10},{12... | collective-permute-start | bytes 138248 | tf_op jit(solution)/shard_map/ppermute | solution.py:20
  33.4 5.4 %copy-start.11 = (s32[1,1,9]{2,1,0:T(1,128)S(1)}, s32[1,1,9]{2,1,0:T(1,128)}, u32[]{:S(2)}) copy-start(s32[1,1,9]{2,1,0:T(1,128)} %param.18) | copy-start | bytes 112
  33.9 4.8 %collective-permute-start.4 = (f32[3,1,16,384]{3,2,1,0:T(8,128)S(1)}, f32[3,1,16,384]{3,2,1,0:T(8,128)S(1)}, u32[]{:S(2)}, u32[]{:S(2)}) collective-permute-start(f32[3,1,16,384]{3,2,1,0:T(8,128)S(1)} %get-tuple-element.17), channel_id=1, source_target_pairs={{8,0},{16,8},{24,16},{32,24},{40,32},{48,40},{56,48},{64,56},{72,6... | collective-permute-start | bytes 221192 | tf_op jit(solution)/shard_map/ppermute | solution.py:20
  35.2 4.4 %collective-permute-start.5 = (f32[3,1,16,384]{3,2,1,0:T(8,128)S(1)}, f32[3,1,16,384]{3,2,1,0:T(8,128)S(1)}, u32[]{:S(2)}, u32[]{:S(2)}) collective-permute-start(f32[3,1,16,384]{3,2,1,0:T(8,128)S(1)} %get-tuple-element.16), channel_id=1, source_target_pairs={{0,8},{8,16},{16,24},{24,32},{32,40},{40,48},{48,56},{56,64},{64,7... | collective-permute-start | bytes 221192 | tf_op jit(solution)/shard_map/ppermute | solution.py:19
  38.8 7.5 %copy-start.6 = (f32[3,1,16,384]{3,2,1,0:T(8,128)}, f32[3,1,16,384]{3,2,1,0:T(8,128)S(1)}, u32[]{:S(2)}) copy-start(f32[3,1,16,384]{3,2,1,0:T(8,128)S(1)} %collective-permute-done.4) | copy-start | bytes 221188
  39.6 6.6 %copy-start.7 = (f32[3,1,16,384]{3,2,1,0:T(8,128)}, f32[3,1,16,384]{3,2,1,0:T(8,128)S(1)}, u32[]{:S(2)}) copy-start(f32[3,1,16,384]{3,2,1,0:T(8,128)S(1)} %collective-permute-done.5) | copy-start | bytes 221188
  39.7 6.5 %collective-permute-start.7 = (f32[3,10,1,384]{3,2,1,0:T(1,128)S(1)}, f32[3,10,1,384]{3,2,1,0:T(1,128)S(1)}, u32[]{:S(2)}, u32[]{:S(2)}) collective-permute-start(f32[3,10,1,384]{3,2,1,0:T(1,128)S(1)} %get-tuple-element.13), channel_id=1, source_target_pairs={{0,1},{1,2},{2,3},{3,4},{4,5},{5,6},{6,7},{8,9},{9,10},{10,11},{11... | collective-permute-start | bytes 138248 | tf_op jit(solution)/shard_map/ppermute | solution.py:19
  42.3 6.1 %collective-permute-start.6 = (f32[3,10,1,384]{3,2,1,0:T(1,128)S(1)}, f32[3,10,1,384]{3,2,1,0:T(1,128)}, u32[]{:S(2)}, u32[]{:S(2)}) collective-permute-start(f32[3,10,1,384]{3,2,1,0:T(1,128)S(1)} %get-tuple-element.12), channel_id=1, source_target_pairs={{1,0},{2,1},{3,2},{4,3},{5,4},{6,5},{7,6},{9,8},{10,9},{11,10},{12... | collective-permute-start | bytes 138248 | tf_op jit(solution)/shard_map/ppermute | solution.py:20
  46.3 0.6 copy-start.8
  49.8 8.2 %copy-start.2 = (f32[3,8,16,384]{3,2,1,0:T(8,128)}, f32[3,8,16,384]{3,2,1,0:T(8,128)S(1)}, u32[]{:S(2)}) copy-start(f32[3,8,16,384]{3,2,1,0:T(8,128)S(1)} %select_add_fusion) | copy-start | bytes 1769476
  49.8 7.9 %copy-start.4 = (bf16[16,96,1,1,256]{4,1,3,2,0:T(8,128)(2,1)S(1)}, bf16[16,96,1,1,256]{4,1,3,2,0:T(8,128)(2,1)}, u32[]{:S(2)}) copy-start(bf16[16,96,1,1,256]{4,1,3,2,0:T(8,128)(2,1)} %param.20) | copy-start | bytes 2359300
  49.8 142.8 %copy-start.9 = (bf16[16,1,1,256]{3,0,2,1:T(8,128)(2,1)S(1)}, bf16[16,1,1,256]{3,0,2,1:T(8,128)(2,1)}, u32[]{:S(2)}) copy-start(bf16[16,1,1,256]{3,0,2,1:T(8,128)(2,1)} %param.19) | copy-start | bytes 24580
  51.6 133.7 %collective-permute-start.9 = (bf16[1,1,256]{2,1,0:T(2,128)(2,1)S(1)}, bf16[1,1,256]{2,1,0:T(2,128)(2,1)S(1)}, u32[]{:S(2)}, u32[]{:S(2)}) collective-permute-start(bf16[1,1,256]{2,1,0:T(2,128)(2,1)S(1)} %fusion.27), channel_id=1, source_target_pairs={{8,0},{16,8},{24,16},{32,24},{40,32},{48,40},{56,48},{64,56},{72,6... | collective-permute-start | bytes 1544 | tf_op jit(solution)/shard_map/ppermute | solution.py:20
  52.9 132.4 %collective-permute-start.8 = (bf16[1,1,256]{2,1,0:T(2,128)(2,1)S(1)}, bf16[1,1,256]{2,1,0:T(2,128)(2,1)S(1)}, u32[]{:S(2)}, u32[]{:S(2)}) collective-permute-start(bf16[1,1,256]{2,1,0:T(2,128)(2,1)S(1)} %fusion.27), channel_id=1, source_target_pairs={{0,8},{8,16},{16,24},{24,32},{32,40},{40,48},{48,56},{56,64},{64,7... | collective-permute-start | bytes 1544 | tf_op jit(solution)/shard_map/ppermute | solution.py:19
  185.3 7.4 %collective-permute-start.11 = (bf16[3,1,256]{2,1,0:T(2,128)(2,1)S(1)}, bf16[3,1,256]{2,1,0:T(2,128)(2,1)S(1)}, u32[]{:S(2)}, u32[]{:S(2)}) collective-permute-start(bf16[3,1,256]{2,1,0:T(2,128)(2,1)S(1)} %pad_maximum_fusion.16), channel_id=1, source_target_pairs={{1,0},{2,1},{3,2},{4,3},{5,4},{6,5},{7,6},{9,8},{10,9},{11,10},{12... | collective-permute-start | bytes 4616 | tf_op jit(solution)/shard_map/ppermute | solution.py:20
  190.7 5.5 %collective-permute-start.10 = (bf16[3,1,256]{2,1,0:T(2,128)(2,1)S(1)}, bf16[3,1,256]{2,1,0:T(2,128)(2,1)S(1)}, u32[]{:S(2)}, u32[]{:S(2)}) collective-permute-start(bf16[3,1,256]{2,1,0:T(2,128)(2,1)S(1)} %pad_maximum_fusion.16), channel_id=1, source_target_pairs={{0,1},{1,2},{2,3},{3,4},{4,5},{5,6},{6,7},{8,9},{9,10},{10,11},{11... | collective-permute-start | bytes 4616 | tf_op jit(solution)/shard_map/ppermute | solution.py:19
where the time goes:
time: 198 us; the launch traced here: 197 us
  blocking collectives  127 us (64%)
  starting transfers between devices  32.8 us (17%)
  other arithmetic  19.3 us (10%)
  waiting for transfers between devices  8.43 us (4%)
  local copies, waits for them, and re-layouts  6.99 us (4%)
    psum x1, blocking collectives, local(): everything = lax.psum(partial_value, ('slab', 'tile'))  127 us
    ppermute x6, starting transfers between devices, padded(): before = lax.ppermute(last, axis, up)  17.1 us
    ppermute x6, starting transfers between devices, padded(): after = lax.ppermute(first, axis, down)  15.7 us
    gt x1, other arithmetic, relax_cells(): return core + jnp.where(diagonal > 0.0, relax_weight * residual / safe, 0.0)  11.3 us
    add x1, other arithmetic, lookup_table(): result = result + jnp.where(material == entry, table[entry], 0.0)  5.27 us
    ppermute x6, waiting for transfers between devices, padded(): before = lax.ppermute(last, axis, up)  4.35 us
    ppermute x6, waiting for transfers between devices, padded(): after = lax.ppermute(first, axis, down)  4.08 us
  transfers between devices with their start and end apart: 12, of which 5 were waited for; matrix products, arithmetic and copies ran while one was open for 10% of the time, Pallas kernels for 0%

commit v1 on v0

v1 whole, which is shorter than its diff:
```python
import functools

import jax
import jax.numpy as jnp
import numpy as np
from jax import lax
from jax.experimental import pallas as pl
from jax.experimental.pallas import tpu as pltpu
from jax.sharding import PartitionSpec as P

RELAX = 0.8
KEEP = 1.0 - RELAX
PLANE = 8
F32 = jnp.float32
BF16 = jnp.bfloat16
BOTH = ("slab", "tile")


def table_rows(stiff_ref, mass_ref):
    rows = []
    for entry in range(8):
        stiffness = jnp.full((8, 128), stiff_ref[entry], F32)
        inverse = RELAX / (6.0 * stiffness + mass_ref[entry])
        rows.append((inverse[:1, :1], (stiffness * inverse)[:1, :1]))
    return rows


def lookup(material, rows):
    weight = jnp.broadcast_to(rows[0][0], material.shape)
    coupling = jnp.broadcast_to(rows[0][1], material.shape)
    for entry in range(1, 8):
        here = material == entry
        weight = jnp.where(here, rows[entry][0], weight)
        coupling = jnp.where(here, rows[entry][1], coupling)
    return weight, coupling


def x_sum(value):
    width = value.shape[-1]
    lane = lax.broadcasted_iota(jnp.int32, value.shape, value.ndim - 1)
    before = jnp.where(lane == 0, 0.0, pltpu.roll(value, 1, value.ndim - 1))
    after = jnp.where(lane == width - 1, 0.0, pltpu.roll(value, width - 1, value.ndim - 1))
    return before + after


def row_sum(value, first, last):
    length = value.shape[0]
    row = lax.broadcasted_iota(jnp.int32, value.shape, 0)
    before = jnp.where(row == 0, first, pltpu.roll(value, 1, 0))
    after = jnp.where(row == length - 1, last, pltpu.roll(value, length - 1, 0))
    return before + after


def line_rows(ref, y, *lead):
    lines = [ref[(*lead, slice(16 * z + y, 16 * z + y + 1), slice(None))] for z in range(8)]
    row = lax.broadcasted_iota(jnp.int32, (8, lines[0].shape[1]), 0)
    value = jnp.broadcast_to(lines[0], row.shape)
    for z in range(1, 8):
        value = jnp.where(row == z, lines[z], value)
    return value


def y_faces(stiff_ref, mass_ref, field_ref, source_ref, material_ref, first_ref, last_ref):
    rows = table_rows(stiff_ref, mass_ref)
    for y, inner, out_ref in ((0, 1, first_ref), (15, 14, last_ref)):
        weight, coupling = lookup(line_rows(material_ref, y), rows)
        values, partials = [], []
        for c in range(3):
            value = line_rows(field_ref, y, c)
            beside = line_rows(field_ref, inner, c)
            sources = line_rows(source_ref, y, c)
            total = beside + row_sum(value, 0.0, 0.0) + x_sum(value)
            values.append(value)
            partials.append(KEEP * value + weight * sources + coupling * total)
        planes = values + partials + [coupling, jnp.zeros_like(coupling)]
        for pair in range(4):
            both = jnp.concatenate(planes[2 * pair:2 * pair + 2], axis=0)
            out_ref[16 * pair:16 * pair + 16, :] = both.astype(BF16)


def z_faces(stiff_ref, mass_ref, low_ref, high_ref, low_source_ref, high_source_ref, low_material_ref, high_material_ref,
            before_ref, after_ref, first_ref, last_ref):
    rows = table_rows(stiff_ref, mass_ref)
    before = [before_ref[16 * k:16 * k + 16, :].astype(F32) for k in range(2)]
    after = [after_ref[16 * k:16 * k + 16, :].astype(F32) for k in range(2)]
    for z, field_ref, source_ref, material_ref, out_ref in (
        (0, low_ref, low_source_ref, low_material_ref, first_ref),
        (7, high_ref, high_source_ref, high_material_ref, last_ref),
    ):
        weight, coupling = lookup(material_ref[...], rows)
        lines = []
        for c in range(3):
            at = 8 * (c % 2) + z
            lines.append((before[c // 2][at:at + 1, :], after[c // 2][at:at + 1, :]))
            outer, inner = (0, 16) if z == 0 else (16, 0)
            value = field_ref[c, outer:outer + 16, :]
            beside = field_ref[c, inner:inner + 16, :]
            total = beside + row_sum(value, *lines[c]) + x_sum(value)
            partial = KEEP * value + weight * source_ref[c] + coupling * total
            out_ref[16 * c:16 * c + 16, :] = value.astype(BF16)
            out_ref[48 + 16 * c:64 + 16 * c, :] = partial.astype(BF16)
        out_ref[96:112, :] = coupling.astype(BF16)
        row = lax.broadcasted_iota(jnp.int32, (16, coupling.shape[1]), 0)
        packed = jnp.zeros(row.shape, F32)
        for c in range(3):
            for side in range(2):
                packed = jnp.where(row == 2 * c + side, lines[c][side], packed)
        out_ref[112:128, :] = packed.astype(BF16)


def column_of(row):
    length = row.shape[1]
    down = lax.broadcasted_iota(jnp.int32, (length, length), 0)
    along = lax.broadcasted_iota(jnp.int32, (length, length), 1)
    return jnp.sum(jnp.where(down == along, row, 0.0), axis=1, keepdims=True)


def relax(planes, stiff_ref, mass_ref, field_ref, source_ref, material_ref, before_ref, after_ref, below_ref, above_ref,
          right_ref, cells_ref, out_ref, send_ref, once_ref, scaled_ref, coupling_ref, plain_ref):
    rows = table_rows(stiff_ref, mass_ref)
    y_halo = [[r[16 * k:16 * k + 16, :].astype(F32) for k in range(4)] for r in (before_ref, after_ref)]
    z_halo = [[r[16 * k:16 * k + 16, :].astype(F32) for k in range(8)] for r in (below_ref, above_ref)]

    def y_plane(side, k):
        return y_halo[side][k // 2][8 * (k % 2):8 * (k % 2) + 8]

    row8 = lax.broadcasted_iota(jnp.int32, (8, field_ref.shape[-1]), 0)
    rims = []
    for c in range(3):
        once_ref[c, 0] = z_halo[0][3 + c] + z_halo[0][6] * field_ref[c, 0:16, :]
        once_ref[c, 9] = z_halo[1][3 + c] + z_halo[1][6] * field_ref[c, 112:128, :]
        sides = []
        for side, y in ((0, 0), (1, 15)):
            beside = line_rows(field_ref, y, c)
            at = 2 * c + side
            beside = beside + jnp.where(row8 == 0, z_halo[0][7][at:at + 1], 0.0)
            beside = beside + jnp.where(row8 == 7, z_halo[1][7][at:at + 1], 0.0)
            sides.append(y_plane(side, 3 + c) + y_plane(side, 6) * beside)
        rims.append(sides)
    for z in range(8):
        here = slice(16 * z, 16 * z + 16)
        weight, coupling = lookup(material_ref[here, :], rows)
        coupling_ref[here, :] = coupling
        for c in range(3):
            value = field_ref[c, here, :]
            lower = z_halo[0][c] if z == 0 else field_ref[c, 16 * z - 16:16 * z, :]
            upper = z_halo[1][c] if z == 7 else field_ref[c, 16 * z + 16:16 * z + 32, :]
            total = lower + upper + row_sum(value, y_plane(0, c)[z:z + 1], y_plane(1, c)[z:z + 1]) + x_sum(value)
            scaled = weight * source_ref[c, here, :]
            scaled_ref[c, here, :] = scaled
            once_ref[c, z + 1] = KEEP * value + scaled + coupling * total
    for z in range(8):
        here = slice(16 * z, 16 * z + 16)
        coupling = coupling_ref[here, :]
        for c in range(3):
            value = once_ref[c, z + 1]
            total = once_ref[c, z] + once_ref[c, z + 2] + x_sum(value)
            total = total + row_sum(value, rims[c][0][z:z + 1], rims[c][1][z:z + 1])
            result = KEEP * value + scaled_ref[c, here, :] + coupling * total
            out_ref[c, here, :] = result
            plain_ref[128 * c + 16 * z:128 * c + 16 * z + 16, :] = result.astype(BF16)

    width = field_ref.shape[-1]
    count = cells_ref.shape[1]
    cells = cells_ref[...].astype(F32)
    line = jnp.floor((cells + 0.5) * (1.0 / width))
    line_column = column_of(line)
    place_column = column_of(cells - width * line)
    along = lax.broadcasted_iota(jnp.int32, (count, width), 1).astype(F32)
    chosen = jnp.where(along == line_column, 1.0, 0.0).astype(BF16)
    picked = jnp.dot(chosen, plain_ref[...], preferred_element_type=F32)
    single = jnp.where(along == place_column, picked, 0.0).astype(BF16)
    spread = jnp.dot(single, jnp.ones((width, 128), BF16), preferred_element_type=F32)
    far = jnp.dot(right_ref[...], spread.astype(BF16), preferred_element_type=F32)
    ranks = 16
    used = planes * ranks
    lane = lax.broadcasted_iota(jnp.int32, (PLANE, 128), 1)
    parts = [jnp.zeros((PLANE, 128), F32) for _ in range(3)]
    for k in range(ranks):
        for z in range(planes):
            group = far[PLANE * (k * planes + z):PLANE * (k * planes + z + 1), :]
            for at in (z * ranks + k, 192 + z * ranks + k):
                parts[at // 128] = jnp.where(lane == at % 128, group, parts[at // 128])
    both = jnp.concatenate(parts, axis=1)
    two = lax.broadcasted_iota(jnp.int32, both.shape, 1)
    high = both.astype(BF16).astype(F32)
    both = jnp.where(two < 192, high, both - high)
    tiles = send_ref.shape[0] // PLANE
    for to in range(PLANE):
        parts_row = jnp.broadcast_to(both[to:to + 1, :], (tiles, both.shape[1]))
        both_rows = parts_row if to % 2 == 0 else jnp.concatenate([both_rows, parts_row], axis=0)
        if to % 2 == 1:
            send_ref[(to - 1) * tiles:(to + 1) * tiles, 0:384] = both_rows.astype(BF16)
    down = lax.broadcasted_iota(jnp.int32, (128, 128), 0)
    across = lax.broadcasted_iota(jnp.int32, (128, 128), 1)
    for half in range(count // 128):
        piece = jnp.where(down == across, spread[128 * half:128 * half + 128, :], 0.0)
        piece = jnp.sum(piece, axis=0, keepdims=True)
        send_ref[:, 384 + 128 * half:512 + 128 * half] = jnp.broadcast_to(piece, (send_ref.shape[0], 128)).astype(BF16)


def fold(rows):
    total = jnp.sum(rows.astype(F32), axis=0, keepdims=True)
    return total + pltpu.roll(jnp.broadcast_to(total, (8, total.shape[1])), 192, 1)


def middle(tiles, got_ref, send_ref):
    across = lax.rem(lax.axis_index("slab"), PLANE)
    tile = lax.axis_index("tile")
    total = fold(got_ref[:, 0:384])
    high = total.astype(BF16).astype(F32)
    lane = lax.broadcasted_iota(jnp.int32, total.shape, 1)
    send = jnp.where(lane < 192, high, total - high)[0:1, :]
    send_ref[:, 0:384] = jnp.broadcast_to(send, (send_ref.shape[0], 384)).astype(BF16)
    row = lax.broadcasted_iota(jnp.int32, (16, got_ref.shape[0]), 0)
    along = lax.broadcasted_iota(jnp.int32, (16, got_ref.shape[0]), 1)
    other = jnp.where(across == 0, PLANE - 1, 0)
    wanted = tile + row - 1
    match = (row < 3) & (wanted >= 0) & (wanted < tiles) & (along == other * tiles + wanted)
    chosen = jnp.where(match, 1.0, 0.0).astype(BF16)
    relay = jnp.dot(chosen, got_ref[:, 384:640], preferred_element_type=F32)
    for b in range(3):
        send_ref[:, 384 + 256 * b:640 + 256 * b] = jnp.broadcast_to(relay[b:b + 1, :], (send_ref.shape[0], 256)).astype(BF16)


def finish(tiles, planes, mask_ref, rank_ref, got_ref, relay_ref, near_ref, left_ref, out_ref):
    slab = lax.axis_index("slab")
    across = lax.rem(slab, PLANE)
    plane = lax.div(slab, PLANE)
    tile = lax.axis_index("tile")
    row = lax.broadcasted_iota(jnp.int32, (16, got_ref.shape[0]), 0)
    along = lax.broadcasted_iota(jnp.int32, (16, got_ref.shape[0]), 1)
    third = lax.shift_right_logical(row * 11, 5)
    up = across + third - 1
    beside = tile + row - 3 * third - 1
    match = (row < 9) & (up >= 0) & (up < PLANE) & (beside >= 0) & (beside < tiles) & (along == up * tiles + beside)
    near = jnp.dot(jnp.where(match, 1.0, 0.0).astype(BF16), got_ref[:, 384:640], preferred_element_type=F32)
    row = lax.broadcasted_iota(jnp.int32, near.shape, 0)
    passed = relay_ref[...].astype(F32)
    from_row = lax.broadcasted_iota(jnp.int32, (passed.shape[0], 768), 0)
    under = jnp.sum(jnp.where((from_row == plane - 1) & (across == 0), passed[:, 384:], 0.0), axis=0, keepdims=True)
    over = jnp.sum(jnp.where((from_row == plane + 1) & (across == PLANE - 1), passed[:, 384:], 0.0), axis=0, keepdims=True)
    for b in range(3):
        near = jnp.where(row == b, near + under[:, 256 * b:256 * b + 256], near)
        near = jnp.where(row == 6 + b, near + over[:, 256 * b:256 * b + 256], near)
    listed = jnp.zeros(near.shape, F32)
    for q in range(9):
        listed = jnp.where(row == q, mask_ref[q].astype(F32), listed)
    near = (near * listed).astype(BF16)
    products = lax.dot_general(near, near_ref[...], (((1,), (1,)), ((), ())), preferred_element_type=F32)
    result = jnp.zeros((1, 256), F32)
    for q in range(9):
        result = result + products[q:q + 1, 256 * q:256 * q + 256]
    total = fold(passed[:, 0:384])[:, 0:256]
    lane = lax.broadcasted_iota(jnp.int32, total.shape, 1)
    own = (lane >= 16 * plane) & (lane < 16 * plane + rank_ref[0])
    total = jnp.where(own, total, 0.0)
    high = total.astype(BF16).astype(F32)
    halves = jnp.concatenate([high, total - high], axis=0).astype(BF16)
    left = jnp.concatenate([left_ref[...]] * 16, axis=0)
    far = jnp.dot(halves, left, preferred_element_type=F32)
    out_ref[...] = result + far[0:1, :] + far[8:9, :]


def vmem():
    return pl.BlockSpec(memory_space=pltpu.VMEM)


def smem():
    return pl.BlockSpec(memory_space=pltpu.SMEM)


def exchange(first, last, axis):
    devices = lax.axis_size(axis)
    up = [(i, i + 1) for i in range(devices - 1)]
    down = [(j, i) for i, j in up]
    return lax.ppermute(last, axis, up), lax.ppermute(first, axis, down)


def local(initial_field, source, material, stiffness_table, mass_table, trace_cells, near_blocks, near_mask, far_left, far_right,
          block_ranks):
    slabs, tiles = lax.axis_size("slab"), lax.axis_size("tile")
    planes = slabs // PLANE
    field = initial_field.reshape(3, 128, 384)
    sources = source.reshape(3, 128, 384)
    cells = material.reshape(128, 384)
    face = jax.ShapeDtypeStruct((64, 384), BF16)
    params = pltpu.CompilerParams(vmem_limit_bytes=24 * 1024 * 1024)
    first, last = pl.pallas_call(
        y_faces,
        out_shape=(face, face),
        in_specs=[smem(), smem(), vmem(), vmem(), vmem()],
        out_specs=(vmem(), vmem()),
        compiler_params=params,
    )(stiffness_table, mass_table, field, sources, cells)
    before, after = exchange(first, last, "tile")
    face = jax.ShapeDtypeStruct((128, 384), BF16)
    first, last = pl.pallas_call(
        z_faces,
        grid=(1,),
        out_shape=(face, face),
        in_specs=[
            smem(), smem(),
            pl.BlockSpec((3, 32, 384), lambda i: (0, 0, 0)), pl.BlockSpec((3, 32, 384), lambda i: (0, 3, 0)),
            pl.BlockSpec((3, 16, 384), lambda i: (0, 0, 0)), pl.BlockSpec((3, 16, 384), lambda i: (0, 7, 0)),
            pl.BlockSpec((16, 384), lambda i: (0, 0)), pl.BlockSpec((16, 384), lambda i: (7, 0)),
            pl.BlockSpec((64, 384), lambda i: (0, 0)), pl.BlockSpec((64, 384), lambda i: (0, 0)),
        ],
        out_specs=(pl.BlockSpec((128, 384), lambda i: (0, 0)), pl.BlockSpec((128, 384), lambda i: (0, 0))),
        compiler_params=params,
    )(stiffness_table, mass_table, field, field, sources, sources, cells, cells, before, after)
    below, above = exchange(first, last, "slab")
    members = PLANE * tiles
    result, send = pl.pallas_call(
        functools.partial(relax, planes),
        out_shape=(jax.ShapeDtypeStruct((3, 128, 384), F32), jax.ShapeDtypeStruct((members, 640), BF16)),
        in_specs=[smem(), smem()] + [vmem()] * 9,
        out_specs=(vmem(), vmem()),
        scratch_shapes=[
            pltpu.VMEM((3, 10, 16, 384), F32),
            pltpu.VMEM((3, 128, 384), F32),
            pltpu.VMEM((128, 384), F32),
            pltpu.VMEM((384, 384), BF16),
        ],
        compiler_params=params,
    )(stiffness_table, mass_table, field, sources, cells, before, after, below, above,
      far_right.reshape(-1, 256), trace_cells.reshape(1, 256))
    ids = np.arange(slabs * tiles).reshape(planes, members)
    got = lax.all_to_all(send, BOTH, 0, 0, axis_index_groups=ids.tolist())
    send = pl.pallas_call(
        functools.partial(middle, tiles),
        out_shape=jax.ShapeDtypeStruct((planes, 1152), BF16),
        in_specs=[vmem()],
        out_specs=vmem(),
        compiler_params=params,
    )(got)
    relay = lax.all_to_all(send, BOTH, 0, 0, axis_index_groups=ids.T.tolist())
    boundary = pl.pallas_call(
        functools.partial(finish, tiles, planes),
        out_shape=jax.ShapeDtypeStruct((1, 256), F32),
        in_specs=[smem(), smem()] + [vmem()] * 4,
        out_specs=vmem(),
        compiler_params=params,
    )(near_mask.reshape(9), block_ranks, got, relay, near_blocks.reshape(-1, 256), far_left.reshape(16, 256))
    return result.reshape(initial_field.shape), boundary.reshape(1, 1, 256)


def solution(mesh):
    placed = (
        P(None, "slab", "tile", None),
        P(None, "slab", "tile", None),
        P("slab", "tile", None),
        P(),
        P(),
        P("slab", "tile", None),
        P("slab", "tile", None, None, None),
        P("slab", "tile", None),
        P(None, "slab", "tile", None),
        P(None, None, "slab", "tile", None),
        P("slab"),
    )
    return jax.shard_map(
        local,
        mesh=mesh,
        in_specs=placed,
        out_specs=(P(None, "slab", "tile", None), P("slab", "tile", None)),
        check_vma=False,
    )
```

time: 198 us -> 82.7 us (0.42)
  the two profiles are of different devices: /device:TPU:40 before, /device:TPU:1 now
where the time goes in v1:
time: 82.7 us; the launch traced here: 81.9 us
  starting transfers between devices  32.8 us (40%)
  blocking collectives  20.6 us (25%)
  waiting for transfers between devices  13.2 us (16%)
  Pallas kernels  6.53 us (8%)
  local copies, waits for them, and re-layouts  6.02 us (7%)
  between operations  1.44 us (2%)
  other arithmetic  1.32 us (2%)
    all_to_all x1, blocking collectives, local(): got = lax.all_to_all(send, BOTH, 0, 0, axis_index_groups=ids.tolist())  20.6 us
    ppermute x4, starting transfers between devices, exchange(): return (lax.ppermute(last, axis, up), lax.ppermute(first, axis, down))  17.6 us
    all_to_all x1, starting transfers between devices, local(): relay = lax.all_to_all(send, BOTH, 0, 0, axis_index_groups=ids.T.tolist())  15.2 us
    all_to_all x1, waiting for transfers between devices, local(): relay = lax.all_to_all(send, BOTH, 0, 0, axis_index_groups=ids.T.tolist())  8.74 us
    unnamed x26, local copies, waits for them, and re-layouts  5.51 us
    ppermute x4, waiting for transfers between devices, exchange(): return (lax.ppermute(last, axis, up), lax.ppermute(first, axis, down))  4.44 us
    pallas_call x1, Pallas kernels, local(): pl.pallas_call(functools.partial(relax, planes), out_shape=(jax.ShapeDtyp...  3.31 us
  transfers between devices with their start and end apart: 5, of which 3 were waited for; matrix products, arithmetic and copies ran while one was open for 0% of the time, Pallas kernels for 0%

profile of v1, /device:TPU:1, one launch (start us, length us, event | category | flops | bytes accessed | tf_op | source)
XLA Modules:
  0.0 81.9 jit_solution(2996285218618528141)
XLA Ops:
  0.6 0.0 copy-start
  0.6 1.1 %copy-done = f32[3,8,16,384]{3,2,1,0:T(8,128)S(1)} copy-done((f32[3,8,16,384]{3,2,1,0:T(8,128)S(1)}, f32[3,8,16,384]{3,2,1,0:T(8,128)}, u32[]{:S(2)}) %copy-start) | copy-done | bytes 589848
  1.7 0.0 copy-start.1
  1.7 1.1 %copy-done.1 = f32[3,8,16,384]{3,2,1,0:T(8,128)S(1)} copy-done((f32[3,8,16,384]{3,2,1,0:T(8,128)S(1)}, f32[3,8,16,384]{3,2,1,0:T(8,128)}, u32[]{:S(2)}) %copy-start.1) | copy-done | bytes 589848
  2.8 0.0 copy-start.2
  2.8 0.9 %copy-done.2 = s32[8,16,384]{2,1,0:T(8,128)S(1)} copy-done((s32[8,16,384]{2,1,0:T(8,128)S(1)}, s32[8,16,384]{2,1,0:T(8,128)}, u32[]{:S(2)}) %copy-start.2) | copy-done | bytes 196632
  3.7 0.0 copy-start.6
  3.7 0.7 copy-done.6
  4.3 0.0 copy-start.7
  4.3 0.7 copy-done.7
  5.0 0.7 shard_map.122
  5.7 4.0 %collective-permute-start = (bf16[64,384]{1,0:T(8,128)(2,1)S(1)}, bf16[64,384]{1,0:T(8,128)(2,1)S(1)}, u32[]{:S(2)}, u32[]{:S(2)}) collective-permute-start(bf16[64,384]{1,0:T(8,128)(2,1)S(1)} %get-tuple-element.8), channel_id=1, source_target_pairs={{0,1},{1,2},{2,3},{3,4},{4,5},{5,6},{6,7},{8,9},{9,10},{10,11},{11... | collective-permute-start | bytes 147464 | tf_op jit(solution)/shard_map/ppermute | solution.py:277
  9.8 0.0 copy-start.4
  9.8 0.0 copy-start.8
  9.8 1.4 %collective-permute-start.1 = (bf16[64,384]{1,0:T(8,128)(2,1)S(1)}, bf16[64,384]{1,0:T(8,128)(2,1)S(1)}, u32[]{:S(2)}, u32[]{:S(2)}) collective-permute-start(bf16[64,384]{1,0:T(8,128)(2,1)S(1)} %get-tuple-element.9), channel_id=1, source_target_pairs={{1,0},{2,1},{3,2},{4,3},{5,4},{6,5},{7,6},{9,8},{10,9},{11,10},{12... | collective-permute-start | bytes 147464 | tf_op jit(solution)/shard_map/ppermute | solution.py:277
  11.2 0.0 collective-permute-done.before_ref
  11.2 3.5 %collective-permute-done.1.after_ref = bf16[64,384]{1,0:T(8,128)(2,1)S(1)} collective-permute-done((bf16[64,384]{1,0:T(8,128)(2,1)S(1)}, bf16[64,384]{1,0:T(8,128)(2,1)S(1)}, u32[]{:S(2)}, u32[]{:S(2)}) %collective-permute-start.1) | collective-permute-done | bytes 49184 | tf_op jit(solution)/shard_map/ppermute | solution.py:277
  14.8 0.7 shard_map.123
  15.5 5.1 %collective-permute-start.2 = (bf16[128,384]{1,0:T(8,128)(2,1)S(1)}, bf16[128,384]{1,0:T(8,128)(2,1)S(1)}, u32[]{:S(2)}, u32[]{:S(2)}) collective-permute-start(bf16[128,384]{1,0:T(8,128)(2,1)S(1)} %get-tuple-element.10), channel_id=1, source_target_pairs={{0,8},{8,16},{16,24},{24,32},{32,40},{40,48},{48,56},{56,64},{64,7... | collective-permute-start | bytes 294920 | tf_op jit(solution)/shard_map/ppermute | solution.py:277
  20.6 7.0 %collective-permute-start.3 = (bf16[128,384]{1,0:T(8,128)(2,1)S(1)}, bf16[128,384]{1,0:T(8,128)(2,1)S(1)}, u32[]{:S(2)}, u32[]{:S(2)}) collective-permute-start(bf16[128,384]{1,0:T(8,128)(2,1)S(1)} %get-tuple-element.11), channel_id=1, source_target_pairs={{8,0},{16,8},{24,16},{32,24},{40,32},{48,40},{56,48},{64,56},{72,6... | collective-permute-start | bytes 294920 | tf_op jit(solution)/shard_map/ppermute | solution.py:277
  27.6 0.0 collective-permute-done.2.below_ref
  27.6 0.9 %collective-permute-done.3.above_ref = bf16[128,384]{1,0:T(8,128)(2,1)S(1)} collective-permute-done((bf16[128,384]{1,0:T(8,128)(2,1)S(1)}, bf16[128,384]{1,0:T(8,128)(2,1)S(1)}, u32[]{:S(2)}, u32[]{:S(2)}) %collective-permute-start.3) | collective-permute-done | bytes 98336 | tf_op jit(solution)/shard_map/ppermute | solution.py:277
  28.5 0.0 copy-done.4
  28.5 0.0 copy-done.8
  28.6 3.3 %shard_map.124 = (f32[3,128,384]{2,1,0:T(8,128)}, bf16[64,640]{1,0:T(8,128)(2,1)S(1)}) custom-call(f32[8]{0:T(128)S(1)} %copy-done.6, f32[8]{0:T(128)S(1)} %copy-done.7, f32[3,128,384]{2,1,0:T(8,128)S(1)} %bitcast.21, f32[3,128,384]{2,1,0:T(8,128)S(1)} %bitcast.25, s32[128,384]{1,0:T(8,128)S(1)} %bitcast.29, ...), custom_call_target="tpu_custom_call" | custom-call | tf_op jit(solution)/shard_map/pallas_call | solution.py:314
  31.9 0.0 copy-start.3
  31.9 0.0 copy-start.5
  31.9 0.0 copy-start.9
  31.9 0.5 broadcast
  32.4 0.7 reduce
  33.0 0.1 reshape.48
  33.2 20.6 %all_to_all.22 = bf16[64,2,320]{2,1,0:T(2,128)(2,1)S(1)} all-to-all(bf16[64,2,320]{2,1,0:T(2,128)(2,1)S(1)} %reshape.48), channel_id=1, replica_groups={{0,1,2,3,4,5,6,7,8,9,10,11,12,13,14,15,16,17,18,19,20,21,22,23,24,25,26..., dimensions={0} | all-to-all | bytes 163840 | tf_op jit(solution)/shard_map/all_to_all | solution.py:329
  53.8 0.2 reshape.49
  54.0 0.1 shard_map.125
  54.1 0.7 reduce.1
  54.8 0.7 reshape.50
  55.5 15.2 %all-to-all-start.1 = ((bf16[12,2,576]{2,1,0:T(2,128)(2,1)}), bf16[12,2,576]{2,1,0:T(2,128)(2,1)S(1)}, u32[]{:S(2)}, u32[]{:S(2)}) async-start(bf16[12,2,576]{2,1,0:T(2,128)(2,1)} %reshape.50), calls=%async_computation.1 | async-start | bytes 61440 | tf_op jit(solution)/shard_map/all_to_all | solution.py:337
  71.3 8.7 %all-to-all-done.1 = bf16[12,2,576]{2,1,0:T(2,128)(2,1)S(1)} async-done(((bf16[12,2,576]{2,1,0:T(2,128)(2,1)}), bf16[12,2,576]{2,1,0:T(2,128)(2,1)S(1)}, u32[]{:S(2)}, u32[]{:S(2)}) %all-to-all-start.1) | async-done | bytes 27680 | tf_op jit(solution)/shard_map/all_to_all | solution.py:337
  80.1 0.1 reshape.51
  80.2 0.0 copy-done.3
  80.2 0.0 copy-done.5
  80.2 0.0 copy-done.9
  80.2 1.6 %shard_map.126 = f32[1,256]{1,0:T(1,128)} custom-call(s32[9]{0:T(128)S(1)} %bitcast.39, s32[1]{0:T(128)S(6)} %copy.25.rank_ref, bf16[64,640]{1,0:T(8,128)(2,1)S(1)} %bitcast.33, bf16[12,1152]{1,0:T(8,128)(2,1)S(1)} %bitcast.34, bf16[2304,256]{1,0:T(8,128)(2,1)S(1)} %bitcast.30, bf16[16,256]{1,0:T(8,128)(2,1)S(1)} %bitcast.37), custom_call_target="tpu_custom_call" | custom-call | tf_op jit(solution)/shard_map/pallas_call | solution.py:338
  (2 shorter events, 0.0 us)
Async XLA Ops:
  0.6 1.1 %copy-start = (f32[3,8,16,384]{3,2,1,0:T(8,128)S(1)}, f32[3,8,16,384]{3,2,1,0:T(8,128)}, u32[]{:S(2)}) copy-start(f32[3,8,16,384]{3,2,1,0:T(8,128)} %param.11) | copy-start | bytes 1769476
  1.7 1.1 %copy-start.1 = (f32[3,8,16,384]{3,2,1,0:T(8,128)S(1)}, f32[3,8,16,384]{3,2,1,0:T(8,128)}, u32[]{:S(2)}) copy-start(f32[3,8,16,384]{3,2,1,0:T(8,128)} %param.12) | copy-start | bytes 1769476
  2.8 0.9 %copy-start.2 = (s32[8,16,384]{2,1,0:T(8,128)S(1)}, s32[8,16,384]{2,1,0:T(8,128)}, u32[]{:S(2)}) copy-start(s32[8,16,384]{2,1,0:T(8,128)} %param.13) | copy-start | bytes 589828
  3.7 0.7 copy-start.6
  4.3 0.7 copy-start.7
  5.7 5.5 %collective-permute-start = (bf16[64,384]{1,0:T(8,128)(2,1)S(1)}, bf16[64,384]{1,0:T(8,128)(2,1)S(1)}, u32[]{:S(2)}, u32[]{:S(2)}) collective-permute-start(bf16[64,384]{1,0:T(8,128)(2,1)S(1)} %get-tuple-element.8), channel_id=1, source_target_pairs={{0,1},{1,2},{2,3},{3,4},{4,5},{5,6},{6,7},{8,9},{9,10},{10,11},{11... | collective-permute-start | bytes 147464 | tf_op jit(solution)/shard_map/ppermute | solution.py:277
  9.8 18.8 %copy-start.4 = (bf16[16,96,1,1,256]{4,1,3,2,0:T(8,128)(2,1)S(1)}, bf16[16,96,1,1,256]{4,1,3,2,0:T(8,128)(2,1)}, u32[]{:S(2)}) copy-start(bf16[16,96,1,1,256]{4,1,3,2,0:T(8,128)(2,1)} %param.20) | copy-start | bytes 2359300
  9.8 18.8 %copy-start.8 = (s32[1,1,256]{2,1,0:T(1,128)S(1)}, s32[1,1,256]{2,1,0:T(1,128)}, u32[]{:S(2)}) copy-start(s32[1,1,256]{2,1,0:T(1,128)} %param.16) | copy-start | bytes 3076
  9.8 5.0 %collective-permute-start.1 = (bf16[64,384]{1,0:T(8,128)(2,1)S(1)}, bf16[64,384]{1,0:T(8,128)(2,1)S(1)}, u32[]{:S(2)}, u32[]{:S(2)}) collective-permute-start(bf16[64,384]{1,0:T(8,128)(2,1)S(1)} %get-tuple-element.9), channel_id=1, source_target_pairs={{1,0},{2,1},{3,2},{4,3},{5,4},{6,5},{7,6},{9,8},{10,9},{11,10},{12... | collective-permute-start | bytes 147464 | tf_op jit(solution)/shard_map/ppermute | solution.py:277
  15.5 12.1 %collective-permute-start.2 = (bf16[128,384]{1,0:T(8,128)(2,1)S(1)}, bf16[128,384]{1,0:T(8,128)(2,1)S(1)}, u32[]{:S(2)}, u32[]{:S(2)}) collective-permute-start(bf16[128,384]{1,0:T(8,128)(2,1)S(1)} %get-tuple-element.10), channel_id=1, source_target_pairs={{0,8},{8,16},{16,24},{24,32},{32,40},{40,48},{48,56},{56,64},{64,7... | collective-permute-start | bytes 294920 | tf_op jit(solution)/shard_map/ppermute | solution.py:277
  20.6 8.0 %collective-permute-start.3 = (bf16[128,384]{1,0:T(8,128)(2,1)S(1)}, bf16[128,384]{1,0:T(8,128)(2,1)S(1)}, u32[]{:S(2)}, u32[]{:S(2)}) collective-permute-start(bf16[128,384]{1,0:T(8,128)(2,1)S(1)} %get-tuple-element.11), channel_id=1, source_target_pairs={{8,0},{16,8},{24,16},{32,24},{40,32},{48,40},{56,48},{64,56},{72,6... | collective-permute-start | bytes 294920 | tf_op jit(solution)/shard_map/ppermute | solution.py:277
  31.9 48.3 %copy-start.3 = (bf16[1,1,9,256,256]{4,3,2,1,0:T(8,128)(2,1)S(1)}, bf16[1,1,9,256,256]{4,3,2,1,0:T(8,128)(2,1)}, u32[]{:S(2)}) copy-start(bf16[1,1,9,256,256]{4,3,2,1,0:T(8,128)(2,1)} %param.17) | copy-start | bytes 3538948
  31.9 48.4 %copy-start.5 = (bf16[16,1,1,256]{3,0,2,1:T(8,128)(2,1)S(1)}, bf16[16,1,1,256]{3,0,2,1:T(8,128)(2,1)}, u32[]{:S(2)}) copy-start(bf16[16,1,1,256]{3,0,2,1:T(8,128)(2,1)} %param.19) | copy-start | bytes 24580
  31.9 48.4 %copy-start.9 = (s32[1,1,9]{2,1,0:T(1,128)S(1)}, s32[1,1,9]{2,1,0:T(1,128)}, u32[]{:S(2)}) copy-start(s32[1,1,9]{2,1,0:T(1,128)} %param.18) | copy-start | bytes 112
  55.5 24.6 %all-to-all-start.1 = ((bf16[12,2,576]{2,1,0:T(2,128)(2,1)}), bf16[12,2,576]{2,1,0:T(2,128)(2,1)S(1)}, u32[]{:S(2)}, u32[]{:S(2)}) async-start(bf16[12,2,576]{2,1,0:T(2,128)(2,1)} %reshape.50), calls=%async_computation.1 | async-start | bytes 61440 | tf_op jit(solution)/shard_map/all_to_all | solution.py:337

commit v2 on v1

--- a/solution.py
+++ b/solution.py
@@ -60,7 +60,14 @@
     return value
 
 
-def y_faces(stiff_ref, mass_ref, field_ref, source_ref, material_ref, first_ref, last_ref):
+def y_faces(stiff_hbm, mass_hbm, field_hbm, source_hbm, material_hbm, first_ref, last_ref,
+            stiff_ref, mass_ref, field_ref, source_ref, material_ref, sems):
+    pairs = ((stiff_hbm, stiff_ref), (mass_hbm, mass_ref), (material_hbm, material_ref), (field_hbm, field_ref), (source_hbm, source_ref))
+    copies = [pltpu.make_async_copy(src, dst, sems.at[k]) for k, (src, dst) in enumerate(pairs)]
+    for copy in copies:
+        copy.start()
+    for copy in copies:
+        copy.wait()
     rows = table_rows(stiff_ref, mass_ref)
     for y, inner, out_ref in ((0, 1, first_ref), (15, 14, last_ref)):
         weight, coupling = lookup(line_rows(material_ref, y), rows)
@@ -106,6 +113,14 @@
             for side in range(2):
                 packed = jnp.where(row == 2 * c + side, lines[c][side], packed)
         out_ref[112:128, :] = packed.astype(BF16)
+
+
+def stacked(lines, height):
+    row = lax.broadcasted_iota(jnp.int32, (height, lines[0].shape[1]), 0)
+    value = jnp.broadcast_to(lines[0], row.shape)
+    for k in range(1, len(lines)):
+        value = jnp.where(row == k, lines[k], value)
+    return value
 
 
 def column_of(row):
@@ -173,93 +188,99 @@
     spread = jnp.dot(single, jnp.ones((width, 128), BF16), preferred_element_type=F32)
     far = jnp.dot(right_ref[...], spread.astype(BF16), preferred_element_type=F32)
     ranks = 16
-    used = planes * ranks
     lane = lax.broadcasted_iota(jnp.int32, (PLANE, 128), 1)
-    parts = [jnp.zeros((PLANE, 128), F32) for _ in range(3)]
+    parts = [jnp.zeros((PLANE, 128), F32) for _ in range(2)]
     for k in range(ranks):
         for z in range(planes):
             group = far[PLANE * (k * planes + z):PLANE * (k * planes + z + 1), :]
-            for at in (z * ranks + k, 192 + z * ranks + k):
-                parts[at // 128] = jnp.where(lane == at % 128, group, parts[at // 128])
-    both = jnp.concatenate(parts, axis=1)
-    two = lax.broadcasted_iota(jnp.int32, both.shape, 1)
-    high = both.astype(BF16).astype(F32)
-    both = jnp.where(two < 192, high, both - high)
+            at = z * ranks + k
+            parts[at // 128] = jnp.where(lane == at % 128, group, parts[at // 128])
+    down = lax.broadcasted_iota(jnp.int32, (128, 128), 0)
+    across = lax.broadcasted_iota(jnp.int32, (128, 128), 1)
+    traces = []
+    for half in range(2):
+        piece = jnp.where(down == across, spread[128 * half:128 * half + 128, :], 0.0)
+        traces.append(jnp.sum(piece, axis=0, keepdims=True))
     tiles = send_ref.shape[0] // PLANE
     for to in range(PLANE):
-        parts_row = jnp.broadcast_to(both[to:to + 1, :], (tiles, both.shape[1]))
-        both_rows = parts_row if to % 2 == 0 else jnp.concatenate([both_rows, parts_row], axis=0)
-        if to % 2 == 1:
-            send_ref[(to - 1) * tiles:(to + 1) * tiles, 0:384] = both_rows.astype(BF16)
-    down = lax.broadcasted_iota(jnp.int32, (128, 128), 0)
-    across = lax.broadcasted_iota(jnp.int32, (128, 128), 1)
-    for half in range(count // 128):
-        piece = jnp.where(down == across, spread[128 * half:128 * half + 128, :], 0.0)
-        piece = jnp.sum(piece, axis=0, keepdims=True)
-        send_ref[:, 384 + 128 * half:512 + 128 * half] = jnp.broadcast_to(piece, (send_ref.shape[0], 128)).astype(BF16)
-
-
-def fold(rows):
-    total = jnp.sum(rows.astype(F32), axis=0, keepdims=True)
-    return total + pltpu.roll(jnp.broadcast_to(total, (8, total.shape[1])), 192, 1)
+        packet = stacked([parts[0][to:to + 1, :], parts[1][to:to + 1, :]] + traces, 4).astype(BF16)
+        for tile in range(tiles):
+            send_ref[to * tiles + tile] = packet
 
 
 def middle(tiles, got_ref, send_ref):
     across = lax.rem(lax.axis_index("slab"), PLANE)
     tile = lax.axis_index("tile")
-    total = fold(got_ref[:, 0:384])
+    total = jnp.sum(got_ref[...].astype(F32), axis=0)
+    other = jnp.where(across == 0, PLANE - 1, 0)
+    relay = []
+    for b in range(3):
+        wanted = tile + b - 1
+        inside = (wanted >= 0) & (wanted < tiles)
+        packet = got_ref[other * tiles + jnp.clip(wanted, 0, tiles - 1)].astype(F32)
+        packet = jnp.where(inside, packet, 0.0)
+        relay += [packet[2:3, :], packet[3:4, :]]
     high = total.astype(BF16).astype(F32)
-    lane = lax.broadcasted_iota(jnp.int32, total.shape, 1)
-    send = jnp.where(lane < 192, high, total - high)[0:1, :]
-    send_ref[:, 0:384] = jnp.broadcast_to(send, (send_ref.shape[0], 384)).astype(BF16)
-    row = lax.broadcasted_iota(jnp.int32, (16, got_ref.shape[0]), 0)
-    along = lax.broadcasted_iota(jnp.int32, (16, got_ref.shape[0]), 1)
-    other = jnp.where(across == 0, PLANE - 1, 0)
-    wanted = tile + row - 1
-    match = (row < 3) & (wanted >= 0) & (wanted < tiles) & (along == other * tiles + wanted)
-    chosen = jnp.where(match, 1.0, 0.0).astype(BF16)
-    relay = jnp.dot(chosen, got_ref[:, 384:640], preferred_element_type=F32)
-    for b in range(3):
-        send_ref[:, 384 + 256 * b:640 + 256 * b] = jnp.broadcast_to(relay[b:b + 1, :], (send_ref.shape[0], 256)).astype(BF16)
-
-
-def finish(tiles, planes, mask_ref, rank_ref, got_ref, relay_ref, near_ref, left_ref, out_ref):
+    low = total - high
+    for half in range(2):
+        packet = stacked([high[half:half + 1, :], low[half:half + 1, :]] + relay, 8).astype(BF16)
+        for z in range(8 * half, min(8 * half + 8, send_ref.shape[0])):
+            send_ref[z] = packet
+
+
+def masked_rows(rows, mask_ref, first):
+    value = jnp.zeros((16, 256), F32)
+    row = lax.broadcasted_iota(jnp.int32, value.shape, 0)
+    for k, (low, high) in enumerate(rows):
+        line = jnp.concatenate([low, high], axis=1) * mask_ref[first + k].astype(F32)
+        value = jnp.where(row == k, line, value)
+    return value.astype(BF16)
+
+
+def products(rows, blocks, count):
+    every = lax.dot_general(rows, blocks, (((1,), (1,)), ((), ())), preferred_element_type=F32)
+    result = every[0:1, 0:256]
+    for k in range(1, count):
+        result = result + every[k:k + 1, 256 * k:256 * k + 256]
+    return result
+
+
+def near_inside(tiles, mask_ref, got_ref, near_ref, out_ref):
+    across = lax.rem(lax.axis_index("slab"), PLANE)
+    tile = lax.axis_index("tile")
+    rows = []
+    for a in range(-1, 2):
+        for b in range(-1, 2):
+            up, beside = across + a, tile + b
+            inside = (up >= 0) & (up < PLANE) & (beside >= 0) & (beside < tiles)
+            packet = got_ref[jnp.clip(up, 0, PLANE - 1) * tiles + jnp.clip(beside, 0, tiles - 1)].astype(F32)
+            packet = jnp.where(inside, packet, 0.0)
+            rows.append((packet[2:3, :], packet[3:4, :]))
+    out_ref[...] = products(masked_rows(rows, mask_ref, 0), near_ref[...], 9)
+
+
+def finish(planes, mask_ref, rank_ref, part_ref, relay_ref, near_ref, left_ref, out_ref):
     slab = lax.axis_index("slab")
     across = lax.rem(slab, PLANE)
     plane = lax.div(slab, PLANE)
-    tile = lax.axis_index("tile")
-    row = lax.broadcasted_iota(jnp.int32, (16, got_ref.shape[0]), 0)
-    along = lax.broadcasted_iota(jnp.int32, (16, got_ref.shape[0]), 1)
-    third = lax.shift_right_logical(row * 11, 5)
-    up = across + third - 1
-    beside = tile + row - 3 * third - 1
-    match = (row < 9) & (up >= 0) & (up < PLANE) & (beside >= 0) & (beside < tiles) & (along == up * tiles + beside)
-    near = jnp.dot(jnp.where(match, 1.0, 0.0).astype(BF16), got_ref[:, 384:640], preferred_element_type=F32)
-    row = lax.broadcasted_iota(jnp.int32, near.shape, 0)
-    passed = relay_ref[...].astype(F32)
-    from_row = lax.broadcasted_iota(jnp.int32, (passed.shape[0], 768), 0)
-    under = jnp.sum(jnp.where((from_row == plane - 1) & (across == 0), passed[:, 384:], 0.0), axis=0, keepdims=True)
-    over = jnp.sum(jnp.where((from_row == plane + 1) & (across == PLANE - 1), passed[:, 384:], 0.0), axis=0, keepdims=True)
-    for b in range(3):
-        near = jnp.where(row == b, near + under[:, 256 * b:256 * b + 256], near)
-        near = jnp.where(row == 6 + b, near + over[:, 256 * b:256 * b + 256], near)
-    listed = jnp.zeros(near.shape, F32)
-    for q in range(9):
-        listed = jnp.where(row == q, mask_ref[q].astype(F32), listed)
-    near = (near * listed).astype(BF16)
-    products = lax.dot_general(near, near_ref[...], (((1,), (1,)), ((), ())), preferred_element_type=F32)
-    result = jnp.zeros((1, 256), F32)
-    for q in range(9):
-        result = result + products[q:q + 1, 256 * q:256 * q + 256]
-    total = fold(passed[:, 0:384])[:, 0:256]
+    upward = across == PLANE - 1
+    start = jnp.where(upward, plane + 1, plane - 1)
+    edge = ((across == 0) | upward) & (start >= 0) & (start < planes)
+    packet = jnp.where(edge, relay_ref[jnp.clip(start, 0, planes - 1)].astype(F32), 0.0)
+    rows = [(packet[2 + 2 * b:3 + 2 * b, :], packet[3 + 2 * b:4 + 2 * b, :]) for b in range(3)]
+    first = jnp.where(upward, 6, 0)
+    blocks = near_ref[pl.ds(pl.multiple_of(256 * first, 256), 768), :]
+    near = products(masked_rows(rows, mask_ref, first), blocks, 3)
+    total = jnp.sum(relay_ref[...].astype(F32), axis=0)
+    total = jnp.broadcast_to(total[0:1, :] + total[1:2, :], (8, 128))
     lane = lax.broadcasted_iota(jnp.int32, total.shape, 1)
-    own = (lane >= 16 * plane) & (lane < 16 * plane + rank_ref[0])
-    total = jnp.where(own, total, 0.0)
+    at = 16 * lax.rem(plane, 8)
+    total = jnp.where((lane >= at) & (lane < at + rank_ref[0]), total, 0.0)
     high = total.astype(BF16).astype(F32)
     halves = jnp.concatenate([high, total - high], axis=0).astype(BF16)
-    left = jnp.concatenate([left_ref[...]] * 16, axis=0)
+    left = jnp.concatenate([left_ref[...]] * 8, axis=0)
     far = jnp.dot(halves, left, preferred_element_type=F32)
-    out_ref[...] = result + far[0:1, :] + far[8:9, :]
+    out_ref[...] = part_ref[...] + near + far[0:1, :] + far[8:9, :]
 
 
 def vmem():
@@ -289,9 +310,13 @@
     first, last = pl.pallas_call(
         y_faces,
         out_shape=(face, face),
-        in_specs=[smem(), smem(), vmem(), vmem(), vmem()],
+        in_specs=[pl.BlockSpec(memory_space=pltpu.HBM)] * 5,
         out_specs=(vmem(), vmem()),
-        compiler_params=params,
+        scratch_shapes=[
+            pltpu.SMEM((8,), F32), pltpu.SMEM((8,), F32), pltpu.VMEM((3, 128, 384), F32), pltpu.VMEM((3, 128, 384), F32),
+            pltpu.VMEM((128, 384), jnp.int32), pltpu.SemaphoreType.DMA((5,)),
+        ],
+        compiler_params=pltpu.CompilerParams(vmem_limit_bytes=48 * 1024 * 1024),
     )(stiffness_table, mass_table, field, sources, cells)
     before, after = exchange(first, last, "tile")
     face = jax.ShapeDtypeStruct((128, 384), BF16)
@@ -313,7 +338,7 @@
     members = PLANE * tiles
     result, send = pl.pallas_call(
         functools.partial(relax, planes),
-        out_shape=(jax.ShapeDtypeStruct((3, 128, 384), F32), jax.ShapeDtypeStruct((members, 640), BF16)),
+        out_shape=(jax.ShapeDtypeStruct((3, 128, 384), F32), jax.ShapeDtypeStruct((members, 4, 128), BF16)),
         in_specs=[smem(), smem()] + [vmem()] * 9,
         out_specs=(vmem(), vmem()),
         scratch_shapes=[
@@ -326,22 +351,32 @@
     )(stiffness_table, mass_table, field, sources, cells, before, after, below, above,
       far_right.reshape(-1, 256), trace_cells.reshape(1, 256))
     ids = np.arange(slabs * tiles).reshape(planes, members)
-    got = lax.all_to_all(send, BOTH, 0, 0, axis_index_groups=ids.tolist())
+    got = lax.all_to_all(send, BOTH, 0, 0, axis_index_groups=ids.tolist(), tiled=True)
     send = pl.pallas_call(
         functools.partial(middle, tiles),
-        out_shape=jax.ShapeDtypeStruct((planes, 1152), BF16),
+        out_shape=jax.ShapeDtypeStruct((planes, 8, 128), BF16),
         in_specs=[vmem()],
         out_specs=vmem(),
         compiler_params=params,
     )(got)
-    relay = lax.all_to_all(send, BOTH, 0, 0, axis_index_groups=ids.T.tolist())
+    relay = lax.all_to_all(send, BOTH, 0, 0, axis_index_groups=ids.T.tolist(), tiled=True)
+    mask = near_mask.reshape(9)
+    blocks = near_blocks.reshape(-1, 256)
+    part = pl.pallas_call(
+        functools.partial(near_inside, tiles),
+        out_shape=jax.ShapeDtypeStruct((1, 256), F32),
+        in_specs=[smem(), vmem(), vmem()],
+        out_specs=vmem(),
+        compiler_params=params,
+        cost_estimate=pl.CostEstimate(flops=2 * 16 * 2304 * 256, bytes_accessed=2304 * 512, transcendentals=0),
+    )(mask, got, blocks)
     boundary = pl.pallas_call(
-        functools.partial(finish, tiles, planes),
+        functools.partial(finish, planes),
         out_shape=jax.ShapeDtypeStruct((1, 256), F32),
         in_specs=[smem(), smem()] + [vmem()] * 4,
         out_specs=vmem(),
         compiler_params=params,
-    )(near_mask.reshape(9), block_ranks, got, relay, near_blocks.reshape(-1, 256), far_left.reshape(16, 256))
+    )(mask, block_ranks, part, relay, blocks, far_left.reshape(16, 256))
     return result.reshape(initial_field.shape), boundary.reshape(1, 1, 256)
 
 

time: 82.7 us -> 79.5 us (0.961)
  local copies, waits for them, and re-layouts: 6.02 us -> 4.38 us
  other arithmetic: 1.32 us -> 0 us
  Pallas kernels: 6.53 us -> 7.78 us
  waiting for transfers between devices: 13.2 us -> 12.1 us
    all_to_all x2 -> x0, other arithmetic: 1.32 us -> none  [the longest x1 0.66 us: local(): got = lax.all_to_all(send, BOTH, 0, 0, axis_index_groups=ids.tolist())]
    unnamed x26 -> x20, local copies, waits for them, and re-layouts: 5.51 us -> 4.38 us
    all_to_all x1, waiting for transfers between devices: 8.74 us -> 7.71 us  [local(): lax.all_to_all(send, BOTH, 0, 0, axis_index_groups=ids.T.tolist(), tiled=...]
    pallas_call x2 -> x3, Pallas kernels: 2.37 us -> 3.07 us  [the longest x1 1.38 us: local(): pl.pallas_call(functools.partial(finish, planes), out_shape=jax.ShapeDtyp...]
  transfers between devices with their start and end apart: 5 -> 5, of which waited for: 3 -> 3; matrix products, arithmetic and copies ran while one was open for 0% -> 0% of each run, Pallas kernels for 0% -> 1%
where the time goes in v2:
time: 79.5 us; the launch traced here: 78.9 us
  starting transfers between devices  32.8 us (41%)
  blocking collectives  20.4 us (26%)
  waiting for transfers between devices  12.1 us (15%)
  Pallas kernels  7.78 us (10%)
  local copies, waits for them, and re-layouts  4.38 us (6%)
  between operations  1.4 us (2%)
    all_to_all x1, blocking collectives, local(): lax.all_to_all(send, BOTH, 0, 0, axis_index_groups=ids.tolist(), tiled=True)  20.4 us
    ppermute x4, starting transfers between devices, exchange(): return (lax.ppermute(last, axis, up), lax.ppermute(first, axis, down))  17.6 us
    all_to_all x1, starting transfers between devices, local(): lax.all_to_all(send, BOTH, 0, 0, axis_index_groups=ids.T.tolist(), tiled=...  15.2 us
    all_to_all x1, waiting for transfers between devices, local(): lax.all_to_all(send, BOTH, 0, 0, axis_index_groups=ids.T.tolist(), tiled=...  7.71 us
    ppermute x4, waiting for transfers between devices, exchange(): return (lax.ppermute(last, axis, up), lax.ppermute(first, axis, down))  4.44 us
    unnamed x20, local copies, waits for them, and re-layouts  4.38 us
    pallas_call x1, Pallas kernels, local(): pl.pallas_call(functools.partial(relax, planes), out_shape=(jax.ShapeDtyp...  3.3 us
  transfers between devices with their start and end apart: 5, of which 3 were waited for; matrix products, arithmetic and copies ran while one was open for 0% of the time, Pallas kernels for 1%

profile of v2, /device:TPU:1, one launch (start us, length us, event | category | flops | bytes accessed | tf_op | source)
XLA Modules:
  0.0 78.9 jit_solution(1967808348192299149)
XLA Ops:
  0.6 0.0 copy-start
  0.6 1.1 %copy-done = f32[3,8,16,384]{3,2,1,0:T(8,128)S(1)} copy-done((f32[3,8,16,384]{3,2,1,0:T(8,128)S(1)}, f32[3,8,16,384]{3,2,1,0:T(8,128)}, u32[]{:S(2)}) %copy-start) | copy-done | bytes 589848
  1.7 0.0 copy-start.1
  1.7 1.1 %copy-done.1 = f32[3,8,16,384]{3,2,1,0:T(8,128)S(1)} copy-done((f32[3,8,16,384]{3,2,1,0:T(8,128)S(1)}, f32[3,8,16,384]{3,2,1,0:T(8,128)}, u32[]{:S(2)}) %copy-start.1) | copy-done | bytes 589848
  2.8 0.0 copy-start.3
  2.8 0.9 %copy-done.3 = s32[8,16,384]{2,1,0:T(8,128)S(1)} copy-done((s32[8,16,384]{2,1,0:T(8,128)S(1)}, s32[8,16,384]{2,1,0:T(8,128)}, u32[]{:S(2)}) %copy-start.3) | copy-done | bytes 196632
  3.7 0.0 copy-start.6
  3.7 0.7 copy-done.6
  4.3 0.0 copy-start.7
  4.3 0.7 copy-done.7
  5.0 0.8 shard_map.122
  5.8 4.0 %collective-permute-start = (bf16[64,384]{1,0:T(8,128)(2,1)S(1)}, bf16[64,384]{1,0:T(8,128)(2,1)S(1)}, u32[]{:S(2)}, u32[]{:S(2)}) collective-permute-start(bf16[64,384]{1,0:T(8,128)(2,1)S(1)} %get-tuple-element.8), channel_id=1, source_target_pairs={{0,1},{1,2},{2,3},{3,4},{4,5},{5,6},{6,7},{8,9},{9,10},{10,11},{11... | collective-permute-start | bytes 147464 | tf_op jit(solution)/shard_map/ppermute | solution.py:298
  9.8 0.0 copy-start.4
  9.8 0.0 copy-start.9
  9.8 1.4 %collective-permute-start.1 = (bf16[64,384]{1,0:T(8,128)(2,1)S(1)}, bf16[64,384]{1,0:T(8,128)(2,1)S(1)}, u32[]{:S(2)}, u32[]{:S(2)}) collective-permute-start(bf16[64,384]{1,0:T(8,128)(2,1)S(1)} %get-tuple-element.9), channel_id=1, source_target_pairs={{1,0},{2,1},{3,2},{4,3},{5,4},{6,5},{7,6},{9,8},{10,9},{11,10},{12... | collective-permute-start | bytes 147464 | tf_op jit(solution)/shard_map/ppermute | solution.py:298
  11.3 0.0 collective-permute-done.before_ref
  11.3 3.5 %collective-permute-done.1.after_ref = bf16[64,384]{1,0:T(8,128)(2,1)S(1)} collective-permute-done((bf16[64,384]{1,0:T(8,128)(2,1)S(1)}, bf16[64,384]{1,0:T(8,128)(2,1)S(1)}, u32[]{:S(2)}, u32[]{:S(2)}) %collective-permute-start.1) | collective-permute-done | bytes 49184 | tf_op jit(solution)/shard_map/ppermute | solution.py:298
  14.8 0.7 shard_map.123
  15.5 5.1 %collective-permute-start.2 = (bf16[128,384]{1,0:T(8,128)(2,1)S(1)}, bf16[128,384]{1,0:T(8,128)(2,1)S(1)}, u32[]{:S(2)}, u32[]{:S(2)}) collective-permute-start(bf16[128,384]{1,0:T(8,128)(2,1)S(1)} %get-tuple-element.10), channel_id=1, source_target_pairs={{0,8},{8,16},{16,24},{24,32},{32,40},{40,48},{48,56},{56,64},{64,7... | collective-permute-start | bytes 294920 | tf_op jit(solution)/shard_map/ppermute | solution.py:298
  20.7 7.0 %collective-permute-start.3 = (bf16[128,384]{1,0:T(8,128)(2,1)S(1)}, bf16[128,384]{1,0:T(8,128)(2,1)S(1)}, u32[]{:S(2)}, u32[]{:S(2)}) collective-permute-start(bf16[128,384]{1,0:T(8,128)(2,1)S(1)} %get-tuple-element.11), channel_id=1, source_target_pairs={{8,0},{16,8},{24,16},{32,24},{40,32},{48,40},{56,48},{64,56},{72,6... | collective-permute-start | bytes 294920 | tf_op jit(solution)/shard_map/ppermute | solution.py:298
  27.7 0.0 collective-permute-done.2.below_ref
  27.7 0.9 %collective-permute-done.3.above_ref = bf16[128,384]{1,0:T(8,128)(2,1)S(1)} collective-permute-done((bf16[128,384]{1,0:T(8,128)(2,1)S(1)}, bf16[128,384]{1,0:T(8,128)(2,1)S(1)}, u32[]{:S(2)}, u32[]{:S(2)}) %collective-permute-start.3) | collective-permute-done | bytes 98336 | tf_op jit(solution)/shard_map/ppermute | solution.py:298
  28.6 0.0 copy-done.4
  28.6 0.0 copy-done.9
  28.6 0.0 copy-start.2
  28.6 0.0 copy-start.8
  28.6 3.3 %shard_map.124 = (f32[3,128,384]{2,1,0:T(8,128)}, bf16[64,4,128]{2,1,0:T(4,128)(2,1)S(1)}) custom-call(f32[8]{0:T(128)S(1)} %copy-done.6, f32[8]{0:T(128)S(1)} %copy-done.7, f32[3,128,384]{2,1,0:T(8,128)S(1)} %bitcast.13, f32[3,128,384]{2,1,0:T(8,128)S(1)} %bitcast.17, s32[128,384]{1,0:T(8,128)S(1)} %bitcast.23, ...), custom_call_target="tpu_custom_call" | custom-call | tf_op jit(solution)/shard_map/pallas_call | solution.py:339
  31.9 0.0 copy-start.5
  31.9 20.4 %all_to_all.10.got_ref = bf16[64,4,128]{2,1,0:T(4,128)(2,1)S(1)} all-to-all(bf16[64,4,128]{2,1,0:T(4,128)(2,1)S(1)} %get-tuple-element.13), channel_id=1, replica_groups={{0,1,2,3,4,5,6,7,8,9,10,11,12,13,14,15,16,17,18,19,20,21,22,23,24,25,26..., dimensions={0} | all-to-all | bytes 131072 | tf_op jit(solution)/shard_map/all_to_all | solution.py:354
  52.4 0.7 shard_map.126
  53.1 15.2 %all-to-all-start.1 = ((bf16[12,8,128]{2,1,0:T(8,128)(2,1)}), bf16[12,8,128]{2,1,0:T(8,128)(2,1)S(1)}, u32[]{:S(2)}, u32[]{:S(2)}) async-start(bf16[12,8,128]{2,1,0:T(8,128)(2,1)} %shard_map.126), calls=%async_computation.1 | async-start | bytes 49152 | tf_op jit(solution)/shard_map/all_to_all | solution.py:362
  68.9 0.0 copy-done.2
  68.9 0.0 copy-done.8
  68.9 0.9 %shard_map.125.part_ref = f32[1,256]{1,0:T(1,128)S(1)} custom-call(s32[9]{0:T(128)S(1)} %bitcast.26, bf16[64,4,128]{2,1,0:T(4,128)(2,1)S(1)} %all_to_all.10.got_ref, bf16[2304,256]{1,0:T(8,128)(2,1)S(1)} %bitcast.18), custom_call_target="tpu_custom_call" | custom-call | flops 18874368 | bytes 1179648 | tf_op jit(solution)/shard_map/pallas_call | solution.py:365
  69.8 7.7 %all-to-all-done.1.relay_ref = bf16[12,8,128]{2,1,0:T(8,128)(2,1)S(1)} async-done(((bf16[12,8,128]{2,1,0:T(8,128)(2,1)}), bf16[12,8,128]{2,1,0:T(8,128)(2,1)S(1)}, u32[]{:S(2)}, u32[]{:S(2)}) %all-to-all-start.1) | async-done | bytes 24608 | tf_op jit(solution)/shard_map/all_to_all | solution.py:362
  77.5 0.0 copy-done.5
  77.5 1.4 %shard_map.127 = f32[1,256]{1,0:T(1,128)} custom-call(s32[9]{0:T(128)S(1)} %bitcast.27, s32[1]{0:T(128)S(6)} %copy.13.rank_ref, f32[1,256]{1,0:T(1,128)S(1)} %shard_map.125.part_ref, bf16[12,8,128]{2,1,0:T(8,128)(2,1)S(1)} %all-to-all-done.1.relay_ref, bf16[2304,256]{1,0:T(8,128)(2,1)S(1)} %bitcast.19, bf16[16,256]{1,0:T(8,128)(2,1)S(1)} %bitcast.25), custom_call_target="tpu_custom_call" | custom-call | tf_op jit(solution)/shard_map/pallas_call | solution.py:373
Async XLA Ops:
  0.6 1.1 %copy-start = (f32[3,8,16,384]{3,2,1,0:T(8,128)S(1)}, f32[3,8,16,384]{3,2,1,0:T(8,128)}, u32[]{:S(2)}) copy-start(f32[3,8,16,384]{3,2,1,0:T(8,128)} %param.11) | copy-start | bytes 1769476
  1.7 1.1 %copy-start.1 = (f32[3,8,16,384]{3,2,1,0:T(8,128)S(1)}, f32[3,8,16,384]{3,2,1,0:T(8,128)}, u32[]{:S(2)}) copy-start(f32[3,8,16,384]{3,2,1,0:T(8,128)} %param.12) | copy-start | bytes 1769476
  2.8 0.9 %copy-start.3 = (s32[8,16,384]{2,1,0:T(8,128)S(1)}, s32[8,16,384]{2,1,0:T(8,128)}, u32[]{:S(2)}) copy-start(s32[8,16,384]{2,1,0:T(8,128)} %param.13) | copy-start | bytes 589828
  3.7 0.7 copy-start.6
  4.3 0.7 copy-start.7
  5.8 5.5 %collective-permute-start = (bf16[64,384]{1,0:T(8,128)(2,1)S(1)}, bf16[64,384]{1,0:T(8,128)(2,1)S(1)}, u32[]{:S(2)}, u32[]{:S(2)}) collective-permute-start(bf16[64,384]{1,0:T(8,128)(2,1)S(1)} %get-tuple-element.8), channel_id=1, source_target_pairs={{0,1},{1,2},{2,3},{3,4},{4,5},{5,6},{6,7},{8,9},{9,10},{10,11},{11... | collective-permute-start | bytes 147464 | tf_op jit(solution)/shard_map/ppermute | solution.py:298
  9.8 18.8 %copy-start.4 = (bf16[16,96,1,1,256]{4,1,3,2,0:T(8,128)(2,1)S(1)}, bf16[16,96,1,1,256]{4,1,3,2,0:T(8,128)(2,1)}, u32[]{:S(2)}) copy-start(bf16[16,96,1,1,256]{4,1,3,2,0:T(8,128)(2,1)} %param.20) | copy-start | bytes 2359300
  9.8 18.8 %copy-start.9 = (s32[1,1,256]{2,1,0:T(1,128)S(1)}, s32[1,1,256]{2,1,0:T(1,128)}, u32[]{:S(2)}) copy-start(s32[1,1,256]{2,1,0:T(1,128)} %param.16) | copy-start | bytes 3076
  9.8 5.0 %collective-permute-start.1 = (bf16[64,384]{1,0:T(8,128)(2,1)S(1)}, bf16[64,384]{1,0:T(8,128)(2,1)S(1)}, u32[]{:S(2)}, u32[]{:S(2)}) collective-permute-start(bf16[64,384]{1,0:T(8,128)(2,1)S(1)} %get-tuple-element.9), channel_id=1, source_target_pairs={{1,0},{2,1},{3,2},{4,3},{5,4},{6,5},{7,6},{9,8},{10,9},{11,10},{12... | collective-permute-start | bytes 147464 | tf_op jit(solution)/shard_map/ppermute | solution.py:298
  15.5 12.1 %collective-permute-start.2 = (bf16[128,384]{1,0:T(8,128)(2,1)S(1)}, bf16[128,384]{1,0:T(8,128)(2,1)S(1)}, u32[]{:S(2)}, u32[]{:S(2)}) collective-permute-start(bf16[128,384]{1,0:T(8,128)(2,1)S(1)} %get-tuple-element.10), channel_id=1, source_target_pairs={{0,8},{8,16},{16,24},{24,32},{32,40},{40,48},{48,56},{56,64},{64,7... | collective-permute-start | bytes 294920 | tf_op jit(solution)/shard_map/ppermute | solution.py:298
  20.7 8.0 %collective-permute-start.3 = (bf16[128,384]{1,0:T(8,128)(2,1)S(1)}, bf16[128,384]{1,0:T(8,128)(2,1)S(1)}, u32[]{:S(2)}, u32[]{:S(2)}) collective-permute-start(bf16[128,384]{1,0:T(8,128)(2,1)S(1)} %get-tuple-element.11), channel_id=1, source_target_pairs={{8,0},{16,8},{24,16},{32,24},{40,32},{48,40},{56,48},{64,56},{72,6... | collective-permute-start | bytes 294920 | tf_op jit(solution)/shard_map/ppermute | solution.py:298
  28.6 40.3 %copy-start.2 = (bf16[1,1,9,256,256]{4,3,2,1,0:T(8,128)(2,1)S(1)}, bf16[1,1,9,256,256]{4,3,2,1,0:T(8,128)(2,1)}, u32[]{:S(2)}) copy-start(bf16[1,1,9,256,256]{4,3,2,1,0:T(8,128)(2,1)} %param.17) | copy-start | bytes 3538948
  28.6 40.3 %copy-start.8 = (s32[1,1,9]{2,1,0:T(1,128)S(1)}, s32[1,1,9]{2,1,0:T(1,128)}, u32[]{:S(2)}) copy-start(s32[1,1,9]{2,1,0:T(1,128)} %param.18) | copy-start | bytes 112
  31.9 45.6 %copy-start.5 = (bf16[16,1,1,256]{3,0,2,1:T(8,128)(2,1)S(1)}, bf16[16,1,1,256]{3,0,2,1:T(8,128)(2,1)}, u32[]{:S(2)}) copy-start(bf16[16,1,1,256]{3,0,2,1:T(8,128)(2,1)} %param.19) | copy-start | bytes 24580
  53.1 24.5 %all-to-all-start.1 = ((bf16[12,8,128]{2,1,0:T(8,128)(2,1)}), bf16[12,8,128]{2,1,0:T(8,128)(2,1)S(1)}, u32[]{:S(2)}, u32[]{:S(2)}) async-start(bf16[12,8,128]{2,1,0:T(8,128)(2,1)} %shard_map.126), calls=%async_computation.1 | async-start | bytes 49152 | tf_op jit(solution)/shard_map/all_to_all | solution.py:362

commit v3 on v2

--- a/solution.py
+++ b/solution.py
@@ -130,62 +130,102 @@
     return jnp.sum(jnp.where(down == along, row, 0.0), axis=1, keepdims=True)
 
 
-def relax(planes, stiff_ref, mass_ref, field_ref, source_ref, material_ref, before_ref, after_ref, below_ref, above_ref,
-          right_ref, cells_ref, out_ref, send_ref, once_ref, scaled_ref, coupling_ref, plain_ref):
+def bands(ref, count):
+    return [ref[16 * k:16 * k + 16, :].astype(F32) for k in range(count)]
+
+
+EDGES = (0, 1, 6, 7)
+
+
+def relax_inner(stiff_ref, mass_ref, field_ref, source_ref, material_ref, before_ref, after_ref, cells_ref,
+                once_ref, scaled_ref, coupling_ref, rim_ref, out_ref, edge_ref, place_ref, spread_ref, plain_ref):
     rows = table_rows(stiff_ref, mass_ref)
-    y_halo = [[r[16 * k:16 * k + 16, :].astype(F32) for k in range(4)] for r in (before_ref, after_ref)]
-    z_halo = [[r[16 * k:16 * k + 16, :].astype(F32) for k in range(8)] for r in (below_ref, above_ref)]
+    halo = [bands(before_ref, 4), bands(after_ref, 4)]
 
     def y_plane(side, k):
-        return y_halo[side][k // 2][8 * (k % 2):8 * (k % 2) + 8]
-
-    row8 = lax.broadcasted_iota(jnp.int32, (8, field_ref.shape[-1]), 0)
-    rims = []
+        return halo[side][k // 2][8 * (k % 2):8 * (k % 2) + 8]
+
     for c in range(3):
-        once_ref[c, 0] = z_halo[0][3 + c] + z_halo[0][6] * field_ref[c, 0:16, :]
-        once_ref[c, 9] = z_halo[1][3 + c] + z_halo[1][6] * field_ref[c, 112:128, :]
-        sides = []
         for side, y in ((0, 0), (1, 15)):
-            beside = line_rows(field_ref, y, c)
-            at = 2 * c + side
-            beside = beside + jnp.where(row8 == 0, z_halo[0][7][at:at + 1], 0.0)
-            beside = beside + jnp.where(row8 == 7, z_halo[1][7][at:at + 1], 0.0)
-            sides.append(y_plane(side, 3 + c) + y_plane(side, 6) * beside)
-        rims.append(sides)
+            rim_ref[6 * side + c] = y_plane(side, 3 + c) + y_plane(side, 6) * line_rows(field_ref, y, c)
+    for side in range(2):
+        rim_ref[6 * side + 3] = y_plane(side, 6)
     for z in range(8):
         here = slice(16 * z, 16 * z + 16)
         weight, coupling = lookup(material_ref[here, :], rows)
         coupling_ref[here, :] = coupling
         for c in range(3):
             value = field_ref[c, here, :]
-            lower = z_halo[0][c] if z == 0 else field_ref[c, 16 * z - 16:16 * z, :]
-            upper = z_halo[1][c] if z == 7 else field_ref[c, 16 * z + 16:16 * z + 32, :]
-            total = lower + upper + row_sum(value, y_plane(0, c)[z:z + 1], y_plane(1, c)[z:z + 1]) + x_sum(value)
+            total = row_sum(value, y_plane(0, c)[z:z + 1], y_plane(1, c)[z:z + 1]) + x_sum(value)
+            if z > 0:
+                total = total + field_ref[c, 16 * z - 16:16 * z, :]
+            if z < 7:
+                total = total + field_ref[c, 16 * z + 16:16 * z + 32, :]
             scaled = weight * source_ref[c, here, :]
             scaled_ref[c, here, :] = scaled
-            once_ref[c, z + 1] = KEEP * value + scaled + coupling * total
-    for z in range(8):
+            once_ref[c, here, :] = KEEP * value + scaled + coupling * total
+    for z in range(2, 6):
         here = slice(16 * z, 16 * z + 16)
-        coupling = coupling_ref[here, :]
         for c in range(3):
-            value = once_ref[c, z + 1]
-            total = once_ref[c, z] + once_ref[c, z + 2] + x_sum(value)
-            total = total + row_sum(value, rims[c][0][z:z + 1], rims[c][1][z:z + 1])
-            result = KEEP * value + scaled_ref[c, here, :] + coupling * total
-            out_ref[c, here, :] = result
-            plain_ref[128 * c + 16 * z:128 * c + 16 * z + 16, :] = result.astype(BF16)
+            value = once_ref[c, here, :]
+            total = once_ref[c, 16 * z - 16:16 * z, :] + once_ref[c, 16 * z + 16:16 * z + 32, :] + x_sum(value)
+            total = total + row_sum(value, rim_ref[c, z:z + 1, :], rim_ref[6 + c, z:z + 1, :])
+            result = KEEP * value + scaled_ref[c, here, :] + coupling_ref[here, :] * total
+            out_ref[c, 16 * z - 32:16 * z - 16, :] = result
+            at = 64 * c + 16 * z - 32
+            plain_ref[at:at + 16, :] = result.astype(BF16)
 
     width = field_ref.shape[-1]
     count = cells_ref.shape[1]
     cells = cells_ref[...].astype(F32)
     line = jnp.floor((cells + 0.5) * (1.0 / width))
+    place_column = column_of(cells - width * line)
     line_column = column_of(line)
-    place_column = column_of(cells - width * line)
-    along = lax.broadcasted_iota(jnp.int32, (count, width), 1).astype(F32)
-    chosen = jnp.where(along == line_column, 1.0, 0.0).astype(BF16)
+    place_ref[...] = jnp.broadcast_to(place_column, (count, 128))
+    along = lax.broadcasted_iota(jnp.int32, (count, 192), 1).astype(F32)
+    part = jnp.floor(along * (1.0 / 64) + 0.001)
+    shift = along - 64.0 * part
+    inner = 128.0 * part + shift + 32.0
+    outer = 128.0 * part + jnp.where(shift < 32.0, shift, shift + 64.0)
+    edge_ref[...] = jnp.where(outer == line_column, 1.0, 0.0).astype(BF16)
+    chosen = jnp.where(inner == line_column, 1.0, 0.0).astype(BF16)
     picked = jnp.dot(chosen, plain_ref[...], preferred_element_type=F32)
+    spread_ref[...] = spread_of(picked, place_column)
+
+
+def spread_of(picked, place_column):
+    along = lax.broadcasted_iota(jnp.int32, picked.shape, 1).astype(F32)
     single = jnp.where(along == place_column, picked, 0.0).astype(BF16)
-    spread = jnp.dot(single, jnp.ones((width, 128), BF16), preferred_element_type=F32)
+    return jnp.dot(single, jnp.ones((picked.shape[1], 128), BF16), preferred_element_type=F32)
+
+
+def relax_edges(planes, field_ref, once_ref, scaled_ref, coupling_ref, rim_ref, inner_ref, edge_ref, place_ref, spread_ref,
+                below_ref, above_ref, right_ref, out_ref, send_ref, plain_ref):
+    halo = [bands(below_ref, 8), bands(above_ref, 8)]
+    row8 = lax.broadcasted_iota(jnp.int32, (8, field_ref.shape[-1]), 0)
+    for c in range(3):
+        out_ref[c, 32:96, :] = inner_ref[c]
+        once = {z: once_ref[c, 16 * z:16 * z + 16, :] for z in (1, 2, 5, 6)}
+        once[0] = once_ref[c, 0:16, :] + coupling_ref[0:16, :] * halo[0][c]
+        once[7] = once_ref[c, 112:128, :] + coupling_ref[112:128, :] * halo[1][c]
+        once[-1] = halo[0][3 + c] + halo[0][6] * field_ref[c, 0:16, :]
+        once[8] = halo[1][3 + c] + halo[1][6] * field_ref[c, 112:128, :]
+        rims = []
+        for side in range(2):
+            at = 2 * c + side
+            corner = jnp.where(row8 == 0, halo[0][7][at:at + 1], 0.0) + jnp.where(row8 == 7, halo[1][7][at:at + 1], 0.0)
+            rims.append(rim_ref[6 * side + c] + rim_ref[6 * side + 3] * corner)
+        for order, z in enumerate(EDGES):
+            here = slice(16 * z, 16 * z + 16)
+            total = once[z - 1] + once[z + 1] + x_sum(once[z])
+            total = total + row_sum(once[z], rims[0][z:z + 1], rims[1][z:z + 1])
+            result = KEEP * once[z] + scaled_ref[c, here, :] + coupling_ref[here, :] * total
+            out_ref[c, here, :] = result
+            at = 64 * c + 16 * order
+            plain_ref[at:at + 16, :] = result.astype(BF16)
+
+    picked = jnp.dot(edge_ref[...], plain_ref[...], preferred_element_type=F32)
+    spread = spread_ref[...] + spread_of(picked, place_ref[:, 0:1])
     far = jnp.dot(right_ref[...], spread.astype(BF16), preferred_element_type=F32)
     ranks = 16
     lane = lax.broadcasted_iota(jnp.int32, (PLANE, 128), 1)
@@ -305,6 +345,7 @@
     field = initial_field.reshape(3, 128, 384)
     sources = source.reshape(3, 128, 384)
     cells = material.reshape(128, 384)
+    volume = jax.ShapeDtypeStruct((3, 128, 384), F32)
     face = jax.ShapeDtypeStruct((64, 384), BF16)
     params = pltpu.CompilerParams(vmem_limit_bytes=24 * 1024 * 1024)
     first, last = pl.pallas_call(
@@ -316,7 +357,7 @@
             pltpu.SMEM((8,), F32), pltpu.SMEM((8,), F32), pltpu.VMEM((3, 128, 384), F32), pltpu.VMEM((3, 128, 384), F32),
             pltpu.VMEM((128, 384), jnp.int32), pltpu.SemaphoreType.DMA((5,)),
         ],
-        compiler_params=pltpu.CompilerParams(vmem_limit_bytes=48 * 1024 * 1024),
+        compiler_params=pltpu.CompilerParams(vmem_limit_bytes=56000 * 1024),
     )(stiffness_table, mass_table, field, sources, cells)
     before, after = exchange(first, last, "tile")
     face = jax.ShapeDtypeStruct((128, 384), BF16)
@@ -336,20 +377,27 @@
     )(stiffness_table, mass_table, field, field, sources, sources, cells, cells, before, after)
     below, above = exchange(first, last, "slab")
     members = PLANE * tiles
+    state = pl.pallas_call(
+        relax_inner,
+        out_shape=(
+            volume, volume, jax.ShapeDtypeStruct((128, 384), F32), jax.ShapeDtypeStruct((12, 8, 384), F32),
+            jax.ShapeDtypeStruct((3, 64, 384), F32), jax.ShapeDtypeStruct((256, 192), BF16),
+            jax.ShapeDtypeStruct((256, 128), F32), jax.ShapeDtypeStruct((256, 128), F32),
+        ),
+        in_specs=[smem(), smem()] + [vmem()] * 6,
+        out_specs=(vmem(),) * 8,
+        scratch_shapes=[pltpu.VMEM((192, 384), BF16)],
+        compiler_params=params,
+        cost_estimate=pl.CostEstimate(flops=6_000_000, bytes_accessed=4_000_000, transcendentals=0),
+    )(stiffness_table, mass_table, field, sources, cells, before, after, trace_cells.reshape(1, 256))
     result, send = pl.pallas_call(
-        functools.partial(relax, planes),
-        out_shape=(jax.ShapeDtypeStruct((3, 128, 384), F32), jax.ShapeDtypeStruct((members, 4, 128), BF16)),
-        in_specs=[smem(), smem()] + [vmem()] * 9,
+        functools.partial(relax_edges, planes),
+        out_shape=(volume, jax.ShapeDtypeStruct((members, 4, 128), BF16)),
+        in_specs=[vmem()] * 12,
         out_specs=(vmem(), vmem()),
-        scratch_shapes=[
-            pltpu.VMEM((3, 10, 16, 384), F32),
-            pltpu.VMEM((3, 128, 384), F32),
-            pltpu.VMEM((128, 384), F32),
-            pltpu.VMEM((384, 384), BF16),
-        ],
-        compiler_params=params,
-    )(stiffness_table, mass_table, field, sources, cells, before, after, below, above,
-      far_right.reshape(-1, 256), trace_cells.reshape(1, 256))
+        scratch_shapes=[pltpu.VMEM((192, 384), BF16)],
+        compiler_params=params,
+    )(field, *state, below, above, far_right.reshape(-1, 256))
     ids = np.arange(slabs * tiles).reshape(planes, members)
     got = lax.all_to_all(send, BOTH, 0, 0, axis_index_groups=ids.tolist(), tiled=True)
     send = pl.pallas_call(

time: 79.5 us -> 75.2 us (0.946)
  local copies, waits for them, and re-layouts: 4.38 us -> 0.05 us
  Pallas kernels: 7.78 us -> 9.56 us
  blocking collectives: 20.4 us -> 19.4 us
    unnamed x20, local copies, waits for them, and re-layouts: 4.38 us -> 0.05 us
    pallas_call x1, Pallas kernels: 0.78 us -> 2.27 us  [local(): pl.pallas_call(y_faces, out_shape=(face, face), in_specs=[pl.BlockSpec(me...]
    all_to_all x1, blocking collectives: 20.4 us -> 19.4 us  [local(): lax.all_to_all(send, BOTH, 0, 0, axis_index_groups=ids.tolist(), tiled=True)]
    pallas_call x1 -> x2, Pallas kernels: 3.3 us -> 3.58 us  [the longest x1 1.84 us: local(): pl.pallas_call(relax_inner, out_shape=(volume, volume, jax.ShapeDtypeStru...]
  transfers between devices with their start and end apart: 5 -> 5, of which waited for: 3 -> 3; matrix products, arithmetic and copies ran while one was open for 0% -> 0% of each run, Pallas kernels for 1% -> 4%
where the time goes in v3:
time: 75.2 us; the launch traced here: 74.8 us
  starting transfers between devices  32.8 us (44%)
  blocking collectives  19.4 us (26%)
  waiting for transfers between devices  11.5 us (15%)
  Pallas kernels  9.56 us (13%)
  between operations  1.48 us (2%)
    all_to_all x1, blocking collectives, local(): lax.all_to_all(send, BOTH, 0, 0, axis_index_groups=ids.tolist(), tiled=True)  19.4 us
    ppermute x4, starting transfers between devices, exchange(): return (lax.ppermute(last, axis, up), lax.ppermute(first, axis, down))  17.6 us
    all_to_all x1, starting transfers between devices, local(): lax.all_to_all(send, BOTH, 0, 0, axis_index_groups=ids.T.tolist(), tiled=...  15.2 us
    all_to_all x1, waiting for transfers between devices, local(): lax.all_to_all(send, BOTH, 0, 0, axis_index_groups=ids.T.tolist(), tiled=...  7.71 us
    ppermute x4, waiting for transfers between devices, exchange(): return (lax.ppermute(last, axis, up), lax.ppermute(first, axis, down))  3.75 us
    pallas_call x1, Pallas kernels, local(): pl.pallas_call(y_faces, out_shape=(face, face), in_specs=[pl.BlockSpec(me...  2.27 us
    pallas_call x1, Pallas kernels, local(): pl.pallas_call(relax_inner, out_shape=(volume, volume, jax.ShapeDtypeStru...  1.84 us
    pallas_call x1, Pallas kernels, local(): pl.pallas_call(functools.partial(relax_edges, planes), out_shape=(volume,...  1.74 us
  transfers between devices with their start and end apart: 5, of which 3 were waited for; matrix products, arithmetic and copies ran while one was open for 0% of the time, Pallas kernels for 4%

profile of v3, /device:TPU:1, one launch (start us, length us, event | category | flops | bytes accessed | tf_op | source)
XLA Modules:
  0.0 74.8 jit_solution(4217263401013853843)
XLA Ops:
  0.6 0.0 copy-start
  0.6 0.0 copy-start.1
  0.7 0.0 copy-start.3
  0.7 0.0 copy-start.6
  0.7 0.0 copy-start.7
  0.7 2.3 %shard_map.122 = (bf16[64,384]{1,0:T(8,128)(2,1)}, bf16[64,384]{1,0:T(8,128)(2,1)}) custom-call(f32[8]{0:T(128)} %stiff_ref.3, f32[8]{0:T(128)} %mass_ref.3, f32[3,128,384]{2,1,0:T(8,128)} %bitcast.10, f32[3,128,384]{2,1,0:T(8,128)} %bitcast.15, s32[128,384]{1,0:T(8,128)} %bitcast.21), custom_call_target="tpu_custom_call" | custom-call | tf_op jit(solution)/shard_map/pallas_call | solution.py:351
  3.0 4.0 %collective-permute-start = (bf16[64,384]{1,0:T(8,128)(2,1)}, bf16[64,384]{1,0:T(8,128)(2,1)S(1)}, u32[]{:S(2)}, u32[]{:S(2)}) collective-permute-start(bf16[64,384]{1,0:T(8,128)(2,1)} %get-tuple-element.16), channel_id=1, source_target_pairs={{0,1},{1,2},{2,3},{3,4},{4,5},{5,6},{6,7},{8,9},{9,10},{10,11},{11... | collective-permute-start | bytes 147464 | tf_op jit(solution)/shard_map/ppermute | solution.py:338
  7.0 0.0 copy-start.9
  7.0 1.3 %collective-permute-start.1 = (bf16[64,384]{1,0:T(8,128)(2,1)}, bf16[64,384]{1,0:T(8,128)(2,1)S(1)}, u32[]{:S(2)}, u32[]{:S(2)}) collective-permute-start(bf16[64,384]{1,0:T(8,128)(2,1)} %get-tuple-element.17), channel_id=1, source_target_pairs={{1,0},{2,1},{3,2},{4,3},{5,4},{6,5},{7,6},{9,8},{10,9},{11,10},{12... | collective-permute-start | bytes 147464 | tf_op jit(solution)/shard_map/ppermute | solution.py:338
  8.3 0.2 collective-permute-done.before_ref
  8.5 3.6 %collective-permute-done.1.after_ref = bf16[64,384]{1,0:T(8,128)(2,1)S(1)} collective-permute-done((bf16[64,384]{1,0:T(8,128)(2,1)}, bf16[64,384]{1,0:T(8,128)(2,1)S(1)}, u32[]{:S(2)}, u32[]{:S(2)}) %collective-permute-start.1) | collective-permute-done | bytes 49184 | tf_op jit(solution)/shard_map/ppermute | solution.py:338
  12.1 0.0 copy-done
  12.1 0.0 copy-done.1
  12.1 0.0 copy-done.3
  12.1 0.0 copy-done.6
  12.1 0.0 copy-done.7
  12.1 0.7 shard_map.124
  12.8 0.0 copy-start.4
  12.8 5.2 %collective-permute-start.2 = (bf16[128,384]{1,0:T(8,128)(2,1)S(1)}, bf16[128,384]{1,0:T(8,128)(2,1)S(1)}, u32[]{:S(2)}, u32[]{:S(2)}) collective-permute-start(bf16[128,384]{1,0:T(8,128)(2,1)S(1)} %get-tuple-element.26), channel_id=1, source_target_pairs={{0,8},{8,16},{16,24},{24,32},{32,40},{40,48},{48,56},{56,64},{64,7... | collective-permute-start | bytes 294920 | tf_op jit(solution)/shard_map/ppermute | solution.py:338
  18.1 7.0 %collective-permute-start.3 = (bf16[128,384]{1,0:T(8,128)(2,1)S(1)}, bf16[128,384]{1,0:T(8,128)(2,1)S(1)}, u32[]{:S(2)}, u32[]{:S(2)}) collective-permute-start(bf16[128,384]{1,0:T(8,128)(2,1)S(1)} %get-tuple-element.27), channel_id=1, source_target_pairs={{8,0},{16,8},{24,16},{32,24},{40,32},{48,40},{56,48},{64,56},{72,6... | collective-permute-start | bytes 294920 | tf_op jit(solution)/shard_map/ppermute | solution.py:338
  25.1 0.0 copy-done.9
  25.1 1.8 %shard_map.123 = (f32[3,128,384]{2,1,0:T(8,128)S(1)}, f32[3,128,384]{2,1,0:T(8,128)S(1)}, f32[128,384]{1,0:T(8,128)S(1)}, f32[12,8,384]{2,1,0:T(8,128)S(1)}, f32...) custom-call(f32[8]{0:T(128)S(1)} %copy-done.6, ...), custom_call_target="tpu_custom_call" | custom-call | flops 6000000 | bytes 4000000 | tf_op jit(solution)/shard_map/pallas_call | solution.py:380
  27.0 0.0 collective-permute-done.2.below_ref
  27.0 0.0 collective-permute-done.3.above_ref
  27.0 0.0 copy-done.4
  27.0 0.0 copy-start.2
  27.0 0.0 copy-start.8
  27.0 1.7 %shard_map.125 = (f32[3,128,384]{2,1,0:T(8,128)}, bf16[64,4,128]{2,1,0:T(4,128)(2,1)S(1)}) custom-call(f32[3,128,384]{2,1,0:T(8,128)S(1)} %bitcast.14, f32[3,128,384]{2,1,0:T(8,128)S(1)} %get-tuple-element.18.once_ref, f32[3,128,384]{2,1,0:T(8,128)S(1)} %get-tuple-element.19.scaled_ref, f32[128,384]{1,0:T(8,128)S(1)} %get-tuple-element.20.coupling_ref, ...), custom_call_target="tpu_custom_call" | custom-call | tf_op jit(solution)/shard_map/pallas_call | solution.py:393
  28.8 0.0 copy-start.5
  28.8 19.4 %all_to_all.10.got_ref = bf16[64,4,128]{2,1,0:T(4,128)(2,1)S(1)} all-to-all(bf16[64,4,128]{2,1,0:T(4,128)(2,1)S(1)} %get-tuple-element.29), channel_id=1, replica_groups={{0,1,2,3,4,5,6,7,8,9,10,11,12,13,14,15,16,17,18,19,20,21,22,23,24,25,26..., dimensions={0} | all-to-all | bytes 131072 | tf_op jit(solution)/shard_map/all_to_all | solution.py:402
  48.2 0.7 shard_map.127
  48.9 15.2 %all-to-all-start.1 = ((bf16[12,8,128]{2,1,0:T(8,128)(2,1)}), bf16[12,8,128]{2,1,0:T(8,128)(2,1)S(1)}, u32[]{:S(2)}, u32[]{:S(2)}) async-start(bf16[12,8,128]{2,1,0:T(8,128)(2,1)} %shard_map.127), calls=%async_computation.1 | async-start | bytes 49152 | tf_op jit(solution)/shard_map/all_to_all | solution.py:410
  64.7 0.0 copy-done.2
  64.7 0.0 copy-done.8
  64.8 0.9 %shard_map.126.part_ref = f32[1,256]{1,0:T(1,128)S(1)} custom-call(s32[9]{0:T(128)S(1)} %bitcast.27, bf16[64,4,128]{2,1,0:T(4,128)(2,1)S(1)} %all_to_all.10.got_ref, bf16[2304,256]{1,0:T(8,128)(2,1)S(1)} %bitcast.19), custom_call_target="tpu_custom_call" | custom-call | flops 18874368 | bytes 1179648 | tf_op jit(solution)/shard_map/pallas_call | solution.py:413
  65.7 7.7 %all-to-all-done.1.relay_ref = bf16[12,8,128]{2,1,0:T(8,128)(2,1)S(1)} async-done(((bf16[12,8,128]{2,1,0:T(8,128)(2,1)}), bf16[12,8,128]{2,1,0:T(8,128)(2,1)S(1)}, u32[]{:S(2)}, u32[]{:S(2)}) %all-to-all-start.1) | async-done | bytes 24608 | tf_op jit(solution)/shard_map/all_to_all | solution.py:410
  73.4 0.0 copy-done.5
  73.4 1.4 %shard_map.128 = f32[1,256]{1,0:T(1,128)} custom-call(s32[9]{0:T(128)S(1)} %bitcast.28, s32[1]{0:T(128)S(6)} %copy.13.rank_ref, f32[1,256]{1,0:T(1,128)S(1)} %shard_map.126.part_ref, bf16[12,8,128]{2,1,0:T(8,128)(2,1)S(1)} %all-to-all-done.1.relay_ref, bf16[2304,256]{1,0:T(8,128)(2,1)S(1)} %bitcast.20, bf16[16,256]{1,0:T(8,128)(2,1)S(1)} %bitcast.26), custom_call_target="tpu_custom_call" | custom-call | tf_op jit(solution)/shard_map/pallas_call | solution.py:421
Async XLA Ops:
  0.6 11.4 %copy-start = (f32[3,8,16,384]{3,2,1,0:T(8,128)S(1)}, f32[3,8,16,384]{3,2,1,0:T(8,128)}, u32[]{:S(2)}) copy-start(f32[3,8,16,384]{3,2,1,0:T(8,128)} %param.11) | copy-start | bytes 1769476
  0.6 11.4 %copy-start.1 = (f32[3,8,16,384]{3,2,1,0:T(8,128)S(1)}, f32[3,8,16,384]{3,2,1,0:T(8,128)}, u32[]{:S(2)}) copy-start(f32[3,8,16,384]{3,2,1,0:T(8,128)} %param.12) | copy-start | bytes 1769476
  0.7 11.4 %copy-start.3 = (s32[8,16,384]{2,1,0:T(8,128)S(1)}, s32[8,16,384]{2,1,0:T(8,128)}, u32[]{:S(2)}) copy-start(s32[8,16,384]{2,1,0:T(8,128)} %param.13) | copy-start | bytes 589828
  0.7 11.4 %copy-start.6 = (f32[8]{0:T(128)S(1)}, f32[8]{0:T(128)}, u32[]{:S(2)}) copy-start(f32[8]{0:T(128)} %stiff_ref.3) | copy-start | bytes 100
  0.7 11.4 %copy-start.7 = (f32[8]{0:T(128)S(1)}, f32[8]{0:T(128)}, u32[]{:S(2)}) copy-start(f32[8]{0:T(128)} %mass_ref.3) | copy-start | bytes 100
  3.0 5.5 %collective-permute-start = (bf16[64,384]{1,0:T(8,128)(2,1)}, bf16[64,384]{1,0:T(8,128)(2,1)S(1)}, u32[]{:S(2)}, u32[]{:S(2)}) collective-permute-start(bf16[64,384]{1,0:T(8,128)(2,1)} %get-tuple-element.16), channel_id=1, source_target_pairs={{0,1},{1,2},{2,3},{3,4},{4,5},{5,6},{6,7},{8,9},{9,10},{10,11},{11... | collective-permute-start | bytes 147464 | tf_op jit(solution)/shard_map/ppermute | solution.py:338
  7.0 18.1 %copy-start.9 = (s32[1,1,256]{2,1,0:T(1,128)S(1)}, s32[1,1,256]{2,1,0:T(1,128)}, u32[]{:S(2)}) copy-start(s32[1,1,256]{2,1,0:T(1,128)} %param.16) | copy-start | bytes 3076
  7.0 5.0 %collective-permute-start.1 = (bf16[64,384]{1,0:T(8,128)(2,1)}, bf16[64,384]{1,0:T(8,128)(2,1)S(1)}, u32[]{:S(2)}, u32[]{:S(2)}) collective-permute-start(bf16[64,384]{1,0:T(8,128)(2,1)} %get-tuple-element.17), channel_id=1, source_target_pairs={{1,0},{2,1},{3,2},{4,3},{5,4},{6,5},{7,6},{9,8},{10,9},{11,10},{12... | collective-permute-start | bytes 147464 | tf_op jit(solution)/shard_map/ppermute | solution.py:338
  12.8 14.2 %copy-start.4 = (bf16[16,96,1,1,256]{4,1,3,2,0:T(8,128)(2,1)S(1)}, bf16[16,96,1,1,256]{4,1,3,2,0:T(8,128)(2,1)}, u32[]{:S(2)}) copy-start(bf16[16,96,1,1,256]{4,1,3,2,0:T(8,128)(2,1)} %param.20) | copy-start | bytes 2359300
  12.8 14.1 %collective-permute-start.2 = (bf16[128,384]{1,0:T(8,128)(2,1)S(1)}, bf16[128,384]{1,0:T(8,128)(2,1)S(1)}, u32[]{:S(2)}, u32[]{:S(2)}) collective-permute-start(bf16[128,384]{1,0:T(8,128)(2,1)S(1)} %get-tuple-element.26), channel_id=1, source_target_pairs={{0,8},{8,16},{16,24},{24,32},{32,40},{40,48},{48,56},{56,64},{64,7... | collective-permute-start | bytes 294920 | tf_op jit(solution)/shard_map/ppermute | solution.py:338
  18.1 8.9 %collective-permute-start.3 = (bf16[128,384]{1,0:T(8,128)(2,1)S(1)}, bf16[128,384]{1,0:T(8,128)(2,1)S(1)}, u32[]{:S(2)}, u32[]{:S(2)}) collective-permute-start(bf16[128,384]{1,0:T(8,128)(2,1)S(1)} %get-tuple-element.27), channel_id=1, source_target_pairs={{8,0},{16,8},{24,16},{32,24},{40,32},{48,40},{56,48},{64,56},{72,6... | collective-permute-start | bytes 294920 | tf_op jit(solution)/shard_map/ppermute | solution.py:338
  27.0 37.7 %copy-start.2 = (bf16[1,1,9,256,256]{4,3,2,1,0:T(8,128)(2,1)S(1)}, bf16[1,1,9,256,256]{4,3,2,1,0:T(8,128)(2,1)}, u32[]{:S(2)}) copy-start(bf16[1,1,9,256,256]{4,3,2,1,0:T(8,128)(2,1)} %param.17) | copy-start | bytes 3538948
  27.0 37.7 %copy-start.8 = (s32[1,1,9]{2,1,0:T(1,128)S(1)}, s32[1,1,9]{2,1,0:T(1,128)}, u32[]{:S(2)}) copy-start(s32[1,1,9]{2,1,0:T(1,128)} %param.18) | copy-start | bytes 112
  28.8 44.6 %copy-start.5 = (bf16[16,1,1,256]{3,0,2,1:T(8,128)(2,1)S(1)}, bf16[16,1,1,256]{3,0,2,1:T(8,128)(2,1)}, u32[]{:S(2)}) copy-start(bf16[16,1,1,256]{3,0,2,1:T(8,128)(2,1)} %param.19) | copy-start | bytes 24580
  48.9 24.5 %all-to-all-start.1 = ((bf16[12,8,128]{2,1,0:T(8,128)(2,1)}), bf16[12,8,128]{2,1,0:T(8,128)(2,1)S(1)}, u32[]{:S(2)}, u32[]{:S(2)}) async-start(bf16[12,8,128]{2,1,0:T(8,128)(2,1)} %shard_map.127), calls=%async_computation.1 | async-start | bytes 49152 | tf_op jit(solution)/shard_map/all_to_all | solution.py:410

commit v4 on v3

--- a/solution.py
+++ b/solution.py
@@ -16,22 +16,27 @@
 BOTH = ("slab", "tile")
 
 
-def table_rows(stiff_ref, mass_ref):
-    rows = []
+def table_rows(stiff_ref, mass_ref, width):
+    weights, couplings = [], []
     for entry in range(8):
-        stiffness = jnp.full((8, 128), stiff_ref[entry], F32)
+        stiffness = jnp.full((1, width), stiff_ref[entry], F32)
         inverse = RELAX / (6.0 * stiffness + mass_ref[entry])
-        rows.append((inverse[:1, :1], (stiffness * inverse)[:1, :1]))
-    return rows
+        weights.append(inverse)
+        couplings.append(stiffness * inverse)
+    return weights + couplings
+
+
+def ready_rows(table_ref):
+    return [table_ref[k:k + 1, :] for k in range(16)]
 
 
 def lookup(material, rows):
-    weight = jnp.broadcast_to(rows[0][0], material.shape)
-    coupling = jnp.broadcast_to(rows[0][1], material.shape)
+    weight = jnp.broadcast_to(rows[0], material.shape)
+    coupling = jnp.broadcast_to(rows[8], material.shape)
     for entry in range(1, 8):
         here = material == entry
-        weight = jnp.where(here, rows[entry][0], weight)
-        coupling = jnp.where(here, rows[entry][1], coupling)
+        weight = jnp.where(here, rows[entry], weight)
+        coupling = jnp.where(here, rows[8 + entry], coupling)
     return weight, coupling
 
 
@@ -60,65 +65,61 @@
     return value
 
 
-def y_faces(stiff_hbm, mass_hbm, field_hbm, source_hbm, material_hbm, first_ref, last_ref,
+def y_faces(stiff_hbm, mass_hbm, field_hbm, source_hbm, material_hbm, first_ref, last_ref, table_ref,
             stiff_ref, mass_ref, field_ref, source_ref, material_ref, sems):
-    pairs = ((stiff_hbm, stiff_ref), (mass_hbm, mass_ref), (material_hbm, material_ref), (field_hbm, field_ref), (source_hbm, source_ref))
+    pairs = [(stiff_hbm, stiff_ref), (mass_hbm, mass_ref)]
+    pairs += [(field_hbm.at[:, :, y, :], field_ref.at[k]) for k, y in enumerate((0, 15, 1, 14))]
+    pairs += [(source_hbm.at[:, :, y, :], source_ref.at[k]) for k, y in enumerate((0, 15))]
+    pairs += [(material_hbm.at[:, y, :], material_ref.at[k]) for k, y in enumerate((0, 15))]
     copies = [pltpu.make_async_copy(src, dst, sems.at[k]) for k, (src, dst) in enumerate(pairs)]
     for copy in copies:
         copy.start()
     for copy in copies:
         copy.wait()
-    rows = table_rows(stiff_ref, mass_ref)
-    for y, inner, out_ref in ((0, 1, first_ref), (15, 14, last_ref)):
-        weight, coupling = lookup(line_rows(material_ref, y), rows)
+    rows = table_rows(stiff_ref, mass_ref, table_ref.shape[1])
+    table_ref[...] = jnp.concatenate(rows, axis=0)
+    for k, out_ref in enumerate((first_ref, last_ref)):
+        weight, coupling = lookup(material_ref[k], rows)
         values, partials = [], []
         for c in range(3):
-            value = line_rows(field_ref, y, c)
-            beside = line_rows(field_ref, inner, c)
-            sources = line_rows(source_ref, y, c)
-            total = beside + row_sum(value, 0.0, 0.0) + x_sum(value)
+            value = field_ref[k, c]
+            total = field_ref[2 + k, c] + row_sum(value, 0.0, 0.0) + x_sum(value)
             values.append(value)
-            partials.append(KEEP * value + weight * sources + coupling * total)
+            partials.append(KEEP * value + weight * source_ref[k, c] + coupling * total)
         planes = values + partials + [coupling, jnp.zeros_like(coupling)]
         for pair in range(4):
             both = jnp.concatenate(planes[2 * pair:2 * pair + 2], axis=0)
             out_ref[16 * pair:16 * pair + 16, :] = both.astype(BF16)
 
 
-def z_faces(stiff_ref, mass_ref, low_ref, high_ref, low_source_ref, high_source_ref, low_material_ref, high_material_ref,
-            before_ref, after_ref, first_ref, last_ref):
-    rows = table_rows(stiff_ref, mass_ref)
-    before = [before_ref[16 * k:16 * k + 16, :].astype(F32) for k in range(2)]
-    after = [after_ref[16 * k:16 * k + 16, :].astype(F32) for k in range(2)]
-    for z, field_ref, source_ref, material_ref, out_ref in (
-        (0, low_ref, low_source_ref, low_material_ref, first_ref),
-        (7, high_ref, high_source_ref, high_material_ref, last_ref),
-    ):
-        weight, coupling = lookup(material_ref[...], rows)
-        lines = []
+def z_faces(table_ref, field_ref, source_ref, material_ref, before_ref, after_ref, far_ref, pair_ref):
+    even = lax.rem(lax.axis_index("slab"), 2) == 0
+    rows = ready_rows(table_ref)
+    before = bands(before_ref, 2)
+    after = bands(after_ref, 2)
+    faces = []
+    for z, beyond in ((0, 1), (7, 6)):
+        here, inner = slice(16 * z, 16 * z + 16), slice(16 * beyond, 16 * beyond + 16)
+        weight, coupling = lookup(material_ref[here, :], rows)
+        lines, values, partials = [], [], []
         for c in range(3):
             at = 8 * (c % 2) + z
-            lines.append((before[c // 2][at:at + 1, :], after[c // 2][at:at + 1, :]))
-            outer, inner = (0, 16) if z == 0 else (16, 0)
-            value = field_ref[c, outer:outer + 16, :]
-            beside = field_ref[c, inner:inner + 16, :]
-            total = beside + row_sum(value, *lines[c]) + x_sum(value)
-            partial = KEEP * value + weight * source_ref[c] + coupling * total
-            out_ref[16 * c:16 * c + 16, :] = value.astype(BF16)
-            out_ref[48 + 16 * c:64 + 16 * c, :] = partial.astype(BF16)
-        out_ref[96:112, :] = coupling.astype(BF16)
-        row = lax.broadcasted_iota(jnp.int32, (16, coupling.shape[1]), 0)
-        packed = jnp.zeros(row.shape, F32)
-        for c in range(3):
-            for side in range(2):
-                packed = jnp.where(row == 2 * c + side, lines[c][side], packed)
-        out_ref[112:128, :] = packed.astype(BF16)
+            lines += [before[c // 2][at:at + 1, :], after[c // 2][at:at + 1, :]]
+            value = field_ref[c, here, :]
+            total = field_ref[c, inner, :] + row_sum(value, lines[2 * c], lines[2 * c + 1]) + x_sum(value)
+            values.append(value)
+            partials.append(KEEP * value + weight * source_ref[c, here, :] + coupling * total)
+        faces.append(values + partials + [coupling, stacked(lines, 16)])
+    for k, (first, last) in enumerate(zip(*faces)):
+        here = slice(16 * k, 16 * k + 16)
+        far_ref[here, :] = jnp.where(even, first, last).astype(BF16)
+        pair_ref[here, :] = jnp.where(even, last, first).astype(BF16)
 
 
 def stacked(lines, height):
     row = lax.broadcasted_iota(jnp.int32, (height, lines[0].shape[1]), 0)
-    value = jnp.broadcast_to(lines[0], row.shape)
-    for k in range(1, len(lines)):
+    value = jnp.zeros(row.shape, F32)
+    for k in range(len(lines)):
         value = jnp.where(row == k, lines[k], value)
     return value
 
@@ -137,9 +138,9 @@
 EDGES = (0, 1, 6, 7)
 
 
-def relax_inner(stiff_ref, mass_ref, field_ref, source_ref, material_ref, before_ref, after_ref, cells_ref,
-                once_ref, scaled_ref, coupling_ref, rim_ref, out_ref, edge_ref, place_ref, spread_ref, plain_ref):
-    rows = table_rows(stiff_ref, mass_ref)
+def relax_inner(table_ref, field_ref, source_ref, material_ref, before_ref, after_ref, cells_ref,
+                once_ref, scaled_ref, coupling_ref, rim_ref, out_hbm, edge_ref, place_ref, spread_ref, plain_ref, out_ref, sems):
+    rows = ready_rows(table_ref)
     halo = [bands(before_ref, 4), bands(after_ref, 4)]
 
     def y_plane(side, k):
@@ -174,6 +175,9 @@
             out_ref[c, 16 * z - 32:16 * z - 16, :] = result
             at = 64 * c + 16 * z - 32
             plain_ref[at:at + 16, :] = result.astype(BF16)
+    copies = [pltpu.make_async_copy(out_ref.at[c], out_hbm.at[c, pl.ds(32, 64), :], sems.at[c]) for c in range(3)]
+    for copy in copies:
+        copy.start()
 
     width = field_ref.shape[-1]
     count = cells_ref.shape[1]
@@ -191,6 +195,8 @@
     chosen = jnp.where(inner == line_column, 1.0, 0.0).astype(BF16)
     picked = jnp.dot(chosen, plain_ref[...], preferred_element_type=F32)
     spread_ref[...] = spread_of(picked, place_column)
+    for copy in copies:
+        copy.wait()
 
 
 def spread_of(picked, place_column):
@@ -199,12 +205,13 @@
     return jnp.dot(single, jnp.ones((picked.shape[1], 128), BF16), preferred_element_type=F32)
 
 
-def relax_edges(planes, field_ref, once_ref, scaled_ref, coupling_ref, rim_ref, inner_ref, edge_ref, place_ref, spread_ref,
-                below_ref, above_ref, right_ref, out_ref, send_ref, plain_ref):
-    halo = [bands(below_ref, 8), bands(above_ref, 8)]
+def relax_edges(planes, field_ref, once_ref, scaled_ref, coupling_ref, rim_ref, edge_ref, place_ref, spread_ref,
+                far_ref, pair_ref, right_ref, out_ref, send_ref, plain_ref):
+    even = lax.rem(lax.axis_index("slab"), 2) == 0
+    both = list(zip(bands(far_ref, 8), bands(pair_ref, 8)))
+    halo = [[jnp.where(even, far, pair) for far, pair in both], [jnp.where(even, pair, far) for far, pair in both]]
     row8 = lax.broadcasted_iota(jnp.int32, (8, field_ref.shape[-1]), 0)
     for c in range(3):
-        out_ref[c, 32:96, :] = inner_ref[c]
         once = {z: once_ref[c, 16 * z:16 * z + 16, :] for z in (1, 2, 5, 6)}
         once[0] = once_ref[c, 0:16, :] + coupling_ref[0:16, :] * halo[0][c]
         once[7] = once_ref[c, 112:128, :] + coupling_ref[112:128, :] * halo[1][c]
@@ -220,7 +227,7 @@
             total = once[z - 1] + once[z + 1] + x_sum(once[z])
             total = total + row_sum(once[z], rims[0][z:z + 1], rims[1][z:z + 1])
             result = KEEP * once[z] + scaled_ref[c, here, :] + coupling_ref[here, :] * total
-            out_ref[c, here, :] = result
+            out_ref[c, 16 * order:16 * order + 16, :] = result
             at = 64 * c + 16 * order
             plain_ref[at:at + 16, :] = result.astype(BF16)
 
@@ -248,6 +255,19 @@
             send_ref[to * tiles + tile] = packet
 
 
+def assemble(inner_hbm, edges_ref, out_hbm, sems):
+    del inner_hbm
+    copies = []
+    for c in range(3):
+        for k, at in enumerate((0, 96)):
+            target = out_hbm.at[c, pl.ds(at, 32), :]
+            copies.append(pltpu.make_async_copy(edges_ref.at[c, pl.ds(32 * k, 32), :], target, sems.at[2 * c + k]))
+    for copy in copies:
+        copy.start()
+    for copy in copies:
+        copy.wait()
+
+
 def middle(tiles, got_ref, send_ref):
     across = lax.rem(lax.axis_index("slab"), PLANE)
     tile = lax.axis_index("tile")
@@ -268,13 +288,9 @@
             send_ref[z] = packet
 
 
-def masked_rows(rows, mask_ref, first):
-    value = jnp.zeros((16, 256), F32)
-    row = lax.broadcasted_iota(jnp.int32, value.shape, 0)
-    for k, (low, high) in enumerate(rows):
-        line = jnp.concatenate([low, high], axis=1) * mask_ref[first + k].astype(F32)
-        value = jnp.where(row == k, line, value)
-    return value.astype(BF16)
+def masked_rows(rows, factors):
+    lines = [jnp.concatenate(row, axis=1) * factor.astype(F32) for row, factor in zip(rows, factors)]
+    return stacked(lines, 16).astype(BF16)
 
 
 def products(rows, blocks, count):
@@ -296,7 +312,7 @@
             packet = got_ref[jnp.clip(up, 0, PLANE - 1) * tiles + jnp.clip(beside, 0, tiles - 1)].astype(F32)
             packet = jnp.where(inside, packet, 0.0)
             rows.append((packet[2:3, :], packet[3:4, :]))
-    out_ref[...] = products(masked_rows(rows, mask_ref, 0), near_ref[...], 9)
+    out_ref[...] = products(masked_rows(rows, [mask_ref[0:1, q:q + 1] for q in range(9)]), near_ref[...], 9)
 
 
 def finish(planes, mask_ref, rank_ref, part_ref, relay_ref, near_ref, left_ref, out_ref):
@@ -310,12 +326,13 @@
     rows = [(packet[2 + 2 * b:3 + 2 * b, :], packet[3 + 2 * b:4 + 2 * b, :]) for b in range(3)]
     first = jnp.where(upward, 6, 0)
     blocks = near_ref[pl.ds(pl.multiple_of(256 * first, 256), 768), :]
-    near = products(masked_rows(rows, mask_ref, first), blocks, 3)
+    factors = [jnp.where(upward, mask_ref[0:1, 6 + b:7 + b], mask_ref[0:1, b:b + 1]) for b in range(3)]
+    near = products(masked_rows(rows, factors), blocks, 3)
     total = jnp.sum(relay_ref[...].astype(F32), axis=0)
     total = jnp.broadcast_to(total[0:1, :] + total[1:2, :], (8, 128))
     lane = lax.broadcasted_iota(jnp.int32, total.shape, 1)
     at = 16 * lax.rem(plane, 8)
-    total = jnp.where((lane >= at) & (lane < at + rank_ref[0]), total, 0.0)
+    total = jnp.where((lane >= at) & (lane < at + rank_ref[...]), total, 0.0)
     high = total.astype(BF16).astype(F32)
     halves = jnp.concatenate([high, total - high], axis=0).astype(BF16)
     left = jnp.concatenate([left_ref[...]] * 8, axis=0)
@@ -327,8 +344,8 @@
     return pl.BlockSpec(memory_space=pltpu.VMEM)
 
 
-def smem():
-    return pl.BlockSpec(memory_space=pltpu.SMEM)
+def hbm():
+    return pl.BlockSpec(memory_space=pltpu.HBM)
 
 
 def exchange(first, last, axis):
@@ -338,66 +355,65 @@
     return lax.ppermute(last, axis, up), lax.ppermute(first, axis, down)
 
 
+def swap(far, pair, axis):
+    devices = lax.axis_size(axis)
+    far = lax.ppermute(far, axis, [(i, i + 1 if i % 2 else i - 1) for i in range(1, devices - 1)])
+    return far, lax.ppermute(pair, axis, [(i, i ^ 1) for i in range(devices)])
+
+
 def local(initial_field, source, material, stiffness_table, mass_table, trace_cells, near_blocks, near_mask, far_left, far_right,
           block_ranks):
     slabs, tiles = lax.axis_size("slab"), lax.axis_size("tile")
     planes = slabs // PLANE
+    volume = jax.ShapeDtypeStruct((3, 128, 384), F32)
+    face = jax.ShapeDtypeStruct((64, 384), BF16)
+    params = pltpu.CompilerParams(vmem_limit_bytes=24 * 1024 * 1024)
+    first, last, table = pl.pallas_call(
+        y_faces,
+        out_shape=(face, face, jax.ShapeDtypeStruct((16, 384), F32)),
+        in_specs=[hbm()] * 5,
+        out_specs=(vmem(),) * 3,
+        scratch_shapes=[
+            pltpu.SMEM((8,), F32), pltpu.SMEM((8,), F32), pltpu.VMEM((4, 3, 8, 384), F32), pltpu.VMEM((2, 3, 8, 384), F32),
+            pltpu.VMEM((2, 8, 384), jnp.int32), pltpu.SemaphoreType.DMA((10,)),
+        ],
+        compiler_params=pltpu.CompilerParams(vmem_limit_bytes=56000 * 1024),
+    )(stiffness_table, mass_table, initial_field, source, material)
     field = initial_field.reshape(3, 128, 384)
     sources = source.reshape(3, 128, 384)
     cells = material.reshape(128, 384)
-    volume = jax.ShapeDtypeStruct((3, 128, 384), F32)
-    face = jax.ShapeDtypeStruct((64, 384), BF16)
-    params = pltpu.CompilerParams(vmem_limit_bytes=24 * 1024 * 1024)
-    first, last = pl.pallas_call(
-        y_faces,
-        out_shape=(face, face),
-        in_specs=[pl.BlockSpec(memory_space=pltpu.HBM)] * 5,
-        out_specs=(vmem(), vmem()),
-        scratch_shapes=[
-            pltpu.SMEM((8,), F32), pltpu.SMEM((8,), F32), pltpu.VMEM((3, 128, 384), F32), pltpu.VMEM((3, 128, 384), F32),
-            pltpu.VMEM((128, 384), jnp.int32), pltpu.SemaphoreType.DMA((5,)),
-        ],
-        compiler_params=pltpu.CompilerParams(vmem_limit_bytes=56000 * 1024),
-    )(stiffness_table, mass_table, field, sources, cells)
     before, after = exchange(first, last, "tile")
     face = jax.ShapeDtypeStruct((128, 384), BF16)
-    first, last = pl.pallas_call(
+    far, pair = pl.pallas_call(
         z_faces,
-        grid=(1,),
         out_shape=(face, face),
-        in_specs=[
-            smem(), smem(),
-            pl.BlockSpec((3, 32, 384), lambda i: (0, 0, 0)), pl.BlockSpec((3, 32, 384), lambda i: (0, 3, 0)),
-            pl.BlockSpec((3, 16, 384), lambda i: (0, 0, 0)), pl.BlockSpec((3, 16, 384), lambda i: (0, 7, 0)),
-            pl.BlockSpec((16, 384), lambda i: (0, 0)), pl.BlockSpec((16, 384), lambda i: (7, 0)),
-            pl.BlockSpec((64, 384), lambda i: (0, 0)), pl.BlockSpec((64, 384), lambda i: (0, 0)),
-        ],
-        out_specs=(pl.BlockSpec((128, 384), lambda i: (0, 0)), pl.BlockSpec((128, 384), lambda i: (0, 0))),
-        compiler_params=params,
-    )(stiffness_table, mass_table, field, field, sources, sources, cells, cells, before, after)
-    below, above = exchange(first, last, "slab")
+        in_specs=[vmem()] * 6,
+        out_specs=(vmem(), vmem()),
+        compiler_params=params,
+    )(table, field, sources, cells, before, after)
+    far, pair = swap(far, pair, "slab")
     members = PLANE * tiles
-    state = pl.pallas_call(
+    *state, inner, edge, place, spread = pl.pallas_call(
         relax_inner,
         out_shape=(
             volume, volume, jax.ShapeDtypeStruct((128, 384), F32), jax.ShapeDtypeStruct((12, 8, 384), F32),
-            jax.ShapeDtypeStruct((3, 64, 384), F32), jax.ShapeDtypeStruct((256, 192), BF16),
+            volume, jax.ShapeDtypeStruct((256, 192), BF16),
             jax.ShapeDtypeStruct((256, 128), F32), jax.ShapeDtypeStruct((256, 128), F32),
         ),
-        in_specs=[smem(), smem()] + [vmem()] * 6,
-        out_specs=(vmem(),) * 8,
-        scratch_shapes=[pltpu.VMEM((192, 384), BF16)],
+        in_specs=[vmem()] * 7,
+        out_specs=(vmem(),) * 4 + (hbm(),) + (vmem(),) * 3,
+        scratch_shapes=[pltpu.VMEM((192, 384), BF16), pltpu.VMEM((3, 64, 384), F32), pltpu.SemaphoreType.DMA((3,))],
         compiler_params=params,
         cost_estimate=pl.CostEstimate(flops=6_000_000, bytes_accessed=4_000_000, transcendentals=0),
-    )(stiffness_table, mass_table, field, sources, cells, before, after, trace_cells.reshape(1, 256))
-    result, send = pl.pallas_call(
+    )(table, field, sources, cells, before, after, trace_cells.reshape(1, 256))
+    edges, send = pl.pallas_call(
         functools.partial(relax_edges, planes),
-        out_shape=(volume, jax.ShapeDtypeStruct((members, 4, 128), BF16)),
-        in_specs=[vmem()] * 12,
+        out_shape=(jax.ShapeDtypeStruct((3, 64, 384), F32), jax.ShapeDtypeStruct((members, 4, 128), BF16)),
+        in_specs=[vmem()] * 11,
         out_specs=(vmem(), vmem()),
         scratch_shapes=[pltpu.VMEM((192, 384), BF16)],
         compiler_params=params,
-    )(field, *state, below, above, far_right.reshape(-1, 256))
+    )(field, *state, edge, place, spread, far, pair, far_right.reshape(-1, 256))
     ids = np.arange(slabs * tiles).reshape(planes, members)
     got = lax.all_to_all(send, BOTH, 0, 0, axis_index_groups=ids.tolist(), tiled=True)
     send = pl.pallas_call(
@@ -408,12 +424,22 @@
         compiler_params=params,
     )(got)
     relay = lax.all_to_all(send, BOTH, 0, 0, axis_index_groups=ids.T.tolist(), tiled=True)
-    mask = near_mask.reshape(9)
+    result = pl.pallas_call(
+        assemble,
+        out_shape=volume,
+        in_specs=[hbm(), vmem()],
+        out_specs=hbm(),
+        input_output_aliases={0: 0},
+        scratch_shapes=[pltpu.SemaphoreType.DMA((6,))],
+        compiler_params=params,
+        cost_estimate=pl.CostEstimate(flops=0, bytes_accessed=600_000, transcendentals=0),
+    )(inner, edges)
+    mask = near_mask.reshape(1, 9)
     blocks = near_blocks.reshape(-1, 256)
     part = pl.pallas_call(
         functools.partial(near_inside, tiles),
         out_shape=jax.ShapeDtypeStruct((1, 256), F32),
-        in_specs=[smem(), vmem(), vmem()],
+        in_specs=[vmem()] * 3,
         out_specs=vmem(),
         compiler_params=params,
         cost_estimate=pl.CostEstimate(flops=2 * 16 * 2304 * 256, bytes_accessed=2304 * 512, transcendentals=0),
@@ -421,10 +447,10 @@
     boundary = pl.pallas_call(
         functools.partial(finish, planes),
         out_shape=jax.ShapeDtypeStruct((1, 256), F32),
-        in_specs=[smem(), smem()] + [vmem()] * 4,
+        in_specs=[vmem()] * 6,
         out_specs=vmem(),
         compiler_params=params,
-    )(mask, block_ranks, part, relay, blocks, far_left.reshape(16, 256))
+    )(mask, block_ranks.reshape(1, 1), part, relay, blocks, far_left.reshape(16, 256))
     return result.reshape(initial_field.shape), boundary.reshape(1, 1, 256)
 
 

time: 75.2 us -> 68.8 us (0.915)
  blocking collectives: 19.4 us -> 16.3 us
  Pallas kernels: 9.56 us -> 7.51 us
  starting transfers between devices: 32.8 us -> 31.1 us
    ppermute x4 -> x2, starting transfers between devices: 17.6 us -> 5.32 us  [exchange(): return (lax.ppermute(last, axis, up), lax.ppermute(first, axis, down))]
    ppermute x0 -> x2, starting transfers between devices: none -> 11.6 us  [the longest x1 6.39 us: swap(): return (far, lax.ppermute(pair, axis, [(i, i ^ 1) for i in range(devices)]))]
    all_to_all x1, blocking collectives: 19.4 us -> 16.3 us  [local(): lax.all_to_all(send, BOTH, 0, 0, axis_index_groups=ids.tolist(), tiled=True)]
    all_to_all x1, starting transfers between devices: 15.2 us -> 14.1 us  [local(): lax.all_to_all(send, BOTH, 0, 0, axis_index_groups=ids.T.tolist(), tiled=...]
    pallas_call x3 -> x4, Pallas kernels: 4.74 us -> 3.78 us  [the longest x1 1.84 us: local(): pl.pallas_call(y_faces, out_shape=(face, face, jax.ShapeDtypeStruct((16,...]
    ppermute x4 -> x2, waiting for transfers between devices: 3.75 us -> 3.74 us  [exchange(): return (lax.ppermute(last, axis, up), lax.ppermute(first, axis, down))]
where the time goes in v4:
time: 68.8 us; the launch traced here: 68.3 us
  starting transfers between devices  31.1 us (45%)
  blocking collectives  16.3 us (24%)
  waiting for transfers between devices  11.2 us (16%)
  Pallas kernels  7.51 us (11%)
  between operations  1.48 us (2%)
  local copies, waits for them, and re-layouts  0.77 us (1%)
    all_to_all x1, blocking collectives, local(): lax.all_to_all(send, BOTH, 0, 0, axis_index_groups=ids.tolist(), tiled=True)  16.3 us
    all_to_all x1, starting transfers between devices, local(): lax.all_to_all(send, BOTH, 0, 0, axis_index_groups=ids.T.tolist(), tiled=...  14.1 us
    all_to_all x1, waiting for transfers between devices, local(): lax.all_to_all(send, BOTH, 0, 0, axis_index_groups=ids.T.tolist(), tiled=...  7.45 us
    ppermute x1, starting transfers between devices, swap(): return (far, lax.ppermute(pair, axis, [(i, i ^ 1) for i in range(devices)]))  6.39 us
    ppermute x2, starting transfers between devices, exchange(): return (lax.ppermute(last, axis, up), lax.ppermute(first, axis, down))  5.32 us
    ppermute x1, starting transfers between devices, swap(): lax.ppermute(far, axis, [(i, i + 1 if i % 2 else i - 1) for i in range(1,...  5.24 us
    ppermute x2, waiting for transfers between devices, exchange(): return (lax.ppermute(last, axis, up), lax.ppermute(first, axis, down))  3.74 us
    pallas_call x1, Pallas kernels, local(): pl.pallas_call(y_faces, out_shape=(face, face, jax.ShapeDtypeStruct((16,...  1.84 us
  transfers between devices with their start and end apart: 5, of which 3 were waited for; matrix products, arithmetic and copies ran while one was open for 0% of the time, Pallas kernels for 4%

profile of v4, /device:TPU:1, one launch (start us, length us, event | category | flops | bytes accessed | tf_op | source)
XLA Modules:
  0.0 68.3 jit_solution(5890999306972772101)
XLA Ops:
  0.6 0.0 copy-start
  0.6 0.0 copy-start.1
  0.7 0.0 copy-start.3
  0.7 0.0 copy-start.8
  0.7 1.8 %shard_map.122 = (bf16[64,384]{1,0:T(8,128)(2,1)}, bf16[64,384]{1,0:T(8,128)(2,1)}, f32[16,384]{1,0:T(8,128)}) custom-call(f32[8]{0:T(128)} %stiff_hbm.1, f32[8]{0:T(128)} %mass_hbm.1, f32[3,8,16,384]{3,2,1,0:T(8,128)} %field_hbm.1, f32[3,8,16,384]{3,2,1,0:T(8,128)} %source_hbm.1, s32[8,16,384]{2,1,0:T(8,128)} %material_hbm.1), custom_call_target="tpu_custom_call" | custom-call | tf_op jit(solution)/shard_map/pallas_call | solution.py:371
  2.5 4.0 %collective-permute-start = (bf16[64,384]{1,0:T(8,128)(2,1)}, bf16[64,384]{1,0:T(8,128)(2,1)S(1)}, u32[]{:S(2)}, u32[]{:S(2)}) collective-permute-start(bf16[64,384]{1,0:T(8,128)(2,1)} %get-tuple-element.18), channel_id=1, source_target_pairs={{0,1},{1,2},{2,3},{3,4},{4,5},{5,6},{6,7},{8,9},{9,10},{10,11},{11... | collective-permute-start | bytes 147464 | tf_op jit(solution)/shard_map/ppermute | solution.py:355
  6.6 1.3 %collective-permute-start.1 = (bf16[64,384]{1,0:T(8,128)(2,1)}, bf16[64,384]{1,0:T(8,128)(2,1)S(1)}, u32[]{:S(2)}, u32[]{:S(2)}) collective-permute-start(bf16[64,384]{1,0:T(8,128)(2,1)} %get-tuple-element.19), channel_id=1, source_target_pairs={{1,0},{2,1},{3,2},{4,3},{5,4},{6,5},{7,6},{9,8},{10,9},{11,10},{12... | collective-permute-start | bytes 147464 | tf_op jit(solution)/shard_map/ppermute | solution.py:355
  7.9 0.2 collective-permute-done.before_ref
  8.0 3.6 %collective-permute-done.1.after_ref = bf16[64,384]{1,0:T(8,128)(2,1)S(1)} collective-permute-done((bf16[64,384]{1,0:T(8,128)(2,1)}, bf16[64,384]{1,0:T(8,128)(2,1)S(1)}, u32[]{:S(2)}, u32[]{:S(2)}) %collective-permute-start.1) | collective-permute-done | bytes 49184 | tf_op jit(solution)/shard_map/ppermute | solution.py:355
  11.6 0.0 copy-done
  11.6 0.0 copy-done.1
  11.6 0.0 copy-done.3
  11.6 0.0 copy-start.5
  11.6 0.7 %copy-done.5 = f32[16,384]{1,0:T(8,128)S(1)} copy-done((f32[16,384]{1,0:T(8,128)S(1)}, f32[16,384]{1,0:T(8,128)}, u32[]{:S(2)}) %copy-start.5) | copy-done | bytes 24600
  12.3 0.0 copy-start.4
  12.4 0.2 shard_map.124
  12.5 5.2 %collective-permute-start.2 = (bf16[128,384]{1,0:T(8,128)(2,1)S(1)}, bf16[128,384]{1,0:T(8,128)(2,1)S(1)}, u32[]{:S(2)}, u32[]{:S(2)}) collective-permute-start(bf16[128,384]{1,0:T(8,128)(2,1)S(1)} %get-tuple-element.28), channel_id=1, source_target_pairs={{8,16},{16,8},{24,32},{32,24},{40,48},{48,40},{56,64},{64,56},{72,... | collective-permute-start | bytes 294920 | tf_op jit(solution)/shard_map/ppermute | solution.py:360
  17.8 6.4 %collective-permute-start.3 = (bf16[128,384]{1,0:T(8,128)(2,1)S(1)}, bf16[128,384]{1,0:T(8,128)(2,1)S(1)}, u32[]{:S(2)}, u32[]{:S(2)}) collective-permute-start(bf16[128,384]{1,0:T(8,128)(2,1)S(1)} %get-tuple-element.29), channel_id=1, source_target_pairs={{0,8},{8,0},{16,24},{24,16},{32,40},{40,32},{48,56},{56,48},{64,72... | collective-permute-start | bytes 294920 | tf_op jit(solution)/shard_map/ppermute | solution.py:361
  24.2 0.0 copy-done.8
  24.2 1.8 %shard_map.123 = (f32[3,128,384]{2,1,0:T(8,128)S(1)}, f32[3,128,384]{2,1,0:T(8,128)S(1)}, f32[128,384]{1,0:T(8,128)S(1)}, f32[12,8,384]{2,1,0:T(8,128)S(1)}, f32...) custom-call(f32[16,384]{1,0:T(8,128)S(1)} %copy-done.5, ...), custom_call_target="tpu_custom_call" | custom-call | flops 6000000 | bytes 4000000 | tf_op jit(solution)/shard_map/pallas_call | solution.py:396
  26.0 0.0 collective-permute-done.2.far_ref
  26.0 0.0 collective-permute-done.3.pair_ref
  26.0 0.0 copy-done.4
  26.0 1.0 %shard_map.125 = (f32[3,64,384]{2,1,0:T(8,128)S(1)}, bf16[64,4,128]{2,1,0:T(4,128)(2,1)S(1)}) custom-call(f32[3,128,384]{2,1,0:T(8,128)S(1)} %bitcast.14, f32[3,128,384]{2,1,0:T(8,128)S(1)} %get-tuple-element.21.once_ref, f32[3,128,384]{2,1,0:T(8,128)S(1)} %get-tuple-element.22.scaled_ref, f32[128,384]{1,0:T(8,128)S(1)} %get-tuple-element.23.coupling_ref, ...), custom_call_target="tpu_custom_call" | custom-call | tf_op jit(solution)/shard_map/pallas_call | solution.py:409
  27.0 0.0 copy-start.2
  27.0 0.0 copy-start.7
  27.0 16.3 %all_to_all.10.got_ref = bf16[64,4,128]{2,1,0:T(4,128)(2,1)S(1)} all-to-all(bf16[64,4,128]{2,1,0:T(4,128)(2,1)S(1)} %get-tuple-element.31), channel_id=1, replica_groups={{0,1,2,3,4,5,6,7,8,9,10,11,12,13,14,15,16,17,18,19,20,21,22,23,24,25,26..., dimensions={0} | all-to-all | bytes 131072 | tf_op jit(solution)/shard_map/all_to_all | solution.py:418
  43.3 0.7 %shard_map.128 = bf16[12,8,128]{2,1,0:T(8,128)(2,1)} custom-call(bf16[64,4,128]{2,1,0:T(4,128)(2,1)S(1)} %all_to_all.10.got_ref), custom_call_target="tpu_custom_call" | custom-call | tf_op jit(solution)/shard_map/pallas_call | solution.py:419
  44.0 14.1 %all-to-all-start.1 = ((bf16[12,8,128]{2,1,0:T(8,128)(2,1)}), bf16[12,8,128]{2,1,0:T(8,128)(2,1)S(1)}, u32[]{:S(2)}, u32[]{:S(2)}) async-start(bf16[12,8,128]{2,1,0:T(8,128)(2,1)} %shard_map.128), calls=%async_computation.1 | async-start | bytes 49152 | tf_op jit(solution)/shard_map/all_to_all | solution.py:426
  58.7 0.0 copy-start.6
  58.7 0.8 %shard_map.126 = f32[3,128,384]{2,1,0:T(8,128)} custom-call(f32[3,128,384]{2,1,0:T(8,128)} %get-tuple-element.20.inner_hbm, f32[3,64,384]{2,1,0:T(8,128)S(1)} %get-tuple-element.30.edges_ref), custom_call_target="tpu_custom_call", output_to_operand_aliasing={{}: (0, {})} | custom-call | bytes 600000 | tf_op jit(solution)/shard_map/pallas_call | solution.py:427
  59.5 0.0 copy-done.2
  59.5 0.0 copy-done.7
  59.5 0.4 shard_map.127.part_ref
  59.9 7.5 %all-to-all-done.1.relay_ref = bf16[12,8,128]{2,1,0:T(8,128)(2,1)S(1)} async-done(((bf16[12,8,128]{2,1,0:T(8,128)(2,1)}), bf16[12,8,128]{2,1,0:T(8,128)(2,1)S(1)}, u32[]{:S(2)}, u32[]{:S(2)}) %all-to-all-start.1) | async-done | bytes 24608 | tf_op jit(solution)/shard_map/all_to_all | solution.py:426
  67.4 0.0 copy-done.6
  67.4 0.9 %shard_map.129 = f32[1,256]{1,0:T(1,128)} custom-call(s32[1,9]{1,0:T(1,128)S(1)} %bitcast.24, s32[1,1]{1,0:T(1,128)} %bitcast.11.rank_ref, f32[1,256]{1,0:T(1,128)S(1)} %shard_map.127.part_ref, bf16[12,8,128]{2,1,0:T(8,128)(2,1)S(1)} %all-to-all-done.1.relay_ref, bf16[2304,256]{1,0:T(8,128)(2,1)S(1)} %bitcast.18, bf16[16,256]{1,0:T(8,128)(2,1)S(1)} %bitcast.22), custom_call_target="tpu_custom_call" | custom-call | tf_op jit(solution)/shard_map/pallas_call | solution.py:447
Async XLA Ops:
  0.6 11.0 %copy-start = (f32[3,8,16,384]{3,2,1,0:T(8,128)S(1)}, f32[3,8,16,384]{3,2,1,0:T(8,128)}, u32[]{:S(2)}) copy-start(f32[3,8,16,384]{3,2,1,0:T(8,128)} %field_hbm.1) | copy-start | bytes 1769476
  0.6 11.0 %copy-start.1 = (f32[3,8,16,384]{3,2,1,0:T(8,128)S(1)}, f32[3,8,16,384]{3,2,1,0:T(8,128)}, u32[]{:S(2)}) copy-start(f32[3,8,16,384]{3,2,1,0:T(8,128)} %source_hbm.1) | copy-start | bytes 1769476
  0.7 11.0 %copy-start.3 = (s32[8,16,384]{2,1,0:T(8,128)S(1)}, s32[8,16,384]{2,1,0:T(8,128)}, u32[]{:S(2)}) copy-start(s32[8,16,384]{2,1,0:T(8,128)} %material_hbm.1) | copy-start | bytes 589828
  0.7 23.5 %copy-start.8 = (s32[1,1,256]{2,1,0:T(1,128)S(1)}, s32[1,1,256]{2,1,0:T(1,128)}, u32[]{:S(2)}) copy-start(s32[1,1,256]{2,1,0:T(1,128)} %param.16) | copy-start | bytes 3076
  2.5 5.5 %collective-permute-start = (bf16[64,384]{1,0:T(8,128)(2,1)}, bf16[64,384]{1,0:T(8,128)(2,1)S(1)}, u32[]{:S(2)}, u32[]{:S(2)}) collective-permute-start(bf16[64,384]{1,0:T(8,128)(2,1)} %get-tuple-element.18), channel_id=1, source_target_pairs={{0,1},{1,2},{2,3},{3,4},{4,5},{5,6},{6,7},{8,9},{9,10},{10,11},{11... | collective-permute-start | bytes 147464 | tf_op jit(solution)/shard_map/ppermute | solution.py:355
  6.6 5.0 %collective-permute-start.1 = (bf16[64,384]{1,0:T(8,128)(2,1)}, bf16[64,384]{1,0:T(8,128)(2,1)S(1)}, u32[]{:S(2)}, u32[]{:S(2)}) collective-permute-start(bf16[64,384]{1,0:T(8,128)(2,1)} %get-tuple-element.19), channel_id=1, source_target_pairs={{1,0},{2,1},{3,2},{4,3},{5,4},{6,5},{7,6},{9,8},{10,9},{11,10},{12... | collective-permute-start | bytes 147464 | tf_op jit(solution)/shard_map/ppermute | solution.py:355
  11.6 0.7 %copy-start.5 = (f32[16,384]{1,0:T(8,128)S(1)}, f32[16,384]{1,0:T(8,128)}, u32[]{:S(2)}) copy-start(f32[16,384]{1,0:T(8,128)} %get-tuple-element.17.table_ref) | copy-start | bytes 73732
  12.3 13.6 %copy-start.4 = (bf16[16,96,1,1,256]{4,1,3,2,0:T(8,128)(2,1)S(1)}, bf16[16,96,1,1,256]{4,1,3,2,0:T(8,128)(2,1)}, u32[]{:S(2)}) copy-start(bf16[16,96,1,1,256]{4,1,3,2,0:T(8,128)(2,1)} %param.20) | copy-start | bytes 2359300
  12.5 13.4 %collective-permute-start.2 = (bf16[128,384]{1,0:T(8,128)(2,1)S(1)}, bf16[128,384]{1,0:T(8,128)(2,1)S(1)}, u32[]{:S(2)}, u32[]{:S(2)}) collective-permute-start(bf16[128,384]{1,0:T(8,128)(2,1)S(1)} %get-tuple-element.28), channel_id=1, source_target_pairs={{8,16},{16,8},{24,32},{32,24},{40,48},{48,40},{56,64},{64,56},{72,... | collective-permute-start | bytes 294920 | tf_op jit(solution)/shard_map/ppermute | solution.py:360
  17.8 8.2 %collective-permute-start.3 = (bf16[128,384]{1,0:T(8,128)(2,1)S(1)}, bf16[128,384]{1,0:T(8,128)(2,1)S(1)}, u32[]{:S(2)}, u32[]{:S(2)}) collective-permute-start(bf16[128,384]{1,0:T(8,128)(2,1)S(1)} %get-tuple-element.29), channel_id=1, source_target_pairs={{0,8},{8,0},{16,24},{24,16},{32,40},{40,32},{48,56},{56,48},{64,72... | collective-permute-start | bytes 294920 | tf_op jit(solution)/shard_map/ppermute | solution.py:361
  27.0 32.5 %copy-start.2 = (bf16[1,1,9,256,256]{4,3,2,1,0:T(8,128)(2,1)S(1)}, bf16[1,1,9,256,256]{4,3,2,1,0:T(8,128)(2,1)}, u32[]{:S(2)}) copy-start(bf16[1,1,9,256,256]{4,3,2,1,0:T(8,128)(2,1)} %param.17) | copy-start | bytes 3538948
  27.0 32.5 %copy-start.7 = (s32[1,1,9]{2,1,0:T(1,128)S(1)}, s32[1,1,9]{2,1,0:T(1,128)}, u32[]{:S(2)}) copy-start(s32[1,1,9]{2,1,0:T(1,128)} %param.18) | copy-start | bytes 112
  44.0 23.4 %all-to-all-start.1 = ((bf16[12,8,128]{2,1,0:T(8,128)(2,1)}), bf16[12,8,128]{2,1,0:T(8,128)(2,1)S(1)}, u32[]{:S(2)}, u32[]{:S(2)}) async-start(bf16[12,8,128]{2,1,0:T(8,128)(2,1)} %shard_map.128), calls=%async_computation.1 | async-start | bytes 49152 | tf_op jit(solution)/shard_map/all_to_all | solution.py:426
  58.7 8.6 %copy-start.6 = (bf16[16,1,1,256]{3,0,2,1:T(8,128)(2,1)S(1)}, bf16[16,1,1,256]{3,0,2,1:T(8,128)(2,1)}, u32[]{:S(2)}) copy-start(bf16[16,1,1,256]{3,0,2,1:T(8,128)(2,1)} %param.19) | copy-start | bytes 24580

commit v5 on v4

--- a/solution.py
+++ b/solution.py
@@ -17,17 +17,12 @@
 
 
 def table_rows(stiff_ref, mass_ref, width):
-    weights, couplings = [], []
-    for entry in range(8):
-        stiffness = jnp.full((1, width), stiff_ref[entry], F32)
-        inverse = RELAX / (6.0 * stiffness + mass_ref[entry])
-        weights.append(inverse)
-        couplings.append(stiffness * inverse)
-    return weights + couplings
-
-
-def ready_rows(table_ref):
-    return [table_ref[k:k + 1, :] for k in range(16)]
+    stiffness = stiff_ref[...]
+    weight = RELAX / (6.0 * stiffness + mass_ref[...])
+    rows = []
+    for table in (weight, stiffness * weight):
+        rows += [jnp.broadcast_to(table[:, entry:entry + 1], (1, width)) for entry in range(8)]
+    return rows
 
 
 def lookup(material, rows):
@@ -65,10 +60,8 @@
     return value
 
 
-def y_faces(stiff_hbm, mass_hbm, field_hbm, source_hbm, material_hbm, first_ref, last_ref, table_ref,
-            stiff_ref, mass_ref, field_ref, source_ref, material_ref, sems):
-    pairs = [(stiff_hbm, stiff_ref), (mass_hbm, mass_ref)]
-    pairs += [(field_hbm.at[:, :, y, :], field_ref.at[k]) for k, y in enumerate((0, 15, 1, 14))]
+def y_faces(field_hbm, source_hbm, material_hbm, first_ref, last_ref, field_ref, source_ref, material_ref, sems):
+    pairs = [(field_hbm.at[:, :, y, :], field_ref.at[k]) for k, y in enumerate((0, 15, 1, 14))]
     pairs += [(source_hbm.at[:, :, y, :], source_ref.at[k]) for k, y in enumerate((0, 15))]
     pairs += [(material_hbm.at[:, y, :], material_ref.at[k]) for k, y in enumerate((0, 15))]
     copies = [pltpu.make_async_copy(src, dst, sems.at[k]) for k, (src, dst) in enumerate(pairs)]
@@ -76,39 +69,34 @@
         copy.start()
     for copy in copies:
         copy.wait()
-    rows = table_rows(stiff_ref, mass_ref, table_ref.shape[1])
-    table_ref[...] = jnp.concatenate(rows, axis=0)
     for k, out_ref in enumerate((first_ref, last_ref)):
-        weight, coupling = lookup(material_ref[k], rows)
-        values, partials = [], []
-        for c in range(3):
-            value = field_ref[k, c]
-            total = field_ref[2 + k, c] + row_sum(value, 0.0, 0.0) + x_sum(value)
-            values.append(value)
-            partials.append(KEEP * value + weight * source_ref[k, c] + coupling * total)
-        planes = values + partials + [coupling, jnp.zeros_like(coupling)]
-        for pair in range(4):
+        values = [field_ref[k, c] for c in range(3)]
+        totals = [field_ref[2 + k, c] + row_sum(values[c], 0.0, 0.0) + x_sum(values[c]) for c in range(3)]
+        planes = values + [source_ref[k, c] for c in range(3)] + totals + [1.0 + material_ref[k].astype(F32)]
+        for pair in range(5):
             both = jnp.concatenate(planes[2 * pair:2 * pair + 2], axis=0)
             out_ref[16 * pair:16 * pair + 16, :] = both.astype(BF16)
 
 
-def z_faces(table_ref, field_ref, source_ref, material_ref, before_ref, after_ref, far_ref, pair_ref):
+def rim_rows(first, last):
+    row = lax.broadcasted_iota(jnp.int32, (16, first.shape[1]), 0)
+    return jnp.where(row == 0, first, jnp.where(row == 15, last, 0.0))
+
+
+def z_faces(field_ref, base_ref, coupling_ref, before_ref, after_ref, far_ref, pair_ref):
     even = lax.rem(lax.axis_index("slab"), 2) == 0
-    rows = ready_rows(table_ref)
     before = bands(before_ref, 2)
     after = bands(after_ref, 2)
     faces = []
-    for z, beyond in ((0, 1), (7, 6)):
-        here, inner = slice(16 * z, 16 * z + 16), slice(16 * beyond, 16 * beyond + 16)
-        weight, coupling = lookup(material_ref[here, :], rows)
+    for z in (0, 7):
+        here = slice(16 * z, 16 * z + 16)
+        coupling = coupling_ref[here, :]
         lines, values, partials = [], [], []
         for c in range(3):
             at = 8 * (c % 2) + z
             lines += [before[c // 2][at:at + 1, :], after[c // 2][at:at + 1, :]]
-            value = field_ref[c, here, :]
-            total = field_ref[c, inner, :] + row_sum(value, lines[2 * c], lines[2 * c + 1]) + x_sum(value)
-            values.append(value)
-            partials.append(KEEP * value + weight * source_ref[c, here, :] + coupling * total)
+            values.append(field_ref[c, here, :])
+            partials.append(base_ref[c, here, :] + coupling * rim_rows(lines[2 * c], lines[2 * c + 1]))
         faces.append(values + partials + [coupling, stacked(lines, 16)])
     for k, (first, last) in enumerate(zip(*faces)):
         here = slice(16 * k, 16 * k + 16)
@@ -138,33 +126,58 @@
 EDGES = (0, 1, 6, 7)
 
 
-def relax_inner(table_ref, field_ref, source_ref, material_ref, before_ref, after_ref, cells_ref,
-                once_ref, scaled_ref, coupling_ref, rim_ref, out_hbm, edge_ref, place_ref, spread_ref, plain_ref, out_ref, sems):
-    rows = ready_rows(table_ref)
-    halo = [bands(before_ref, 4), bands(after_ref, 4)]
-
-    def y_plane(side, k):
-        return halo[side][k // 2][8 * (k % 2):8 * (k % 2) + 8]
-
-    for c in range(3):
-        for side, y in ((0, 0), (1, 15)):
-            rim_ref[6 * side + c] = y_plane(side, 3 + c) + y_plane(side, 6) * line_rows(field_ref, y, c)
-    for side in range(2):
-        rim_ref[6 * side + 3] = y_plane(side, 6)
+def no_halo(stiff_ref, mass_ref, field_ref, source_ref, material_ref, cells_ref,
+            base_ref, scaled_ref, coupling_ref, edge_ref, chosen_ref, place_ref):
+    rows = table_rows(stiff_ref, mass_ref, field_ref.shape[-1])
     for z in range(8):
         here = slice(16 * z, 16 * z + 16)
         weight, coupling = lookup(material_ref[here, :], rows)
         coupling_ref[here, :] = coupling
         for c in range(3):
             value = field_ref[c, here, :]
-            total = row_sum(value, y_plane(0, c)[z:z + 1], y_plane(1, c)[z:z + 1]) + x_sum(value)
+            total = row_sum(value, 0.0, 0.0) + x_sum(value)
             if z > 0:
                 total = total + field_ref[c, 16 * z - 16:16 * z, :]
             if z < 7:
                 total = total + field_ref[c, 16 * z + 16:16 * z + 32, :]
             scaled = weight * source_ref[c, here, :]
             scaled_ref[c, here, :] = scaled
-            once_ref[c, here, :] = KEEP * value + scaled + coupling * total
+            base_ref[c, here, :] = KEEP * value + scaled + coupling * total
+
+    width = field_ref.shape[-1]
+    count = cells_ref.shape[1]
+    cells = cells_ref[...].astype(F32)
+    line = jnp.floor((cells + 0.5) * (1.0 / width))
+    place_ref[...] = jnp.broadcast_to(column_of(cells - width * line), (count, 128))
+    line_column = column_of(line)
+    along = lax.broadcasted_iota(jnp.int32, (count, 192), 1).astype(F32)
+    part = jnp.floor(along * (1.0 / 64) + 0.001)
+    shift = along - 64.0 * part
+    inner = 128.0 * part + shift + 32.0
+    outer = 128.0 * part + jnp.where(shift < 32.0, shift, shift + 64.0)
+    edge_ref[...] = jnp.where(outer == line_column, 1.0, 0.0).astype(BF16)
+    chosen_ref[...] = jnp.where(inner == line_column, 1.0, 0.0).astype(BF16)
+
+
+def relax_inner(stiff_ref, mass_ref, field_ref, base_ref, scaled_ref, coupling_ref, before_ref, after_ref, chosen_ref, place_ref,
+                once_ref, rim_ref, out_ref, spread_ref, plain_ref):
+    rows = table_rows(stiff_ref, mass_ref, field_ref.shape[-1])
+    lines = []
+    for side, (ref, y) in enumerate(((before_ref, 0), (after_ref, 15))):
+        halo = bands(ref, 5)
+        planes = [halo[k // 2][8 * (k % 2):8 * (k % 2) + 8] for k in range(10)]
+        weight, coupling = lookup(planes[9] - 1.0, rows)
+        coupling = jnp.where(planes[9] > 0.0, coupling, 0.0)
+        rim_ref[6 * side + 3] = coupling
+        for c in range(3):
+            total = planes[6 + c] + line_rows(field_ref, y, c)
+            rim_ref[6 * side + c] = KEEP * planes[c] + weight * planes[3 + c] + coupling * total
+        lines.append(planes[:3])
+    for z in range(8):
+        here = slice(16 * z, 16 * z + 16)
+        for c in range(3):
+            halo = rim_rows(lines[0][c][z:z + 1], lines[1][c][z:z + 1])
+            once_ref[c, here, :] = base_ref[c, here, :] + coupling_ref[here, :] * halo
     for z in range(2, 6):
         here = slice(16 * z, 16 * z + 16)
         for c in range(3):
@@ -175,28 +188,8 @@
             out_ref[c, 16 * z - 32:16 * z - 16, :] = result
             at = 64 * c + 16 * z - 32
             plain_ref[at:at + 16, :] = result.astype(BF16)
-    copies = [pltpu.make_async_copy(out_ref.at[c], out_hbm.at[c, pl.ds(32, 64), :], sems.at[c]) for c in range(3)]
-    for copy in copies:
-        copy.start()
-
-    width = field_ref.shape[-1]
-    count = cells_ref.shape[1]
-    cells = cells_ref[...].astype(F32)
-    line = jnp.floor((cells + 0.5) * (1.0 / width))
-    place_column = column_of(cells - width * line)
-    line_column = column_of(line)
-    place_ref[...] = jnp.broadcast_to(place_column, (count, 128))
-    along = lax.broadcasted_iota(jnp.int32, (count, 192), 1).astype(F32)
-    part = jnp.floor(along * (1.0 / 64) + 0.001)
-    shift = along - 64.0 * part
-    inner = 128.0 * part + shift + 32.0
-    outer = 128.0 * part + jnp.where(shift < 32.0, shift, shift + 64.0)
-    edge_ref[...] = jnp.where(outer == line_column, 1.0, 0.0).astype(BF16)
-    chosen = jnp.where(inner == line_column, 1.0, 0.0).astype(BF16)
-    picked = jnp.dot(chosen, plain_ref[...], preferred_element_type=F32)
-    spread_ref[...] = spread_of(picked, place_column)
-    for copy in copies:
-        copy.wait()
+    picked = jnp.dot(chosen_ref[...], plain_ref[...], preferred_element_type=F32)
+    spread_ref[...] = spread_of(picked, place_ref[:, 0:1])
 
 
 def spread_of(picked, place_column):
@@ -255,13 +248,11 @@
             send_ref[to * tiles + tile] = packet
 
 
-def assemble(inner_hbm, edges_ref, out_hbm, sems):
-    del inner_hbm
+def assemble(inner_ref, edges_ref, out_hbm, sems):
     copies = []
     for c in range(3):
-        for k, at in enumerate((0, 96)):
-            target = out_hbm.at[c, pl.ds(at, 32), :]
-            copies.append(pltpu.make_async_copy(edges_ref.at[c, pl.ds(32 * k, 32), :], target, sems.at[2 * c + k]))
+        for source, target in ((edges_ref.at[c, 0:32], (0, 32)), (inner_ref.at[c], (32, 64)), (edges_ref.at[c, 32:64], (96, 32))):
+            copies.append(pltpu.make_async_copy(source, out_hbm.at[c, pl.ds(*target), :], sems.at[len(copies)]))
     for copy in copies:
         copy.start()
     for copy in copies:
@@ -366,46 +357,53 @@
     slabs, tiles = lax.axis_size("slab"), lax.axis_size("tile")
     planes = slabs // PLANE
     volume = jax.ShapeDtypeStruct((3, 128, 384), F32)
-    face = jax.ShapeDtypeStruct((64, 384), BF16)
+    face = jax.ShapeDtypeStruct((80, 384), BF16)
     params = pltpu.CompilerParams(vmem_limit_bytes=24 * 1024 * 1024)
-    first, last, table = pl.pallas_call(
+    first, last = pl.pallas_call(
         y_faces,
-        out_shape=(face, face, jax.ShapeDtypeStruct((16, 384), F32)),
-        in_specs=[hbm()] * 5,
-        out_specs=(vmem(),) * 3,
+        out_shape=(face, face),
+        in_specs=[hbm()] * 3,
+        out_specs=(vmem(), vmem()),
         scratch_shapes=[
-            pltpu.SMEM((8,), F32), pltpu.SMEM((8,), F32), pltpu.VMEM((4, 3, 8, 384), F32), pltpu.VMEM((2, 3, 8, 384), F32),
-            pltpu.VMEM((2, 8, 384), jnp.int32), pltpu.SemaphoreType.DMA((10,)),
+            pltpu.VMEM((4, 3, 8, 384), F32), pltpu.VMEM((2, 3, 8, 384), F32), pltpu.VMEM((2, 8, 384), jnp.int32),
+            pltpu.SemaphoreType.DMA((8,)),
         ],
-        compiler_params=pltpu.CompilerParams(vmem_limit_bytes=56000 * 1024),
-    )(stiffness_table, mass_table, initial_field, source, material)
+        compiler_params=pltpu.CompilerParams(vmem_limit_bytes=55050 * 1024),
+    )(initial_field, source, material)
+    tables = (stiffness_table.reshape(1, 8), mass_table.reshape(1, 8))
     field = initial_field.reshape(3, 128, 384)
     sources = source.reshape(3, 128, 384)
     cells = material.reshape(128, 384)
     before, after = exchange(first, last, "tile")
+    index = jax.ShapeDtypeStruct((256, 192), BF16)
+    column = jax.ShapeDtypeStruct((256, 128), F32)
+    base, scaled, coupling, edge, chosen, place = pl.pallas_call(
+        no_halo,
+        out_shape=(volume, volume, jax.ShapeDtypeStruct((128, 384), F32), index, index, column),
+        in_specs=[vmem()] * 6,
+        out_specs=(vmem(),) * 6,
+        compiler_params=params,
+        cost_estimate=pl.CostEstimate(flops=6_000_000, bytes_accessed=3_000_000, transcendentals=0),
+    )(*tables, field, sources, cells, trace_cells.reshape(1, 256))
     face = jax.ShapeDtypeStruct((128, 384), BF16)
     far, pair = pl.pallas_call(
         z_faces,
         out_shape=(face, face),
-        in_specs=[vmem()] * 6,
+        in_specs=[vmem()] * 5,
         out_specs=(vmem(), vmem()),
         compiler_params=params,
-    )(table, field, sources, cells, before, after)
+    )(field, base, coupling, before, after)
     far, pair = swap(far, pair, "slab")
     members = PLANE * tiles
-    *state, inner, edge, place, spread = pl.pallas_call(
+    once, rim, inner, spread = pl.pallas_call(
         relax_inner,
-        out_shape=(
-            volume, volume, jax.ShapeDtypeStruct((128, 384), F32), jax.ShapeDtypeStruct((12, 8, 384), F32),
-            volume, jax.ShapeDtypeStruct((256, 192), BF16),
-            jax.ShapeDtypeStruct((256, 128), F32), jax.ShapeDtypeStruct((256, 128), F32),
-        ),
-        in_specs=[vmem()] * 7,
-        out_specs=(vmem(),) * 4 + (hbm(),) + (vmem(),) * 3,
-        scratch_shapes=[pltpu.VMEM((192, 384), BF16), pltpu.VMEM((3, 64, 384), F32), pltpu.SemaphoreType.DMA((3,))],
-        compiler_params=params,
-        cost_estimate=pl.CostEstimate(flops=6_000_000, bytes_accessed=4_000_000, transcendentals=0),
-    )(table, field, sources, cells, before, after, trace_cells.reshape(1, 256))
+        out_shape=(volume, jax.ShapeDtypeStruct((12, 8, 384), F32), jax.ShapeDtypeStruct((3, 64, 384), F32), column),
+        in_specs=[vmem()] * 10,
+        out_specs=(vmem(),) * 4,
+        scratch_shapes=[pltpu.VMEM((192, 384), BF16)],
+        compiler_params=params,
+        cost_estimate=pl.CostEstimate(flops=4_000_000, bytes_accessed=3_000_000, transcendentals=0),
+    )(*tables, field, base, scaled, coupling, before, after, chosen, place)
     edges, send = pl.pallas_call(
         functools.partial(relax_edges, planes),
         out_shape=(jax.ShapeDtypeStruct((3, 64, 384), F32), jax.ShapeDtypeStruct((members, 4, 128), BF16)),
@@ -413,7 +411,7 @@
         out_specs=(vmem(), vmem()),
         scratch_shapes=[pltpu.VMEM((192, 384), BF16)],
         compiler_params=params,
-    )(field, *state, edge, place, spread, far, pair, far_right.reshape(-1, 256))
+    )(field, once, scaled, coupling, rim, edge, place, spread, far, pair, far_right.reshape(-1, 256))
     ids = np.arange(slabs * tiles).reshape(planes, members)
     got = lax.all_to_all(send, BOTH, 0, 0, axis_index_groups=ids.tolist(), tiled=True)
     send = pl.pallas_call(
@@ -427,10 +425,9 @@
     result = pl.pallas_call(
         assemble,
         out_shape=volume,
-        in_specs=[hbm(), vmem()],
+        in_specs=[vmem(), vmem()],
         out_specs=hbm(),
-        input_output_aliases={0: 0},
-        scratch_shapes=[pltpu.SemaphoreType.DMA((6,))],
+        scratch_shapes=[pltpu.SemaphoreType.DMA((9,))],
         compiler_params=params,
         cost_estimate=pl.CostEstimate(flops=0, bytes_accessed=600_000, transcendentals=0),
     )(inner, edges)

time: 68.8 us -> 67 us (0.974)
  waiting for transfers between devices: 11.2 us -> 10.2 us
  Pallas kernels: 7.51 us -> 6.67 us
    ppermute x2, waiting for transfers between devices: 3.74 us -> 2.8 us  [exchange(): return (lax.ppermute(last, axis, up), lax.ppermute(first, axis, down))]
    pallas_call x4 -> x5, Pallas kernels: 4.53 us -> 3.68 us  [the longest x1 1.18 us: local(): pl.pallas_call(y_faces, out_shape=(face, face), in_specs=[hbm()] * 3, out...]
where the time goes in v5:
time: 67 us; the launch traced here: 66.6 us
  starting transfers between devices  31.6 us (47%)
  blocking collectives  16.3 us (24%)
  waiting for transfers between devices  10.2 us (15%)
  Pallas kernels  6.67 us (10%)
  between operations  1.52 us (2%)
    all_to_all x1, blocking collectives, local(): lax.all_to_all(send, BOTH, 0, 0, axis_index_groups=ids.tolist(), tiled=True)  16.3 us
    all_to_all x1, starting transfers between devices, local(): lax.all_to_all(send, BOTH, 0, 0, axis_index_groups=ids.T.tolist(), tiled=...  14.8 us
    all_to_all x1, waiting for transfers between devices, local(): lax.all_to_all(send, BOTH, 0, 0, axis_index_groups=ids.T.tolist(), tiled=...  7.33 us
    ppermute x1, starting transfers between devices, swap(): return (far, lax.ppermute(pair, axis, [(i, i ^ 1) for i in range(devices)]))  6.39 us
    ppermute x2, starting transfers between devices, exchange(): return (lax.ppermute(last, axis, up), lax.ppermute(first, axis, down))  5.33 us
    ppermute x1, starting transfers between devices, swap(): lax.ppermute(far, axis, [(i, i + 1 if i % 2 else i - 1) for i in range(1,...  5.11 us
    ppermute x2, waiting for transfers between devices, exchange(): return (lax.ppermute(last, axis, up), lax.ppermute(first, axis, down))  2.8 us
  transfers between devices with their start and end apart: 5, of which 3 were waited for; matrix products, arithmetic and copies ran while one was open for 0% of the time, Pallas kernels for 4%

profile of v5, /device:TPU:1, one launch (start us, length us, event | category | flops | bytes accessed | tf_op | source)
XLA Modules:
  0.0 66.6 jit_solution(15618982208140525927)
XLA Ops:
  0.6 0.0 copy-start
  0.6 0.0 copy-start.2
  0.7 0.0 copy-start.4
  0.7 0.0 copy-start.7
  0.7 0.0 copy-start.8
  0.7 0.0 copy-start.9
  0.7 1.2 %shard_map.123 = (bf16[80,384]{1,0:T(8,128)(2,1)S(1)}, bf16[80,384]{1,0:T(8,128)(2,1)S(1)}) custom-call(f32[3,8,16,384]{3,2,1,0:T(8,128)} %field_hbm.1, f32[3,8,16,384]{3,2,1,0:T(8,128)} %source_hbm.1, s32[8,16,384]{2,1,0:T(8,128)} %material_hbm.1), custom_call_target="tpu_custom_call" | custom-call | tf_op jit(solution)/shard_map/pallas_call | solution.py:362
  1.9 4.0 %collective-permute-start = (bf16[80,384]{1,0:T(8,128)(2,1)S(1)}, bf16[80,384]{1,0:T(8,128)(2,1)S(1)}, u32[]{:S(2)}, u32[]{:S(2)}) collective-permute-start(bf16[80,384]{1,0:T(8,128)(2,1)S(1)} %get-tuple-element.21), channel_id=1, source_target_pairs={{0,1},{1,2},{2,3},{3,4},{4,5},{5,6},{6,7},{8,9},{9,10},{10,11},{11... | collective-permute-start | bytes 184328 | tf_op jit(solution)/shard_map/ppermute | solution.py:346
  5.9 1.3 %collective-permute-start.1 = (bf16[80,384]{1,0:T(8,128)(2,1)S(1)}, bf16[80,384]{1,0:T(8,128)(2,1)S(1)}, u32[]{:S(2)}, u32[]{:S(2)}) collective-permute-start(bf16[80,384]{1,0:T(8,128)(2,1)S(1)} %get-tuple-element.22), channel_id=1, source_target_pairs={{1,0},{2,1},{3,2},{4,3},{5,4},{6,5},{7,6},{9,8},{10,9},{11,10},{12... | collective-permute-start | bytes 184328 | tf_op jit(solution)/shard_map/ppermute | solution.py:346
  7.2 0.0 copy-done
  7.2 0.0 copy-done.2
  7.2 0.0 copy-done.4
  7.2 0.0 copy-done.7
  7.3 0.0 copy-done.8
  7.3 0.0 copy-done.9
  7.3 0.8 %shard_map.122 = (f32[3,128,384]{2,1,0:T(8,128)S(1)}, f32[3,128,384]{2,1,0:T(8,128)S(1)}, f32[128,384]{1,0:T(8,128)S(1)}, bf16[256,192]{1,0:T(8,128)(2,1)S(1)}, ...) custom-call(f32[1,8]{1,0:T(1,128)S(1)} %bitcast.26, f32[1,8]{1,0:T(1,128)S(1)} %bitcast.28, ...), custom_call_target="tpu_custom_call" | custom-call | flops 6000000 | bytes 3000000 | tf_op jit(solution)/shard_map/pallas_call | solution.py:380
  8.1 0.0 collective-permute-done.before_ref
  8.1 2.8 %collective-permute-done.1.after_ref = bf16[80,384]{1,0:T(8,128)(2,1)S(1)} collective-permute-done((bf16[80,384]{1,0:T(8,128)(2,1)S(1)}, bf16[80,384]{1,0:T(8,128)(2,1)S(1)}, u32[]{:S(2)}, u32[]{:S(2)}) %collective-permute-start.1) | collective-permute-done | bytes 61472 | tf_op jit(solution)/shard_map/ppermute | solution.py:346
  10.9 0.1 shard_map.125
  10.9 5.1 %collective-permute-start.2 = (bf16[128,384]{1,0:T(8,128)(2,1)S(1)}, bf16[128,384]{1,0:T(8,128)(2,1)S(1)}, u32[]{:S(2)}, u32[]{:S(2)}) collective-permute-start(bf16[128,384]{1,0:T(8,128)(2,1)S(1)} %get-tuple-element.30), channel_id=1, source_target_pairs={{8,16},{16,8},{24,32},{32,24},{40,48},{48,40},{56,64},{64,56},{72,... | collective-permute-start | bytes 294920 | tf_op jit(solution)/shard_map/ppermute | solution.py:351
  16.1 6.4 %collective-permute-start.3 = (bf16[128,384]{1,0:T(8,128)(2,1)S(1)}, bf16[128,384]{1,0:T(8,128)(2,1)S(1)}, u32[]{:S(2)}, u32[]{:S(2)}) collective-permute-start(bf16[128,384]{1,0:T(8,128)(2,1)S(1)} %get-tuple-element.31), channel_id=1, source_target_pairs={{0,8},{8,0},{16,24},{24,16},{32,40},{40,32},{48,56},{56,48},{64,72... | collective-permute-start | bytes 294920 | tf_op jit(solution)/shard_map/ppermute | solution.py:352
  22.5 0.0 copy-start.3
  22.5 0.8 %shard_map.124 = (f32[3,128,384]{2,1,0:T(8,128)S(1)}, f32[12,8,384]{2,1,0:T(8,128)S(1)}, f32[3,64,384]{2,1,0:T(8,128)S(1)}, f32[256,128]{1,0:T(8,128)S(1)}) custom-call(f32[1,8]{1,0:T(1,128)S(1)} %bitcast.27, f32[1,8]{1,0:T(1,128)S(1)} %bitcast.29, f32[3,128,384]{2,1,0:T(8,128)S(1)} %bitcast.16, f32[3,128,384]{2,1,0:T(8,128)S(1)} %get-tuple-element.18.base_ref, ...), custom_call_target="tpu_custom_call" | custom-call | flops 4000000 | bytes 3000000 | tf_op jit(solution)/shard_map/pallas_call | solution.py:398
  23.3 0.0 collective-permute-done.2.far_ref
  23.3 0.1 collective-permute-done.3.pair_ref
  23.4 0.2 copy-done.3
  23.6 1.0 %shard_map.126 = (f32[3,64,384]{2,1,0:T(8,128)S(1)}, bf16[64,4,128]{2,1,0:T(4,128)(2,1)S(1)}) custom-call(f32[3,128,384]{2,1,0:T(8,128)S(1)} %bitcast.17, f32[3,128,384]{2,1,0:T(8,128)S(1)} %get-tuple-element.26.once_ref, f32[3,128,384]{2,1,0:T(8,128)S(1)} %get-tuple-element.19.scaled_ref, f32[128,384]{1,0:T(8,128)S(1)} %get-tuple-element.20.coupling_ref, ...), custom_call_target="tpu_custom_call" | custom-call | tf_op jit(solution)/shard_map/pallas_call | solution.py:407
  24.6 0.0 copy-start.1
  24.6 0.0 copy-start.6
  24.6 16.3 %all_to_all.10.got_ref = bf16[64,4,128]{2,1,0:T(4,128)(2,1)S(1)} all-to-all(bf16[64,4,128]{2,1,0:T(4,128)(2,1)S(1)} %get-tuple-element.33), channel_id=1, replica_groups={{0,1,2,3,4,5,6,7,8,9,10,11,12,13,14,15,16,17,18,19,20,21,22,23,24,25,26..., dimensions={0} | all-to-all | bytes 131072 | tf_op jit(solution)/shard_map/all_to_all | solution.py:416
  40.9 0.7 %shard_map.129 = bf16[12,8,128]{2,1,0:T(8,128)(2,1)} custom-call(bf16[64,4,128]{2,1,0:T(4,128)(2,1)S(1)} %all_to_all.10.got_ref), custom_call_target="tpu_custom_call" | custom-call | tf_op jit(solution)/shard_map/pallas_call | solution.py:417
  41.6 14.8 %all-to-all-start.1 = ((bf16[12,8,128]{2,1,0:T(8,128)(2,1)}), bf16[12,8,128]{2,1,0:T(8,128)(2,1)S(1)}, u32[]{:S(2)}, u32[]{:S(2)}) async-start(bf16[12,8,128]{2,1,0:T(8,128)(2,1)} %shard_map.129), calls=%async_computation.1 | async-start | bytes 49152 | tf_op jit(solution)/shard_map/all_to_all | solution.py:424
  57.0 0.0 copy-start.5
  57.0 0.9 %shard_map.127 = f32[3,128,384]{2,1,0:T(8,128)} custom-call(f32[3,64,384]{2,1,0:T(8,128)S(1)} %get-tuple-element.25.inner_ref, f32[3,64,384]{2,1,0:T(8,128)S(1)} %get-tuple-element.32.edges_ref), custom_call_target="tpu_custom_call" | custom-call | bytes 600000 | tf_op jit(solution)/shard_map/pallas_call | solution.py:425
  57.9 0.0 copy-done.1
  57.9 0.0 copy-done.6
  57.9 0.4 shard_map.128.part_ref
  58.3 7.3 %all-to-all-done.1.relay_ref = bf16[12,8,128]{2,1,0:T(8,128)(2,1)S(1)} async-done(((bf16[12,8,128]{2,1,0:T(8,128)(2,1)}), bf16[12,8,128]{2,1,0:T(8,128)(2,1)S(1)}, u32[]{:S(2)}, u32[]{:S(2)}) %all-to-all-start.1) | async-done | bytes 24608 | tf_op jit(solution)/shard_map/all_to_all | solution.py:424
  65.7 0.0 copy-done.5
  65.7 0.9 %shard_map.130 = f32[1,256]{1,0:T(1,128)} custom-call(s32[1,9]{1,0:T(1,128)S(1)} %bitcast.25, s32[1,1]{1,0:T(1,128)} %bitcast.13.rank_ref, f32[1,256]{1,0:T(1,128)S(1)} %shard_map.128.part_ref, bf16[12,8,128]{2,1,0:T(8,128)(2,1)S(1)} %all-to-all-done.1.relay_ref, bf16[2304,256]{1,0:T(8,128)(2,1)S(1)} %bitcast.19, bf16[16,256]{1,0:T(8,128)(2,1)S(1)} %bitcast.23), custom_call_target="tpu_custom_call" | custom-call | tf_op jit(solution)/shard_map/pallas_call | solution.py:444
Async XLA Ops:
  0.6 6.6 %copy-start = (f32[3,8,16,384]{3,2,1,0:T(8,128)S(1)}, f32[3,8,16,384]{3,2,1,0:T(8,128)}, u32[]{:S(2)}) copy-start(f32[3,8,16,384]{3,2,1,0:T(8,128)} %field_hbm.1) | copy-start | bytes 1769476
  0.6 6.6 %copy-start.2 = (f32[3,8,16,384]{3,2,1,0:T(8,128)S(1)}, f32[3,8,16,384]{3,2,1,0:T(8,128)}, u32[]{:S(2)}) copy-start(f32[3,8,16,384]{3,2,1,0:T(8,128)} %source_hbm.1) | copy-start | bytes 1769476
  0.7 6.6 %copy-start.4 = (s32[8,16,384]{2,1,0:T(8,128)S(1)}, s32[8,16,384]{2,1,0:T(8,128)}, u32[]{:S(2)}) copy-start(s32[8,16,384]{2,1,0:T(8,128)} %material_hbm.1) | copy-start | bytes 589828
  0.7 6.6 %copy-start.7 = (f32[8]{0:T(128)S(1)}, f32[8]{0:T(128)}, u32[]{:S(2)}) copy-start(f32[8]{0:T(128)} %param.14) | copy-start | bytes 100
  0.7 6.6 %copy-start.8 = (f32[8]{0:T(128)S(1)}, f32[8]{0:T(128)}, u32[]{:S(2)}) copy-start(f32[8]{0:T(128)} %param.15) | copy-start | bytes 100
  0.7 6.6 %copy-start.9 = (s32[1,1,256]{2,1,0:T(1,128)S(1)}, s32[1,1,256]{2,1,0:T(1,128)}, u32[]{:S(2)}) copy-start(s32[1,1,256]{2,1,0:T(1,128)} %param.16) | copy-start | bytes 3076
  1.9 6.2 %collective-permute-start = (bf16[80,384]{1,0:T(8,128)(2,1)S(1)}, bf16[80,384]{1,0:T(8,128)(2,1)S(1)}, u32[]{:S(2)}, u32[]{:S(2)}) collective-permute-start(bf16[80,384]{1,0:T(8,128)(2,1)S(1)} %get-tuple-element.21), channel_id=1, source_target_pairs={{0,1},{1,2},{2,3},{3,4},{4,5},{5,6},{6,7},{8,9},{9,10},{10,11},{11... | collective-permute-start | bytes 184328 | tf_op jit(solution)/shard_map/ppermute | solution.py:346
  5.9 5.0 %collective-permute-start.1 = (bf16[80,384]{1,0:T(8,128)(2,1)S(1)}, bf16[80,384]{1,0:T(8,128)(2,1)S(1)}, u32[]{:S(2)}, u32[]{:S(2)}) collective-permute-start(bf16[80,384]{1,0:T(8,128)(2,1)S(1)} %get-tuple-element.22), channel_id=1, source_target_pairs={{1,0},{2,1},{3,2},{4,3},{5,4},{6,5},{7,6},{9,8},{10,9},{11,10},{12... | collective-permute-start | bytes 184328 | tf_op jit(solution)/shard_map/ppermute | solution.py:346
  10.9 12.3 %collective-permute-start.2 = (bf16[128,384]{1,0:T(8,128)(2,1)S(1)}, bf16[128,384]{1,0:T(8,128)(2,1)S(1)}, u32[]{:S(2)}, u32[]{:S(2)}) collective-permute-start(bf16[128,384]{1,0:T(8,128)(2,1)S(1)} %get-tuple-element.30), channel_id=1, source_target_pairs={{8,16},{16,8},{24,32},{32,24},{40,48},{48,40},{56,64},{64,56},{72,... | collective-permute-start | bytes 294920 | tf_op jit(solution)/shard_map/ppermute | solution.py:351
  16.1 7.3 %collective-permute-start.3 = (bf16[128,384]{1,0:T(8,128)(2,1)S(1)}, bf16[128,384]{1,0:T(8,128)(2,1)S(1)}, u32[]{:S(2)}, u32[]{:S(2)}) collective-permute-start(bf16[128,384]{1,0:T(8,128)(2,1)S(1)} %get-tuple-element.31), channel_id=1, source_target_pairs={{0,8},{8,0},{16,24},{24,16},{32,40},{40,32},{48,56},{56,48},{64,72... | collective-permute-start | bytes 294920 | tf_op jit(solution)/shard_map/ppermute | solution.py:352
  22.5 1.1 %copy-start.3 = (bf16[16,96,1,1,256]{4,1,3,2,0:T(8,128)(2,1)S(1)}, bf16[16,96,1,1,256]{4,1,3,2,0:T(8,128)(2,1)}, u32[]{:S(2)}) copy-start(bf16[16,96,1,1,256]{4,1,3,2,0:T(8,128)(2,1)} %param.20) | copy-start | bytes 2359300
  24.6 33.3 %copy-start.1 = (bf16[1,1,9,256,256]{4,3,2,1,0:T(8,128)(2,1)S(1)}, bf16[1,1,9,256,256]{4,3,2,1,0:T(8,128)(2,1)}, u32[]{:S(2)}) copy-start(bf16[1,1,9,256,256]{4,3,2,1,0:T(8,128)(2,1)} %param.17) | copy-start | bytes 3538948
  24.6 33.3 %copy-start.6 = (s32[1,1,9]{2,1,0:T(1,128)S(1)}, s32[1,1,9]{2,1,0:T(1,128)}, u32[]{:S(2)}) copy-start(s32[1,1,9]{2,1,0:T(1,128)} %param.18) | copy-start | bytes 112
  41.6 24.1 %all-to-all-start.1 = ((bf16[12,8,128]{2,1,0:T(8,128)(2,1)}), bf16[12,8,128]{2,1,0:T(8,128)(2,1)S(1)}, u32[]{:S(2)}, u32[]{:S(2)}) async-start(bf16[12,8,128]{2,1,0:T(8,128)(2,1)} %shard_map.129), calls=%async_computation.1 | async-start | bytes 49152 | tf_op jit(solution)/shard_map/all_to_all | solution.py:424
  57.0 8.6 %copy-start.5 = (bf16[16,1,1,256]{3,0,2,1:T(8,128)(2,1)S(1)}, bf16[16,1,1,256]{3,0,2,1:T(8,128)(2,1)}, u32[]{:S(2)}) copy-start(bf16[16,1,1,256]{3,0,2,1:T(8,128)(2,1)} %param.19) | copy-start | bytes 24580

commit v6 on v5

--- a/solution.py
+++ b/solution.py
@@ -259,6 +259,10 @@
         copy.wait()
 
 
+def seat(z, planes):
+    return (z + planes - planes // 2) % planes
+
+
 def middle(tiles, got_ref, send_ref):
     across = lax.rem(lax.axis_index("slab"), PLANE)
     tile = lax.axis_index("tile")
@@ -276,7 +280,7 @@
     for half in range(2):
         packet = stacked([high[half:half + 1, :], low[half:half + 1, :]] + relay, 8).astype(BF16)
         for z in range(8 * half, min(8 * half + 8, send_ref.shape[0])):
-            send_ref[z] = packet
+            send_ref[seat(z, send_ref.shape[0])] = packet
 
 
 def masked_rows(rows, factors):
@@ -313,7 +317,7 @@
     upward = across == PLANE - 1
     start = jnp.where(upward, plane + 1, plane - 1)
     edge = ((across == 0) | upward) & (start >= 0) & (start < planes)
-    packet = jnp.where(edge, relay_ref[jnp.clip(start, 0, planes - 1)].astype(F32), 0.0)
+    packet = jnp.where(edge, relay_ref[lax.rem(jnp.clip(start, 0, planes - 1) + planes - planes // 2, planes)].astype(F32), 0.0)
     rows = [(packet[2 + 2 * b:3 + 2 * b, :], packet[3 + 2 * b:4 + 2 * b, :]) for b in range(3)]
     first = jnp.where(upward, 6, 0)
     blocks = near_ref[pl.ds(pl.multiple_of(256 * first, 256), 768), :]
@@ -421,7 +425,7 @@
         out_specs=vmem(),
         compiler_params=params,
     )(got)
-    relay = lax.all_to_all(send, BOTH, 0, 0, axis_index_groups=ids.T.tolist(), tiled=True)
+    relay = lax.all_to_all(send, BOTH, 0, 0, axis_index_groups=np.roll(ids, -(planes // 2), axis=0).T.tolist(), tiled=True)
     result = pl.pallas_call(
         assemble,
         out_shape=volume,

time: 67 us -> 63.7 us (0.951)
  waiting for transfers between devices: 10.2 us -> 2.93 us
  starting transfers between devices: 31.6 us -> 35.7 us
    all_to_all x1, waiting for transfers between devices: 7.33 us -> 0.02 us  [local(): lax.all_to_all(send, BOTH, 0, 0, axis_index_groups=np.roll(ids, -(planes...]
    all_to_all x1, starting transfers between devices: 14.8 us -> 18.9 us  [local(): lax.all_to_all(send, BOTH, 0, 0, axis_index_groups=np.roll(ids, -(planes...]
  transfers between devices with their start and end apart: 5 -> 5, of which waited for: 3 -> 2; matrix products, arithmetic and copies ran while one was open for 0% -> 0% of each run, Pallas kernels for 4% -> 4%
where the time goes in v6:
time: 63.7 us; the launch traced here: 63.4 us
  starting transfers between devices  35.7 us (56%)
  blocking collectives  16.3 us (26%)
  Pallas kernels  6.67 us (10%)
  waiting for transfers between devices  2.93 us (5%)
  between operations  1.53 us (2%)
    all_to_all x1, starting transfers between devices, local(): lax.all_to_all(send, BOTH, 0, 0, axis_index_groups=np.roll(ids, -(planes...  18.9 us
    all_to_all x1, blocking collectives, local(): lax.all_to_all(send, BOTH, 0, 0, axis_index_groups=ids.tolist(), tiled=True)  16.3 us
    ppermute x1, starting transfers between devices, swap(): return (far, lax.ppermute(pair, axis, [(i, i ^ 1) for i in range(devices)]))  6.39 us
    ppermute x2, starting transfers between devices, exchange(): return (lax.ppermute(last, axis, up), lax.ppermute(first, axis, down))  5.33 us
    ppermute x1, starting transfers between devices, swap(): lax.ppermute(far, axis, [(i, i + 1 if i % 2 else i - 1) for i in range(1,...  5.11 us
    ppermute x2, waiting for transfers between devices, exchange(): return (lax.ppermute(last, axis, up), lax.ppermute(first, axis, down))  2.8 us
  transfers between devices with their start and end apart: 5, of which 2 were waited for; matrix products, arithmetic and copies ran while one was open for 0% of the time, Pallas kernels for 4%

profile of v6, /device:TPU:1, one launch (start us, length us, event | category | flops | bytes accessed | tf_op | source)
XLA Modules:
  0.0 63.4 jit_solution(7806164890432076012)
XLA Ops:
  0.6 0.0 copy-start
  0.6 0.0 copy-start.2
  0.7 0.0 copy-start.4
  0.7 0.0 copy-start.7
  0.7 0.0 copy-start.8
  0.7 0.0 copy-start.9
  0.7 1.2 %shard_map.123 = (bf16[80,384]{1,0:T(8,128)(2,1)S(1)}, bf16[80,384]{1,0:T(8,128)(2,1)S(1)}) custom-call(f32[3,8,16,384]{3,2,1,0:T(8,128)} %field_hbm.1, f32[3,8,16,384]{3,2,1,0:T(8,128)} %source_hbm.1, s32[8,16,384]{2,1,0:T(8,128)} %material_hbm.1), custom_call_target="tpu_custom_call" | custom-call | tf_op jit(solution)/shard_map/pallas_call | solution.py:366
  1.9 4.0 %collective-permute-start = (bf16[80,384]{1,0:T(8,128)(2,1)S(1)}, bf16[80,384]{1,0:T(8,128)(2,1)S(1)}, u32[]{:S(2)}, u32[]{:S(2)}) collective-permute-start(bf16[80,384]{1,0:T(8,128)(2,1)S(1)} %get-tuple-element.21), channel_id=1, source_target_pairs={{0,1},{1,2},{2,3},{3,4},{4,5},{5,6},{6,7},{8,9},{9,10},{10,11},{11... | collective-permute-start | bytes 184328 | tf_op jit(solution)/shard_map/ppermute | solution.py:350
  5.9 1.3 %collective-permute-start.1 = (bf16[80,384]{1,0:T(8,128)(2,1)S(1)}, bf16[80,384]{1,0:T(8,128)(2,1)S(1)}, u32[]{:S(2)}, u32[]{:S(2)}) collective-permute-start(bf16[80,384]{1,0:T(8,128)(2,1)S(1)} %get-tuple-element.22), channel_id=1, source_target_pairs={{1,0},{2,1},{3,2},{4,3},{5,4},{6,5},{7,6},{9,8},{10,9},{11,10},{12... | collective-permute-start | bytes 184328 | tf_op jit(solution)/shard_map/ppermute | solution.py:350
  7.2 0.0 copy-done
  7.2 0.0 copy-done.2
  7.2 0.0 copy-done.4
  7.2 0.0 copy-done.7
  7.3 0.0 copy-done.8
  7.3 0.0 copy-done.9
  7.3 0.8 %shard_map.122 = (f32[3,128,384]{2,1,0:T(8,128)S(1)}, f32[3,128,384]{2,1,0:T(8,128)S(1)}, f32[128,384]{1,0:T(8,128)S(1)}, bf16[256,192]{1,0:T(8,128)(2,1)S(1)}, ...) custom-call(f32[1,8]{1,0:T(1,128)S(1)} %bitcast.26, f32[1,8]{1,0:T(1,128)S(1)} %bitcast.28, ...), custom_call_target="tpu_custom_call" | custom-call | flops 6000000 | bytes 3000000 | tf_op jit(solution)/shard_map/pallas_call | solution.py:384
  8.1 0.0 collective-permute-done.before_ref
  8.1 2.8 %collective-permute-done.1.after_ref = bf16[80,384]{1,0:T(8,128)(2,1)S(1)} collective-permute-done((bf16[80,384]{1,0:T(8,128)(2,1)S(1)}, bf16[80,384]{1,0:T(8,128)(2,1)S(1)}, u32[]{:S(2)}, u32[]{:S(2)}) %collective-permute-start.1) | collective-permute-done | bytes 61472 | tf_op jit(solution)/shard_map/ppermute | solution.py:350
  10.9 0.1 shard_map.125
  10.9 5.1 %collective-permute-start.2 = (bf16[128,384]{1,0:T(8,128)(2,1)S(1)}, bf16[128,384]{1,0:T(8,128)(2,1)S(1)}, u32[]{:S(2)}, u32[]{:S(2)}) collective-permute-start(bf16[128,384]{1,0:T(8,128)(2,1)S(1)} %get-tuple-element.30), channel_id=1, source_target_pairs={{8,16},{16,8},{24,32},{32,24},{40,48},{48,40},{56,64},{64,56},{72,... | collective-permute-start | bytes 294920 | tf_op jit(solution)/shard_map/ppermute | solution.py:355
  16.1 6.4 %collective-permute-start.3 = (bf16[128,384]{1,0:T(8,128)(2,1)S(1)}, bf16[128,384]{1,0:T(8,128)(2,1)S(1)}, u32[]{:S(2)}, u32[]{:S(2)}) collective-permute-start(bf16[128,384]{1,0:T(8,128)(2,1)S(1)} %get-tuple-element.31), channel_id=1, source_target_pairs={{0,8},{8,0},{16,24},{24,16},{32,40},{40,32},{48,56},{56,48},{64,72... | collective-permute-start | bytes 294920 | tf_op jit(solution)/shard_map/ppermute | solution.py:356
  22.5 0.0 copy-start.3
  22.5 0.8 %shard_map.124 = (f32[3,128,384]{2,1,0:T(8,128)S(1)}, f32[12,8,384]{2,1,0:T(8,128)S(1)}, f32[3,64,384]{2,1,0:T(8,128)S(1)}, f32[256,128]{1,0:T(8,128)S(1)}) custom-call(f32[1,8]{1,0:T(1,128)S(1)} %bitcast.27, f32[1,8]{1,0:T(1,128)S(1)} %bitcast.29, f32[3,128,384]{2,1,0:T(8,128)S(1)} %bitcast.16, f32[3,128,384]{2,1,0:T(8,128)S(1)} %get-tuple-element.18.base_ref, ...), custom_call_target="tpu_custom_call" | custom-call | flops 4000000 | bytes 3000000 | tf_op jit(solution)/shard_map/pallas_call | solution.py:402
  23.3 0.0 collective-permute-done.2.far_ref
  23.3 0.1 collective-permute-done.3.pair_ref
  23.4 0.2 copy-done.3
  23.6 1.0 %shard_map.126 = (f32[3,64,384]{2,1,0:T(8,128)S(1)}, bf16[64,4,128]{2,1,0:T(4,128)(2,1)S(1)}) custom-call(f32[3,128,384]{2,1,0:T(8,128)S(1)} %bitcast.17, f32[3,128,384]{2,1,0:T(8,128)S(1)} %get-tuple-element.26.once_ref, f32[3,128,384]{2,1,0:T(8,128)S(1)} %get-tuple-element.19.scaled_ref, f32[128,384]{1,0:T(8,128)S(1)} %get-tuple-element.20.coupling_ref, ...), custom_call_target="tpu_custom_call" | custom-call | tf_op jit(solution)/shard_map/pallas_call | solution.py:411
  24.6 0.0 copy-start.1
  24.6 0.0 copy-start.6
  24.6 16.3 %all_to_all.10.got_ref = bf16[64,4,128]{2,1,0:T(4,128)(2,1)S(1)} all-to-all(bf16[64,4,128]{2,1,0:T(4,128)(2,1)S(1)} %get-tuple-element.33), channel_id=1, replica_groups={{0,1,2,3,4,5,6,7,8,9,10,11,12,13,14,15,16,17,18,19,20,21,22,23,24,25,26..., dimensions={0} | all-to-all | bytes 131072 | tf_op jit(solution)/shard_map/all_to_all | solution.py:420
  40.9 0.7 %shard_map.129 = bf16[12,8,128]{2,1,0:T(8,128)(2,1)} custom-call(bf16[64,4,128]{2,1,0:T(4,128)(2,1)S(1)} %all_to_all.10.got_ref), custom_call_target="tpu_custom_call" | custom-call | tf_op jit(solution)/shard_map/pallas_call | solution.py:421
  41.6 18.9 %all-to-all-start.1 = ((bf16[12,8,128]{2,1,0:T(8,128)(2,1)}), bf16[12,8,128]{2,1,0:T(8,128)(2,1)S(1)}, u32[]{:S(2)}, u32[]{:S(2)}) async-start(bf16[12,8,128]{2,1,0:T(8,128)(2,1)} %shard_map.129), calls=%async_computation.1 | async-start | bytes 49152 | tf_op jit(solution)/shard_map/all_to_all | solution.py:428
  61.1 0.0 copy-start.5
  61.1 0.9 %shard_map.127 = f32[3,128,384]{2,1,0:T(8,128)} custom-call(f32[3,64,384]{2,1,0:T(8,128)S(1)} %get-tuple-element.25.inner_ref, f32[3,64,384]{2,1,0:T(8,128)S(1)} %get-tuple-element.32.edges_ref), custom_call_target="tpu_custom_call" | custom-call | bytes 600000 | tf_op jit(solution)/shard_map/pallas_call | solution.py:429
  62.0 0.0 copy-done.1
  62.0 0.0 copy-done.6
  62.0 0.4 shard_map.128.part_ref
  62.4 0.0 all-to-all-done.1.relay_ref
  62.4 0.1 copy-done.5
  62.5 0.9 %shard_map.130 = f32[1,256]{1,0:T(1,128)} custom-call(s32[1,9]{1,0:T(1,128)S(1)} %bitcast.25, s32[1,1]{1,0:T(1,128)} %bitcast.13.rank_ref, f32[1,256]{1,0:T(1,128)S(1)} %shard_map.128.part_ref, bf16[12,8,128]{2,1,0:T(8,128)(2,1)S(1)} %all-to-all-done.1.relay_ref, bf16[2304,256]{1,0:T(8,128)(2,1)S(1)} %bitcast.19, bf16[16,256]{1,0:T(8,128)(2,1)S(1)} %bitcast.23), custom_call_target="tpu_custom_call" | custom-call | tf_op jit(solution)/shard_map/pallas_call | solution.py:448
Async XLA Ops:
  0.6 6.6 %copy-start = (f32[3,8,16,384]{3,2,1,0:T(8,128)S(1)}, f32[3,8,16,384]{3,2,1,0:T(8,128)}, u32[]{:S(2)}) copy-start(f32[3,8,16,384]{3,2,1,0:T(8,128)} %field_hbm.1) | copy-start | bytes 1769476
  0.6 6.6 %copy-start.2 = (f32[3,8,16,384]{3,2,1,0:T(8,128)S(1)}, f32[3,8,16,384]{3,2,1,0:T(8,128)}, u32[]{:S(2)}) copy-start(f32[3,8,16,384]{3,2,1,0:T(8,128)} %source_hbm.1) | copy-start | bytes 1769476
  0.7 6.6 %copy-start.4 = (s32[8,16,384]{2,1,0:T(8,128)S(1)}, s32[8,16,384]{2,1,0:T(8,128)}, u32[]{:S(2)}) copy-start(s32[8,16,384]{2,1,0:T(8,128)} %material_hbm.1) | copy-start | bytes 589828
  0.7 6.6 %copy-start.7 = (f32[8]{0:T(128)S(1)}, f32[8]{0:T(128)}, u32[]{:S(2)}) copy-start(f32[8]{0:T(128)} %param.14) | copy-start | bytes 100
  0.7 6.6 %copy-start.8 = (f32[8]{0:T(128)S(1)}, f32[8]{0:T(128)}, u32[]{:S(2)}) copy-start(f32[8]{0:T(128)} %param.15) | copy-start | bytes 100
  0.7 6.6 %copy-start.9 = (s32[1,1,256]{2,1,0:T(1,128)S(1)}, s32[1,1,256]{2,1,0:T(1,128)}, u32[]{:S(2)}) copy-start(s32[1,1,256]{2,1,0:T(1,128)} %param.16) | copy-start | bytes 3076
  1.9 6.2 %collective-permute-start = (bf16[80,384]{1,0:T(8,128)(2,1)S(1)}, bf16[80,384]{1,0:T(8,128)(2,1)S(1)}, u32[]{:S(2)}, u32[]{:S(2)}) collective-permute-start(bf16[80,384]{1,0:T(8,128)(2,1)S(1)} %get-tuple-element.21), channel_id=1, source_target_pairs={{0,1},{1,2},{2,3},{3,4},{4,5},{5,6},{6,7},{8,9},{9,10},{10,11},{11... | collective-permute-start | bytes 184328 | tf_op jit(solution)/shard_map/ppermute | solution.py:350
  5.9 5.0 %collective-permute-start.1 = (bf16[80,384]{1,0:T(8,128)(2,1)S(1)}, bf16[80,384]{1,0:T(8,128)(2,1)S(1)}, u32[]{:S(2)}, u32[]{:S(2)}) collective-permute-start(bf16[80,384]{1,0:T(8,128)(2,1)S(1)} %get-tuple-element.22), channel_id=1, source_target_pairs={{1,0},{2,1},{3,2},{4,3},{5,4},{6,5},{7,6},{9,8},{10,9},{11,10},{12... | collective-permute-start | bytes 184328 | tf_op jit(solution)/shard_map/ppermute | solution.py:350
  10.9 12.3 %collective-permute-start.2 = (bf16[128,384]{1,0:T(8,128)(2,1)S(1)}, bf16[128,384]{1,0:T(8,128)(2,1)S(1)}, u32[]{:S(2)}, u32[]{:S(2)}) collective-permute-start(bf16[128,384]{1,0:T(8,128)(2,1)S(1)} %get-tuple-element.30), channel_id=1, source_target_pairs={{8,16},{16,8},{24,32},{32,24},{40,48},{48,40},{56,64},{64,56},{72,... | collective-permute-start | bytes 294920 | tf_op jit(solution)/shard_map/ppermute | solution.py:355
  16.1 7.3 %collective-permute-start.3 = (bf16[128,384]{1,0:T(8,128)(2,1)S(1)}, bf16[128,384]{1,0:T(8,128)(2,1)S(1)}, u32[]{:S(2)}, u32[]{:S(2)}) collective-permute-start(bf16[128,384]{1,0:T(8,128)(2,1)S(1)} %get-tuple-element.31), channel_id=1, source_target_pairs={{0,8},{8,0},{16,24},{24,16},{32,40},{40,32},{48,56},{56,48},{64,72... | collective-permute-start | bytes 294920 | tf_op jit(solution)/shard_map/ppermute | solution.py:356
  22.5 1.1 %copy-start.3 = (bf16[16,96,1,1,256]{4,1,3,2,0:T(8,128)(2,1)S(1)}, bf16[16,96,1,1,256]{4,1,3,2,0:T(8,128)(2,1)}, u32[]{:S(2)}) copy-start(bf16[16,96,1,1,256]{4,1,3,2,0:T(8,128)(2,1)} %param.20) | copy-start | bytes 2359300
  24.6 37.4 %copy-start.1 = (bf16[1,1,9,256,256]{4,3,2,1,0:T(8,128)(2,1)S(1)}, bf16[1,1,9,256,256]{4,3,2,1,0:T(8,128)(2,1)}, u32[]{:S(2)}) copy-start(bf16[1,1,9,256,256]{4,3,2,1,0:T(8,128)(2,1)} %param.17) | copy-start | bytes 3538948
  24.6 37.4 %copy-start.6 = (s32[1,1,9]{2,1,0:T(1,128)S(1)}, s32[1,1,9]{2,1,0:T(1,128)}, u32[]{:S(2)}) copy-start(s32[1,1,9]{2,1,0:T(1,128)} %param.18) | copy-start | bytes 112
  41.6 20.8 %all-to-all-start.1 = ((bf16[12,8,128]{2,1,0:T(8,128)(2,1)}), bf16[12,8,128]{2,1,0:T(8,128)(2,1)S(1)}, u32[]{:S(2)}, u32[]{:S(2)}) async-start(bf16[12,8,128]{2,1,0:T(8,128)(2,1)} %shard_map.129), calls=%async_computation.1 | async-start | bytes 49152 | tf_op jit(solution)/shard_map/all_to_all | solution.py:428
  61.1 1.4 %copy-start.5 = (bf16[16,1,1,256]{3,0,2,1:T(8,128)(2,1)S(1)}, bf16[16,1,1,256]{3,0,2,1:T(8,128)(2,1)}, u32[]{:S(2)}) copy-start(bf16[16,1,1,256]{3,0,2,1:T(8,128)(2,1)} %param.19) | copy-start | bytes 24580

commit v7 on v5

--- a/solution.py
+++ b/solution.py
@@ -14,6 +14,14 @@
 F32 = jnp.float32
 BF16 = jnp.bfloat16
 BOTH = ("slab", "tile")
+
+
+def seat(member, count):
+    return (member + count - count // 2) % count
+
+
+def seated(member, count):
+    return lax.rem(jnp.clip(member, 0, count - 1) + count - count // 2, count)
 
 
 def table_rows(stiff_ref, mass_ref, width):
@@ -245,7 +253,7 @@
     for to in range(PLANE):
         packet = stacked([parts[0][to:to + 1, :], parts[1][to:to + 1, :]] + traces, 4).astype(BF16)
         for tile in range(tiles):
-            send_ref[to * tiles + tile] = packet
+            send_ref[seat(to, PLANE) * tiles + seat(tile, tiles)] = packet
 
 
 def assemble(inner_ref, edges_ref, out_hbm, sems):
@@ -268,7 +276,7 @@
     for b in range(3):
         wanted = tile + b - 1
         inside = (wanted >= 0) & (wanted < tiles)
-        packet = got_ref[other * tiles + jnp.clip(wanted, 0, tiles - 1)].astype(F32)
+        packet = got_ref[seated(other, PLANE) * tiles + seated(wanted, tiles)].astype(F32)
         packet = jnp.where(inside, packet, 0.0)
         relay += [packet[2:3, :], packet[3:4, :]]
     high = total.astype(BF16).astype(F32)
@@ -276,7 +284,7 @@
     for half in range(2):
         packet = stacked([high[half:half + 1, :], low[half:half + 1, :]] + relay, 8).astype(BF16)
         for z in range(8 * half, min(8 * half + 8, send_ref.shape[0])):
-            send_ref[z] = packet
+            send_ref[seat(z, send_ref.shape[0])] = packet
 
 
 def masked_rows(rows, factors):
@@ -300,7 +308,7 @@
         for b in range(-1, 2):
             up, beside = across + a, tile + b
             inside = (up >= 0) & (up < PLANE) & (beside >= 0) & (beside < tiles)
-            packet = got_ref[jnp.clip(up, 0, PLANE - 1) * tiles + jnp.clip(beside, 0, tiles - 1)].astype(F32)
+            packet = got_ref[seated(up, PLANE) * tiles + seated(beside, tiles)].astype(F32)
             packet = jnp.where(inside, packet, 0.0)
             rows.append((packet[2:3, :], packet[3:4, :]))
     out_ref[...] = products(masked_rows(rows, [mask_ref[0:1, q:q + 1] for q in range(9)]), near_ref[...], 9)
@@ -313,7 +321,7 @@
     upward = across == PLANE - 1
     start = jnp.where(upward, plane + 1, plane - 1)
     edge = ((across == 0) | upward) & (start >= 0) & (start < planes)
-    packet = jnp.where(edge, relay_ref[jnp.clip(start, 0, planes - 1)].astype(F32), 0.0)
+    packet = jnp.where(edge, relay_ref[seated(start, planes)].astype(F32), 0.0)
     rows = [(packet[2 + 2 * b:3 + 2 * b, :], packet[3 + 2 * b:4 + 2 * b, :]) for b in range(3)]
     first = jnp.where(upward, 6, 0)
     blocks = near_ref[pl.ds(pl.multiple_of(256 * first, 256), 768), :]
@@ -412,7 +420,8 @@
         scratch_shapes=[pltpu.VMEM((192, 384), BF16)],
         compiler_params=params,
     )(field, once, scaled, coupling, rim, edge, place, spread, far, pair, far_right.reshape(-1, 256))
-    ids = np.arange(slabs * tiles).reshape(planes, members)
+    ids = np.arange(slabs * tiles).reshape(planes, PLANE, tiles)
+    ids = np.roll(ids, (-(planes // 2), -(PLANE // 2), -(tiles // 2)), axis=(0, 1, 2)).reshape(planes, members)
     got = lax.all_to_all(send, BOTH, 0, 0, axis_index_groups=ids.tolist(), tiled=True)
     send = pl.pallas_call(
         functools.partial(middle, tiles),

time: 67 us -> 61.2 us (0.913)
  waiting for transfers between devices: 10.2 us -> 2.93 us
  starting transfers between devices: 31.6 us -> 36.5 us
  blocking collectives: 16.3 us -> 12.8 us
    all_to_all x1, waiting for transfers between devices: 7.33 us -> 0.02 us  [local(): lax.all_to_all(send, BOTH, 0, 0, axis_index_groups=ids.T.tolist(), tiled=...]
    all_to_all x1, starting transfers between devices: 14.8 us -> 19.7 us  [local(): lax.all_to_all(send, BOTH, 0, 0, axis_index_groups=ids.T.tolist(), tiled=...]
    all_to_all x1, blocking collectives: 16.3 us -> 12.8 us  [local(): lax.all_to_all(send, BOTH, 0, 0, axis_index_groups=ids.tolist(), tiled=True)]
  transfers between devices with their start and end apart: 5 -> 5, of which waited for: 3 -> 2; matrix products, arithmetic and copies ran while one was open for 0% -> 0% of each run, Pallas kernels for 4% -> 5%
where the time goes in v7:
time: 61.2 us; the launch traced here: 60.7 us
  starting transfers between devices  36.5 us (60%)
  blocking collectives  12.8 us (21%)
  Pallas kernels  6.67 us (11%)
  waiting for transfers between devices  2.93 us (5%)
  between operations  1.53 us (2%)
    all_to_all x1, starting transfers between devices, local(): lax.all_to_all(send, BOTH, 0, 0, axis_index_groups=ids.T.tolist(), tiled=...  19.7 us
    all_to_all x1, blocking collectives, local(): lax.all_to_all(send, BOTH, 0, 0, axis_index_groups=ids.tolist(), tiled=True)  12.8 us
    ppermute x1, starting transfers between devices, swap(): return (far, lax.ppermute(pair, axis, [(i, i ^ 1) for i in range(devices)]))  6.39 us
    ppermute x2, starting transfers between devices, exchange(): return (lax.ppermute(last, axis, up), lax.ppermute(first, axis, down))  5.33 us
    ppermute x1, starting transfers between devices, swap(): lax.ppermute(far, axis, [(i, i + 1 if i % 2 else i - 1) for i in range(1,...  5.11 us
    ppermute x2, waiting for transfers between devices, exchange(): return (lax.ppermute(last, axis, up), lax.ppermute(first, axis, down))  2.8 us
  transfers between devices with their start and end apart: 5, of which 2 were waited for; matrix products, arithmetic and copies ran while one was open for 0% of the time, Pallas kernels for 5%

profile of v7, /device:TPU:1, one launch (start us, length us, event | category | flops | bytes accessed | tf_op | source)
XLA Modules:
  0.0 60.7 jit_solution(16237591211146039853)
XLA Ops:
  0.6 0.0 copy-start
  0.6 0.0 copy-start.2
  0.7 0.0 copy-start.4
  0.7 0.0 copy-start.7
  0.7 0.0 copy-start.8
  0.7 0.0 copy-start.9
  0.7 1.2 %shard_map.123 = (bf16[80,384]{1,0:T(8,128)(2,1)S(1)}, bf16[80,384]{1,0:T(8,128)(2,1)S(1)}) custom-call(f32[3,8,16,384]{3,2,1,0:T(8,128)} %field_hbm.1, f32[3,8,16,384]{3,2,1,0:T(8,128)} %source_hbm.1, s32[8,16,384]{2,1,0:T(8,128)} %material_hbm.1), custom_call_target="tpu_custom_call" | custom-call | tf_op jit(solution)/shard_map/pallas_call | solution.py:370
  1.9 4.0 %collective-permute-start = (bf16[80,384]{1,0:T(8,128)(2,1)S(1)}, bf16[80,384]{1,0:T(8,128)(2,1)S(1)}, u32[]{:S(2)}, u32[]{:S(2)}) collective-permute-start(bf16[80,384]{1,0:T(8,128)(2,1)S(1)} %get-tuple-element.21), channel_id=1, source_target_pairs={{0,1},{1,2},{2,3},{3,4},{4,5},{5,6},{6,7},{8,9},{9,10},{10,11},{11... | collective-permute-start | bytes 184328 | tf_op jit(solution)/shard_map/ppermute | solution.py:354
  5.9 1.3 %collective-permute-start.1 = (bf16[80,384]{1,0:T(8,128)(2,1)S(1)}, bf16[80,384]{1,0:T(8,128)(2,1)S(1)}, u32[]{:S(2)}, u32[]{:S(2)}) collective-permute-start(bf16[80,384]{1,0:T(8,128)(2,1)S(1)} %get-tuple-element.22), channel_id=1, source_target_pairs={{1,0},{2,1},{3,2},{4,3},{5,4},{6,5},{7,6},{9,8},{10,9},{11,10},{12... | collective-permute-start | bytes 184328 | tf_op jit(solution)/shard_map/ppermute | solution.py:354
  7.2 0.0 copy-done
  7.2 0.0 copy-done.2
  7.2 0.0 copy-done.4
  7.2 0.0 copy-done.7
  7.3 0.0 copy-done.8
  7.3 0.0 copy-done.9
  7.3 0.8 %shard_map.122 = (f32[3,128,384]{2,1,0:T(8,128)S(1)}, f32[3,128,384]{2,1,0:T(8,128)S(1)}, f32[128,384]{1,0:T(8,128)S(1)}, bf16[256,192]{1,0:T(8,128)(2,1)S(1)}, ...) custom-call(f32[1,8]{1,0:T(1,128)S(1)} %bitcast.26, f32[1,8]{1,0:T(1,128)S(1)} %bitcast.28, ...), custom_call_target="tpu_custom_call" | custom-call | flops 6000000 | bytes 3000000 | tf_op jit(solution)/shard_map/pallas_call | solution.py:388
  8.1 0.0 collective-permute-done.before_ref
  8.1 2.8 %collective-permute-done.1.after_ref = bf16[80,384]{1,0:T(8,128)(2,1)S(1)} collective-permute-done((bf16[80,384]{1,0:T(8,128)(2,1)S(1)}, bf16[80,384]{1,0:T(8,128)(2,1)S(1)}, u32[]{:S(2)}, u32[]{:S(2)}) %collective-permute-start.1) | collective-permute-done | bytes 61472 | tf_op jit(solution)/shard_map/ppermute | solution.py:354
  10.9 0.1 shard_map.125
  10.9 5.1 %collective-permute-start.2 = (bf16[128,384]{1,0:T(8,128)(2,1)S(1)}, bf16[128,384]{1,0:T(8,128)(2,1)S(1)}, u32[]{:S(2)}, u32[]{:S(2)}) collective-permute-start(bf16[128,384]{1,0:T(8,128)(2,1)S(1)} %get-tuple-element.30), channel_id=1, source_target_pairs={{8,16},{16,8},{24,32},{32,24},{40,48},{48,40},{56,64},{64,56},{72,... | collective-permute-start | bytes 294920 | tf_op jit(solution)/shard_map/ppermute | solution.py:359
  16.1 6.4 %collective-permute-start.3 = (bf16[128,384]{1,0:T(8,128)(2,1)S(1)}, bf16[128,384]{1,0:T(8,128)(2,1)S(1)}, u32[]{:S(2)}, u32[]{:S(2)}) collective-permute-start(bf16[128,384]{1,0:T(8,128)(2,1)S(1)} %get-tuple-element.31), channel_id=1, source_target_pairs={{0,8},{8,0},{16,24},{24,16},{32,40},{40,32},{48,56},{56,48},{64,72... | collective-permute-start | bytes 294920 | tf_op jit(solution)/shard_map/ppermute | solution.py:360
  22.5 0.0 copy-start.3
  22.5 0.8 %shard_map.124 = (f32[3,128,384]{2,1,0:T(8,128)S(1)}, f32[12,8,384]{2,1,0:T(8,128)S(1)}, f32[3,64,384]{2,1,0:T(8,128)S(1)}, f32[256,128]{1,0:T(8,128)S(1)}) custom-call(f32[1,8]{1,0:T(1,128)S(1)} %bitcast.27, f32[1,8]{1,0:T(1,128)S(1)} %bitcast.29, f32[3,128,384]{2,1,0:T(8,128)S(1)} %bitcast.16, f32[3,128,384]{2,1,0:T(8,128)S(1)} %get-tuple-element.18.base_ref, ...), custom_call_target="tpu_custom_call" | custom-call | flops 4000000 | bytes 3000000 | tf_op jit(solution)/shard_map/pallas_call | solution.py:406
  23.3 0.0 collective-permute-done.2.far_ref
  23.3 0.1 collective-permute-done.3.pair_ref
  23.4 0.2 copy-done.3
  23.6 1.0 %shard_map.126 = (f32[3,64,384]{2,1,0:T(8,128)S(1)}, bf16[64,4,128]{2,1,0:T(4,128)(2,1)S(1)}) custom-call(f32[3,128,384]{2,1,0:T(8,128)S(1)} %bitcast.17, f32[3,128,384]{2,1,0:T(8,128)S(1)} %get-tuple-element.26.once_ref, f32[3,128,384]{2,1,0:T(8,128)S(1)} %get-tuple-element.19.scaled_ref, f32[128,384]{1,0:T(8,128)S(1)} %get-tuple-element.20.coupling_ref, ...), custom_call_target="tpu_custom_call" | custom-call | tf_op jit(solution)/shard_map/pallas_call | solution.py:415
  24.6 0.0 copy-start.1
  24.6 0.0 copy-start.6
  24.6 12.8 %all_to_all.10.got_ref = bf16[64,4,128]{2,1,0:T(4,128)(2,1)S(1)} all-to-all(bf16[64,4,128]{2,1,0:T(4,128)(2,1)S(1)} %get-tuple-element.33), channel_id=1, replica_groups={{420,421,422,423,416,417,418,419,428,429,430,431,424,425,426,427,436,43..., dimensions={0} | all-to-all | bytes 131072 | tf_op jit(solution)/shard_map/all_to_all | solution.py:425
  37.4 0.7 %shard_map.129 = bf16[12,8,128]{2,1,0:T(8,128)(2,1)} custom-call(bf16[64,4,128]{2,1,0:T(4,128)(2,1)S(1)} %all_to_all.10.got_ref), custom_call_target="tpu_custom_call" | custom-call | tf_op jit(solution)/shard_map/pallas_call | solution.py:426
  38.1 19.7 %all-to-all-start.1 = ((bf16[12,8,128]{2,1,0:T(8,128)(2,1)}), bf16[12,8,128]{2,1,0:T(8,128)(2,1)S(1)}, u32[]{:S(2)}, u32[]{:S(2)}) async-start(bf16[12,8,128]{2,1,0:T(8,128)(2,1)} %shard_map.129), calls=%async_computation.1 | async-start | bytes 49152 | tf_op jit(solution)/shard_map/all_to_all | solution.py:433
  58.4 0.0 copy-start.5
  58.4 0.9 %shard_map.127 = f32[3,128,384]{2,1,0:T(8,128)} custom-call(f32[3,64,384]{2,1,0:T(8,128)S(1)} %get-tuple-element.25.inner_ref, f32[3,64,384]{2,1,0:T(8,128)S(1)} %get-tuple-element.32.edges_ref), custom_call_target="tpu_custom_call" | custom-call | bytes 600000 | tf_op jit(solution)/shard_map/pallas_call | solution.py:434
  59.3 0.0 copy-done.1
  59.3 0.0 copy-done.6
  59.3 0.4 shard_map.128.part_ref
  59.7 0.0 all-to-all-done.1.relay_ref
  59.8 0.1 copy-done.5
  59.8 0.9 %shard_map.130 = f32[1,256]{1,0:T(1,128)} custom-call(s32[1,9]{1,0:T(1,128)S(1)} %bitcast.25, s32[1,1]{1,0:T(1,128)} %bitcast.13.rank_ref, f32[1,256]{1,0:T(1,128)S(1)} %shard_map.128.part_ref, bf16[12,8,128]{2,1,0:T(8,128)(2,1)S(1)} %all-to-all-done.1.relay_ref, bf16[2304,256]{1,0:T(8,128)(2,1)S(1)} %bitcast.19, bf16[16,256]{1,0:T(8,128)(2,1)S(1)} %bitcast.23), custom_call_target="tpu_custom_call" | custom-call | tf_op jit(solution)/shard_map/pallas_call | solution.py:453
Async XLA Ops:
  0.6 6.6 %copy-start = (f32[3,8,16,384]{3,2,1,0:T(8,128)S(1)}, f32[3,8,16,384]{3,2,1,0:T(8,128)}, u32[]{:S(2)}) copy-start(f32[3,8,16,384]{3,2,1,0:T(8,128)} %field_hbm.1) | copy-start | bytes 1769476
  0.6 6.6 %copy-start.2 = (f32[3,8,16,384]{3,2,1,0:T(8,128)S(1)}, f32[3,8,16,384]{3,2,1,0:T(8,128)}, u32[]{:S(2)}) copy-start(f32[3,8,16,384]{3,2,1,0:T(8,128)} %source_hbm.1) | copy-start | bytes 1769476
  0.7 6.6 %copy-start.4 = (s32[8,16,384]{2,1,0:T(8,128)S(1)}, s32[8,16,384]{2,1,0:T(8,128)}, u32[]{:S(2)}) copy-start(s32[8,16,384]{2,1,0:T(8,128)} %material_hbm.1) | copy-start | bytes 589828
  0.7 6.6 %copy-start.7 = (f32[8]{0:T(128)S(1)}, f32[8]{0:T(128)}, u32[]{:S(2)}) copy-start(f32[8]{0:T(128)} %param.14) | copy-start | bytes 100
  0.7 6.6 %copy-start.8 = (f32[8]{0:T(128)S(1)}, f32[8]{0:T(128)}, u32[]{:S(2)}) copy-start(f32[8]{0:T(128)} %param.15) | copy-start | bytes 100
  0.7 6.6 %copy-start.9 = (s32[1,1,256]{2,1,0:T(1,128)S(1)}, s32[1,1,256]{2,1,0:T(1,128)}, u32[]{:S(2)}) copy-start(s32[1,1,256]{2,1,0:T(1,128)} %param.16) | copy-start | bytes 3076
  1.9 6.2 %collective-permute-start = (bf16[80,384]{1,0:T(8,128)(2,1)S(1)}, bf16[80,384]{1,0:T(8,128)(2,1)S(1)}, u32[]{:S(2)}, u32[]{:S(2)}) collective-permute-start(bf16[80,384]{1,0:T(8,128)(2,1)S(1)} %get-tuple-element.21), channel_id=1, source_target_pairs={{0,1},{1,2},{2,3},{3,4},{4,5},{5,6},{6,7},{8,9},{9,10},{10,11},{11... | collective-permute-start | bytes 184328 | tf_op jit(solution)/shard_map/ppermute | solution.py:354
  5.9 5.0 %collective-permute-start.1 = (bf16[80,384]{1,0:T(8,128)(2,1)S(1)}, bf16[80,384]{1,0:T(8,128)(2,1)S(1)}, u32[]{:S(2)}, u32[]{:S(2)}) collective-permute-start(bf16[80,384]{1,0:T(8,128)(2,1)S(1)} %get-tuple-element.22), channel_id=1, source_target_pairs={{1,0},{2,1},{3,2},{4,3},{5,4},{6,5},{7,6},{9,8},{10,9},{11,10},{12... | collective-permute-start | bytes 184328 | tf_op jit(solution)/shard_map/ppermute | solution.py:354
  10.9 12.3 %collective-permute-start.2 = (bf16[128,384]{1,0:T(8,128)(2,1)S(1)}, bf16[128,384]{1,0:T(8,128)(2,1)S(1)}, u32[]{:S(2)}, u32[]{:S(2)}) collective-permute-start(bf16[128,384]{1,0:T(8,128)(2,1)S(1)} %get-tuple-element.30), channel_id=1, source_target_pairs={{8,16},{16,8},{24,32},{32,24},{40,48},{48,40},{56,64},{64,56},{72,... | collective-permute-start | bytes 294920 | tf_op jit(solution)/shard_map/ppermute | solution.py:359
  16.1 7.3 %collective-permute-start.3 = (bf16[128,384]{1,0:T(8,128)(2,1)S(1)}, bf16[128,384]{1,0:T(8,128)(2,1)S(1)}, u32[]{:S(2)}, u32[]{:S(2)}) collective-permute-start(bf16[128,384]{1,0:T(8,128)(2,1)S(1)} %get-tuple-element.31), channel_id=1, source_target_pairs={{0,8},{8,0},{16,24},{24,16},{32,40},{40,32},{48,56},{56,48},{64,72... | collective-permute-start | bytes 294920 | tf_op jit(solution)/shard_map/ppermute | solution.py:360
  22.5 1.1 %copy-start.3 = (bf16[16,96,1,1,256]{4,1,3,2,0:T(8,128)(2,1)S(1)}, bf16[16,96,1,1,256]{4,1,3,2,0:T(8,128)(2,1)}, u32[]{:S(2)}) copy-start(bf16[16,96,1,1,256]{4,1,3,2,0:T(8,128)(2,1)} %param.20) | copy-start | bytes 2359300
  24.6 34.7 %copy-start.1 = (bf16[1,1,9,256,256]{4,3,2,1,0:T(8,128)(2,1)S(1)}, bf16[1,1,9,256,256]{4,3,2,1,0:T(8,128)(2,1)}, u32[]{:S(2)}) copy-start(bf16[1,1,9,256,256]{4,3,2,1,0:T(8,128)(2,1)} %param.17) | copy-start | bytes 3538948
  24.6 34.7 %copy-start.6 = (s32[1,1,9]{2,1,0:T(1,128)S(1)}, s32[1,1,9]{2,1,0:T(1,128)}, u32[]{:S(2)}) copy-start(s32[1,1,9]{2,1,0:T(1,128)} %param.18) | copy-start | bytes 112
  38.1 21.6 %all-to-all-start.1 = ((bf16[12,8,128]{2,1,0:T(8,128)(2,1)}), bf16[12,8,128]{2,1,0:T(8,128)(2,1)S(1)}, u32[]{:S(2)}, u32[]{:S(2)}) async-start(bf16[12,8,128]{2,1,0:T(8,128)(2,1)} %shard_map.129), calls=%async_computation.1 | async-start | bytes 49152 | tf_op jit(solution)/shard_map/all_to_all | solution.py:433
  58.4 1.4 %copy-start.5 = (bf16[16,1,1,256]{3,0,2,1:T(8,128)(2,1)S(1)}, bf16[16,1,1,256]{3,0,2,1:T(8,128)(2,1)}, u32[]{:S(2)}) copy-start(bf16[16,1,1,256]{3,0,2,1:T(8,128)(2,1)} %param.19) | copy-start | bytes 24580

commit v8 on v7

--- a/solution.py
+++ b/solution.py
@@ -17,11 +17,17 @@
 
 
 def seat(member, count):
-    return (member + count - count // 2) % count
+    away = member - count // 2
+    return 2 * abs(away) - (away < 0)
 
 
 def seated(member, count):
-    return lax.rem(jnp.clip(member, 0, count - 1) + count - count // 2, count)
+    away = jnp.clip(member, 0, count - 1) - count // 2
+    return 2 * jnp.abs(away) - jnp.where(away < 0, 1, 0)
+
+
+def seating(count):
+    return np.argsort([seat(member, count) for member in range(count)])
 
 
 def table_rows(stiff_ref, mass_ref, width):
@@ -421,7 +427,7 @@
         compiler_params=params,
     )(field, once, scaled, coupling, rim, edge, place, spread, far, pair, far_right.reshape(-1, 256))
     ids = np.arange(slabs * tiles).reshape(planes, PLANE, tiles)
-    ids = np.roll(ids, (-(planes // 2), -(PLANE // 2), -(tiles // 2)), axis=(0, 1, 2)).reshape(planes, members)
+    ids = ids[np.ix_(seating(planes), seating(PLANE), seating(tiles))].reshape(planes, members)
     got = lax.all_to_all(send, BOTH, 0, 0, axis_index_groups=ids.tolist(), tiled=True)
     send = pl.pallas_call(
         functools.partial(middle, tiles),

time: 61.2 us -> 61.1 us (level)
  transfers between devices with their start and end apart: 5 -> 5, of which waited for: 2 -> 3; matrix products, arithmetic and copies ran while one was open for 0% -> 0% of each run, Pallas kernels for 5% -> 5%
where the time goes in v8:
time: 61.1 us; the launch traced here: 60.7 us
  starting transfers between devices  36.5 us (60%)
  blocking collectives  12.8 us (21%)
  Pallas kernels  6.67 us (11%)
  waiting for transfers between devices  3.03 us (5%)
  between operations  1.52 us (2%)
    all_to_all x1, starting transfers between devices, local(): lax.all_to_all(send, BOTH, 0, 0, axis_index_groups=ids.T.tolist(), tiled=...  19.7 us
    all_to_all x1, blocking collectives, local(): lax.all_to_all(send, BOTH, 0, 0, axis_index_groups=ids.tolist(), tiled=True)  12.8 us
    ppermute x1, starting transfers between devices, swap(): return (far, lax.ppermute(pair, axis, [(i, i ^ 1) for i in range(devices)]))  6.39 us
    ppermute x2, starting transfers between devices, exchange(): return (lax.ppermute(last, axis, up), lax.ppermute(first, axis, down))  5.33 us
    ppermute x1, starting transfers between devices, swap(): lax.ppermute(far, axis, [(i, i + 1 if i % 2 else i - 1) for i in range(1,...  5.11 us
    ppermute x2, waiting for transfers between devices, exchange(): return (lax.ppermute(last, axis, up), lax.ppermute(first, axis, down))  2.8 us
  transfers between devices with their start and end apart: 5, of which 3 were waited for; matrix products, arithmetic and copies ran while one was open for 0% of the time, Pallas kernels for 5%

profile of v8, /device:TPU:1, one launch (start us, length us, event | category | flops | bytes accessed | tf_op | source)
XLA Modules:
  0.0 60.7 jit_solution(14739571682471275451)
XLA Ops:
  0.6 0.0 copy-start
  0.6 0.0 copy-start.2
  0.7 0.0 copy-start.4
  0.7 0.0 copy-start.7
  0.7 0.0 copy-start.8
  0.7 0.0 copy-start.9
  0.7 1.2 %shard_map.123 = (bf16[80,384]{1,0:T(8,128)(2,1)S(1)}, bf16[80,384]{1,0:T(8,128)(2,1)S(1)}) custom-call(f32[3,8,16,384]{3,2,1,0:T(8,128)} %field_hbm.1, f32[3,8,16,384]{3,2,1,0:T(8,128)} %source_hbm.1, s32[8,16,384]{2,1,0:T(8,128)} %material_hbm.1), custom_call_target="tpu_custom_call" | custom-call | tf_op jit(solution)/shard_map/pallas_call | solution.py:376
  1.9 4.0 %collective-permute-start = (bf16[80,384]{1,0:T(8,128)(2,1)S(1)}, bf16[80,384]{1,0:T(8,128)(2,1)S(1)}, u32[]{:S(2)}, u32[]{:S(2)}) collective-permute-start(bf16[80,384]{1,0:T(8,128)(2,1)S(1)} %get-tuple-element.21), channel_id=1, source_target_pairs={{0,1},{1,2},{2,3},{3,4},{4,5},{5,6},{6,7},{8,9},{9,10},{10,11},{11... | collective-permute-start | bytes 184328 | tf_op jit(solution)/shard_map/ppermute | solution.py:360
  5.9 1.3 %collective-permute-start.1 = (bf16[80,384]{1,0:T(8,128)(2,1)S(1)}, bf16[80,384]{1,0:T(8,128)(2,1)S(1)}, u32[]{:S(2)}, u32[]{:S(2)}) collective-permute-start(bf16[80,384]{1,0:T(8,128)(2,1)S(1)} %get-tuple-element.22), channel_id=1, source_target_pairs={{1,0},{2,1},{3,2},{4,3},{5,4},{6,5},{7,6},{9,8},{10,9},{11,10},{12... | collective-permute-start | bytes 184328 | tf_op jit(solution)/shard_map/ppermute | solution.py:360
  7.2 0.0 copy-done
  7.2 0.0 copy-done.2
  7.2 0.0 copy-done.4
  7.2 0.0 copy-done.7
  7.3 0.0 copy-done.8
  7.3 0.0 copy-done.9
  7.3 0.8 %shard_map.122 = (f32[3,128,384]{2,1,0:T(8,128)S(1)}, f32[3,128,384]{2,1,0:T(8,128)S(1)}, f32[128,384]{1,0:T(8,128)S(1)}, bf16[256,192]{1,0:T(8,128)(2,1)S(1)}, ...) custom-call(f32[1,8]{1,0:T(1,128)S(1)} %bitcast.26, f32[1,8]{1,0:T(1,128)S(1)} %bitcast.28, ...), custom_call_target="tpu_custom_call" | custom-call | flops 6000000 | bytes 3000000 | tf_op jit(solution)/shard_map/pallas_call | solution.py:394
  8.1 0.0 collective-permute-done.before_ref
  8.1 2.8 %collective-permute-done.1.after_ref = bf16[80,384]{1,0:T(8,128)(2,1)S(1)} collective-permute-done((bf16[80,384]{1,0:T(8,128)(2,1)S(1)}, bf16[80,384]{1,0:T(8,128)(2,1)S(1)}, u32[]{:S(2)}, u32[]{:S(2)}) %collective-permute-start.1) | collective-permute-done | bytes 61472 | tf_op jit(solution)/shard_map/ppermute | solution.py:360
  10.9 0.1 shard_map.125
  10.9 5.1 %collective-permute-start.2 = (bf16[128,384]{1,0:T(8,128)(2,1)S(1)}, bf16[128,384]{1,0:T(8,128)(2,1)S(1)}, u32[]{:S(2)}, u32[]{:S(2)}) collective-permute-start(bf16[128,384]{1,0:T(8,128)(2,1)S(1)} %get-tuple-element.30), channel_id=1, source_target_pairs={{8,16},{16,8},{24,32},{32,24},{40,48},{48,40},{56,64},{64,56},{72,... | collective-permute-start | bytes 294920 | tf_op jit(solution)/shard_map/ppermute | solution.py:365
  16.1 6.4 %collective-permute-start.3 = (bf16[128,384]{1,0:T(8,128)(2,1)S(1)}, bf16[128,384]{1,0:T(8,128)(2,1)S(1)}, u32[]{:S(2)}, u32[]{:S(2)}) collective-permute-start(bf16[128,384]{1,0:T(8,128)(2,1)S(1)} %get-tuple-element.31), channel_id=1, source_target_pairs={{0,8},{8,0},{16,24},{24,16},{32,40},{40,32},{48,56},{56,48},{64,72... | collective-permute-start | bytes 294920 | tf_op jit(solution)/shard_map/ppermute | solution.py:366
  22.5 0.0 copy-start.3
  22.5 0.8 %shard_map.124 = (f32[3,128,384]{2,1,0:T(8,128)S(1)}, f32[12,8,384]{2,1,0:T(8,128)S(1)}, f32[3,64,384]{2,1,0:T(8,128)S(1)}, f32[256,128]{1,0:T(8,128)S(1)}) custom-call(f32[1,8]{1,0:T(1,128)S(1)} %bitcast.27, f32[1,8]{1,0:T(1,128)S(1)} %bitcast.29, f32[3,128,384]{2,1,0:T(8,128)S(1)} %bitcast.16, f32[3,128,384]{2,1,0:T(8,128)S(1)} %get-tuple-element.18.base_ref, ...), custom_call_target="tpu_custom_call" | custom-call | flops 4000000 | bytes 3000000 | tf_op jit(solution)/shard_map/pallas_call | solution.py:412
  23.3 0.0 collective-permute-done.2.far_ref
  23.3 0.1 collective-permute-done.3.pair_ref
  23.4 0.2 copy-done.3
  23.6 1.0 %shard_map.126 = (f32[3,64,384]{2,1,0:T(8,128)S(1)}, bf16[64,4,128]{2,1,0:T(4,128)(2,1)S(1)}) custom-call(f32[3,128,384]{2,1,0:T(8,128)S(1)} %bitcast.17, f32[3,128,384]{2,1,0:T(8,128)S(1)} %get-tuple-element.26.once_ref, f32[3,128,384]{2,1,0:T(8,128)S(1)} %get-tuple-element.19.scaled_ref, f32[128,384]{1,0:T(8,128)S(1)} %get-tuple-element.20.coupling_ref, ...), custom_call_target="tpu_custom_call" | custom-call | tf_op jit(solution)/shard_map/pallas_call | solution.py:421
  24.6 0.0 copy-start.1
  24.6 0.0 copy-start.6
  24.6 12.8 %all_to_all.10.got_ref = bf16[64,4,128]{2,1,0:T(4,128)(2,1)S(1)} all-to-all(bf16[64,4,128]{2,1,0:T(4,128)(2,1)S(1)} %get-tuple-element.33), channel_id=1, replica_groups={{420,419,421,418,422,417,423,416,412,411,413,410,414,409,415,408,428,42..., dimensions={0} | all-to-all | bytes 131072 | tf_op jit(solution)/shard_map/all_to_all | solution.py:431
  37.4 0.7 %shard_map.129 = bf16[12,8,128]{2,1,0:T(8,128)(2,1)} custom-call(bf16[64,4,128]{2,1,0:T(4,128)(2,1)S(1)} %all_to_all.10.got_ref), custom_call_target="tpu_custom_call" | custom-call | tf_op jit(solution)/shard_map/pallas_call | solution.py:432
  38.1 19.7 %all-to-all-start.1 = ((bf16[12,8,128]{2,1,0:T(8,128)(2,1)}), bf16[12,8,128]{2,1,0:T(8,128)(2,1)S(1)}, u32[]{:S(2)}, u32[]{:S(2)}) async-start(bf16[12,8,128]{2,1,0:T(8,128)(2,1)} %shard_map.129), calls=%async_computation.1 | async-start | bytes 49152 | tf_op jit(solution)/shard_map/all_to_all | solution.py:439
  58.4 0.0 copy-start.5
  58.4 0.9 %shard_map.127 = f32[3,128,384]{2,1,0:T(8,128)} custom-call(f32[3,64,384]{2,1,0:T(8,128)S(1)} %get-tuple-element.25.inner_ref, f32[3,64,384]{2,1,0:T(8,128)S(1)} %get-tuple-element.32.edges_ref), custom_call_target="tpu_custom_call" | custom-call | bytes 600000 | tf_op jit(solution)/shard_map/pallas_call | solution.py:440
  59.3 0.0 copy-done.1
  59.3 0.0 copy-done.6
  59.3 0.4 shard_map.128.part_ref
  59.7 0.1 all-to-all-done.1.relay_ref
  59.8 0.0 copy-done.5
  59.8 0.9 %shard_map.130 = f32[1,256]{1,0:T(1,128)} custom-call(s32[1,9]{1,0:T(1,128)S(1)} %bitcast.25, s32[1,1]{1,0:T(1,128)} %bitcast.13.rank_ref, f32[1,256]{1,0:T(1,128)S(1)} %shard_map.128.part_ref, bf16[12,8,128]{2,1,0:T(8,128)(2,1)S(1)} %all-to-all-done.1.relay_ref, bf16[2304,256]{1,0:T(8,128)(2,1)S(1)} %bitcast.19, bf16[16,256]{1,0:T(8,128)(2,1)S(1)} %bitcast.23), custom_call_target="tpu_custom_call" | custom-call | tf_op jit(solution)/shard_map/pallas_call | solution.py:459
Async XLA Ops:
  0.6 6.6 %copy-start = (f32[3,8,16,384]{3,2,1,0:T(8,128)S(1)}, f32[3,8,16,384]{3,2,1,0:T(8,128)}, u32[]{:S(2)}) copy-start(f32[3,8,16,384]{3,2,1,0:T(8,128)} %field_hbm.1) | copy-start | bytes 1769476
  0.6 6.6 %copy-start.2 = (f32[3,8,16,384]{3,2,1,0:T(8,128)S(1)}, f32[3,8,16,384]{3,2,1,0:T(8,128)}, u32[]{:S(2)}) copy-start(f32[3,8,16,384]{3,2,1,0:T(8,128)} %source_hbm.1) | copy-start | bytes 1769476
  0.7 6.6 %copy-start.4 = (s32[8,16,384]{2,1,0:T(8,128)S(1)}, s32[8,16,384]{2,1,0:T(8,128)}, u32[]{:S(2)}) copy-start(s32[8,16,384]{2,1,0:T(8,128)} %material_hbm.1) | copy-start | bytes 589828
  0.7 6.6 %copy-start.7 = (f32[8]{0:T(128)S(1)}, f32[8]{0:T(128)}, u32[]{:S(2)}) copy-start(f32[8]{0:T(128)} %param.14) | copy-start | bytes 100
  0.7 6.6 %copy-start.8 = (f32[8]{0:T(128)S(1)}, f32[8]{0:T(128)}, u32[]{:S(2)}) copy-start(f32[8]{0:T(128)} %param.15) | copy-start | bytes 100
  0.7 6.6 %copy-start.9 = (s32[1,1,256]{2,1,0:T(1,128)S(1)}, s32[1,1,256]{2,1,0:T(1,128)}, u32[]{:S(2)}) copy-start(s32[1,1,256]{2,1,0:T(1,128)} %param.16) | copy-start | bytes 3076
  1.9 6.2 %collective-permute-start = (bf16[80,384]{1,0:T(8,128)(2,1)S(1)}, bf16[80,384]{1,0:T(8,128)(2,1)S(1)}, u32[]{:S(2)}, u32[]{:S(2)}) collective-permute-start(bf16[80,384]{1,0:T(8,128)(2,1)S(1)} %get-tuple-element.21), channel_id=1, source_target_pairs={{0,1},{1,2},{2,3},{3,4},{4,5},{5,6},{6,7},{8,9},{9,10},{10,11},{11... | collective-permute-start | bytes 184328 | tf_op jit(solution)/shard_map/ppermute | solution.py:360
  5.9 5.0 %collective-permute-start.1 = (bf16[80,384]{1,0:T(8,128)(2,1)S(1)}, bf16[80,384]{1,0:T(8,128)(2,1)S(1)}, u32[]{:S(2)}, u32[]{:S(2)}) collective-permute-start(bf16[80,384]{1,0:T(8,128)(2,1)S(1)} %get-tuple-element.22), channel_id=1, source_target_pairs={{1,0},{2,1},{3,2},{4,3},{5,4},{6,5},{7,6},{9,8},{10,9},{11,10},{12... | collective-permute-start | bytes 184328 | tf_op jit(solution)/shard_map/ppermute | solution.py:360
  10.9 12.3 %collective-permute-start.2 = (bf16[128,384]{1,0:T(8,128)(2,1)S(1)}, bf16[128,384]{1,0:T(8,128)(2,1)S(1)}, u32[]{:S(2)}, u32[]{:S(2)}) collective-permute-start(bf16[128,384]{1,0:T(8,128)(2,1)S(1)} %get-tuple-element.30), channel_id=1, source_target_pairs={{8,16},{16,8},{24,32},{32,24},{40,48},{48,40},{56,64},{64,56},{72,... | collective-permute-start | bytes 294920 | tf_op jit(solution)/shard_map/ppermute | solution.py:365
  16.1 7.3 %collective-permute-start.3 = (bf16[128,384]{1,0:T(8,128)(2,1)S(1)}, bf16[128,384]{1,0:T(8,128)(2,1)S(1)}, u32[]{:S(2)}, u32[]{:S(2)}) collective-permute-start(bf16[128,384]{1,0:T(8,128)(2,1)S(1)} %get-tuple-element.31), channel_id=1, source_target_pairs={{0,8},{8,0},{16,24},{24,16},{32,40},{40,32},{48,56},{56,48},{64,72... | collective-permute-start | bytes 294920 | tf_op jit(solution)/shard_map/ppermute | solution.py:366
  22.5 1.1 %copy-start.3 = (bf16[16,96,1,1,256]{4,1,3,2,0:T(8,128)(2,1)S(1)}, bf16[16,96,1,1,256]{4,1,3,2,0:T(8,128)(2,1)}, u32[]{:S(2)}) copy-start(bf16[16,96,1,1,256]{4,1,3,2,0:T(8,128)(2,1)} %param.20) | copy-start | bytes 2359300
  24.6 34.7 %copy-start.1 = (bf16[1,1,9,256,256]{4,3,2,1,0:T(8,128)(2,1)S(1)}, bf16[1,1,9,256,256]{4,3,2,1,0:T(8,128)(2,1)}, u32[]{:S(2)}) copy-start(bf16[1,1,9,256,256]{4,3,2,1,0:T(8,128)(2,1)} %param.17) | copy-start | bytes 3538948
  24.6 34.7 %copy-start.6 = (s32[1,1,9]{2,1,0:T(1,128)S(1)}, s32[1,1,9]{2,1,0:T(1,128)}, u32[]{:S(2)}) copy-start(s32[1,1,9]{2,1,0:T(1,128)} %param.18) | copy-start | bytes 112
  38.1 21.7 %all-to-all-start.1 = ((bf16[12,8,128]{2,1,0:T(8,128)(2,1)}), bf16[12,8,128]{2,1,0:T(8,128)(2,1)S(1)}, u32[]{:S(2)}, u32[]{:S(2)}) async-start(bf16[12,8,128]{2,1,0:T(8,128)(2,1)} %shard_map.129), calls=%async_computation.1 | async-start | bytes 49152 | tf_op jit(solution)/shard_map/all_to_all | solution.py:439
  58.4 1.4 %copy-start.5 = (bf16[16,1,1,256]{3,0,2,1:T(8,128)(2,1)S(1)}, bf16[16,1,1,256]{3,0,2,1:T(8,128)(2,1)}, u32[]{:S(2)}) copy-start(bf16[16,1,1,256]{3,0,2,1:T(8,128)(2,1)} %param.19) | copy-start | bytes 24580

commit v9 on v7

--- a/solution.py
+++ b/solution.py
@@ -68,7 +68,17 @@
     return value
 
 
-def y_faces(field_hbm, source_hbm, material_hbm, first_ref, last_ref, field_ref, source_ref, material_ref, sems):
+def even_slab():
+    return lax.rem(lax.axis_index("slab"), 2) == 0
+
+
+def in_order(one_ref, two_ref, count):
+    even = even_slab()
+    both = list(zip(bands(one_ref, count), bands(two_ref, count)))
+    return [jnp.where(even, one, two) for one, two in both], [jnp.where(even, two, one) for one, two in both]
+
+
+def y_faces(field_hbm, source_hbm, material_hbm, one_ref, two_ref, field_ref, source_ref, material_ref, sems):
     pairs = [(field_hbm.at[:, :, y, :], field_ref.at[k]) for k, y in enumerate((0, 15, 1, 14))]
     pairs += [(source_hbm.at[:, :, y, :], source_ref.at[k]) for k, y in enumerate((0, 15))]
     pairs += [(material_hbm.at[:, y, :], material_ref.at[k]) for k, y in enumerate((0, 15))]
@@ -77,13 +87,17 @@
         copy.start()
     for copy in copies:
         copy.wait()
-    for k, out_ref in enumerate((first_ref, last_ref)):
+    faces = []
+    for k in range(2):
         values = [field_ref[k, c] for c in range(3)]
         totals = [field_ref[2 + k, c] + row_sum(values[c], 0.0, 0.0) + x_sum(values[c]) for c in range(3)]
         planes = values + [source_ref[k, c] for c in range(3)] + totals + [1.0 + material_ref[k].astype(F32)]
-        for pair in range(5):
-            both = jnp.concatenate(planes[2 * pair:2 * pair + 2], axis=0)
-            out_ref[16 * pair:16 * pair + 16, :] = both.astype(BF16)
+        faces.append([jnp.concatenate(planes[2 * pair:2 * pair + 2], axis=0) for pair in range(5)])
+    even = even_slab()
+    for pair, (first, last) in enumerate(zip(*faces)):
+        here = slice(16 * pair, 16 * pair + 16)
+        one_ref[here, :] = jnp.where(even, last, first).astype(BF16)
+        two_ref[here, :] = jnp.where(even, first, last).astype(BF16)
 
 
 def rim_rows(first, last):
@@ -91,10 +105,9 @@
     return jnp.where(row == 0, first, jnp.where(row == 15, last, 0.0))
 
 
-def z_faces(field_ref, base_ref, coupling_ref, before_ref, after_ref, far_ref, pair_ref):
-    even = lax.rem(lax.axis_index("slab"), 2) == 0
-    before = bands(before_ref, 2)
-    after = bands(after_ref, 2)
+def z_faces(field_ref, base_ref, coupling_ref, one_ref, two_ref, far_ref, pair_ref):
+    even = even_slab()
+    before, after = in_order(one_ref, two_ref, 2)
     faces = []
     for z in (0, 7):
         here = slice(16 * z, 16 * z + 16)
@@ -167,12 +180,11 @@
     chosen_ref[...] = jnp.where(inner == line_column, 1.0, 0.0).astype(BF16)
 
 
-def relax_inner(stiff_ref, mass_ref, field_ref, base_ref, scaled_ref, coupling_ref, before_ref, after_ref, chosen_ref, place_ref,
+def relax_inner(stiff_ref, mass_ref, field_ref, base_ref, scaled_ref, coupling_ref, one_ref, two_ref, chosen_ref, place_ref,
                 once_ref, rim_ref, out_ref, spread_ref, plain_ref):
     rows = table_rows(stiff_ref, mass_ref, field_ref.shape[-1])
     lines = []
-    for side, (ref, y) in enumerate(((before_ref, 0), (after_ref, 15))):
-        halo = bands(ref, 5)
+    for side, (halo, y) in enumerate(zip(in_order(one_ref, two_ref, 5), (0, 15))):
         planes = [halo[k // 2][8 * (k % 2):8 * (k % 2) + 8] for k in range(10)]
         weight, coupling = lookup(planes[9] - 1.0, rows)
         coupling = jnp.where(planes[9] > 0.0, coupling, 0.0)
@@ -208,9 +220,7 @@
 
 def relax_edges(planes, field_ref, once_ref, scaled_ref, coupling_ref, rim_ref, edge_ref, place_ref, spread_ref,
                 far_ref, pair_ref, right_ref, out_ref, send_ref, plain_ref):
-    even = lax.rem(lax.axis_index("slab"), 2) == 0
-    both = list(zip(bands(far_ref, 8), bands(pair_ref, 8)))
-    halo = [[jnp.where(even, far, pair) for far, pair in both], [jnp.where(even, pair, far) for far, pair in both]]
+    halo = in_order(far_ref, pair_ref, 8)
     row8 = lax.broadcasted_iota(jnp.int32, (8, field_ref.shape[-1]), 0)
     for c in range(3):
         once = {z: once_ref[c, 16 * z:16 * z + 16, :] for z in (1, 2, 5, 6)}
@@ -347,11 +357,16 @@
     return pl.BlockSpec(memory_space=pltpu.HBM)
 
 
-def exchange(first, last, axis):
-    devices = lax.axis_size(axis)
-    up = [(i, i + 1) for i in range(devices - 1)]
-    down = [(j, i) for i, j in up]
-    return lax.ppermute(last, axis, up), lax.ppermute(first, axis, down)
+def exchange(one, two):
+    slabs, tiles = lax.axis_size("slab"), lax.axis_size("tile")
+    sent = []
+    for value, sign in ((one, 1), (two, -1)):
+        pairs = []
+        for i in range(slabs):
+            step = sign if i % 2 == 0 else -sign
+            pairs += [(i * tiles + j, i * tiles + j + step) for j in range(tiles) if 0 <= j + step < tiles]
+        sent.append(lax.ppermute(value, BOTH, pairs))
+    return sent
 
 
 def swap(far, pair, axis):
@@ -367,7 +382,7 @@
     volume = jax.ShapeDtypeStruct((3, 128, 384), F32)
     face = jax.ShapeDtypeStruct((80, 384), BF16)
     params = pltpu.CompilerParams(vmem_limit_bytes=24 * 1024 * 1024)
-    first, last = pl.pallas_call(
+    one, two = pl.pallas_call(
         y_faces,
         out_shape=(face, face),
         in_specs=[hbm()] * 3,
@@ -382,7 +397,7 @@
     field = initial_field.reshape(3, 128, 384)
     sources = source.reshape(3, 128, 384)
     cells = material.reshape(128, 384)
-    before, after = exchange(first, last, "tile")
+    one, two = exchange(one, two)
     index = jax.ShapeDtypeStruct((256, 192), BF16)
     column = jax.ShapeDtypeStruct((256, 128), F32)
     base, scaled, coupling, edge, chosen, place = pl.pallas_call(
@@ -400,7 +415,7 @@
         in_specs=[vmem()] * 5,
         out_specs=(vmem(), vmem()),
         compiler_params=params,
-    )(field, base, coupling, before, after)
+    )(field, base, coupling, one, two)
     far, pair = swap(far, pair, "slab")
     members = PLANE * tiles
     once, rim, inner, spread = pl.pallas_call(
@@ -411,7 +426,7 @@
         scratch_shapes=[pltpu.VMEM((192, 384), BF16)],
         compiler_params=params,
         cost_estimate=pl.CostEstimate(flops=4_000_000, bytes_accessed=3_000_000, transcendentals=0),
-    )(*tables, field, base, scaled, coupling, before, after, chosen, place)
+    )(*tables, field, base, scaled, coupling, one, two, chosen, place)
     edges, send = pl.pallas_call(
         functools.partial(relax_edges, planes),
         out_shape=(jax.ShapeDtypeStruct((3, 64, 384), F32), jax.ShapeDtypeStruct((members, 4, 128), BF16)),

time: 61.2 us -> 61.2 us (level)
  waiting for transfers between devices: 2.93 us -> 0.51 us
  starting transfers between devices: 36.5 us -> 38.9 us
    ppermute x2, waiting for transfers between devices: 2.8 us -> 0.41 us  [exchange(): sent.append(lax.ppermute(value, BOTH, pairs))]
    ppermute x1, starting transfers between devices: 5.11 us -> 6.87 us  [swap(): lax.ppermute(far, axis, [(i, i + 1 if i % 2 else i - 1) for i in range(1,...]
    ppermute x2, starting transfers between devices: 5.33 us -> 5.95 us  [exchange(): sent.append(lax.ppermute(value, BOTH, pairs))]
where the time goes in v9:
time: 61.2 us; the launch traced here: 60.7 us
  starting transfers between devices  38.9 us (64%)
  blocking collectives  12.8 us (21%)
  Pallas kernels  6.72 us (11%)
  between operations  1.53 us (2%)
    all_to_all x1, starting transfers between devices, local(): lax.all_to_all(send, BOTH, 0, 0, axis_index_groups=ids.T.tolist(), tiled=...  19.7 us
    all_to_all x1, blocking collectives, local(): lax.all_to_all(send, BOTH, 0, 0, axis_index_groups=ids.tolist(), tiled=True)  12.8 us
    ppermute x1, starting transfers between devices, swap(): lax.ppermute(far, axis, [(i, i + 1 if i % 2 else i - 1) for i in range(1,...  6.87 us
    ppermute x1, starting transfers between devices, swap(): return (far, lax.ppermute(pair, axis, [(i, i ^ 1) for i in range(devices)]))  6.39 us
    ppermute x2, starting transfers between devices, exchange(): sent.append(lax.ppermute(value, BOTH, pairs))  5.95 us
  transfers between devices with their start and end apart: 5, of which 2 were waited for; matrix products, arithmetic and copies ran while one was open for 0% of the time, Pallas kernels for 5%

profile of v9, /device:TPU:1, one launch (start us, length us, event | category | flops | bytes accessed | tf_op | source)
XLA Modules:
  0.0 60.7 jit_solution(12430968173301864480)
XLA Ops:
  0.6 0.0 copy-start
  0.6 0.0 copy-start.2
  0.7 0.0 copy-start.4
  0.7 0.0 copy-start.7
  0.7 0.0 copy-start.8
  0.7 0.0 copy-start.9
  0.7 1.2 %shard_map.123 = (bf16[80,384]{1,0:T(8,128)(2,1)S(1)}, bf16[80,384]{1,0:T(8,128)(2,1)S(1)}) custom-call(f32[3,8,16,384]{3,2,1,0:T(8,128)} %field_hbm.1, f32[3,8,16,384]{3,2,1,0:T(8,128)} %source_hbm.1, s32[8,16,384]{2,1,0:T(8,128)} %material_hbm.1), custom_call_target="tpu_custom_call" | custom-call | tf_op jit(solution)/shard_map/pallas_call | solution.py:385
  1.9 1.3 %collective-permute-start = (bf16[80,384]{1,0:T(8,128)(2,1)S(1)}, bf16[80,384]{1,0:T(8,128)(2,1)S(1)}, u32[]{:S(2)}, u32[]{:S(2)}) collective-permute-start(bf16[80,384]{1,0:T(8,128)(2,1)S(1)} %get-tuple-element.21), channel_id=1, source_target_pairs={{0,1},{1,2},{2,3},{3,4},{4,5},{5,6},{6,7},{9,8},{10,9},{11,10},{12... | collective-permute-start | bytes 184328 | tf_op jit(solution)/shard_map/ppermute | solution.py:368
  3.2 4.7 %collective-permute-start.1 = (bf16[80,384]{1,0:T(8,128)(2,1)S(1)}, bf16[80,384]{1,0:T(8,128)(2,1)S(1)}, u32[]{:S(2)}, u32[]{:S(2)}) collective-permute-start(bf16[80,384]{1,0:T(8,128)(2,1)S(1)} %get-tuple-element.22), channel_id=1, source_target_pairs={{1,0},{2,1},{3,2},{4,3},{5,4},{6,5},{7,6},{8,9},{9,10},{10,11},{11... | collective-permute-start | bytes 184328 | tf_op jit(solution)/shard_map/ppermute | solution.py:368
  7.9 0.0 copy-done
  7.9 0.0 copy-done.2
  7.9 0.0 copy-done.4
  7.9 0.0 copy-done.7
  7.9 0.0 copy-done.8
  7.9 0.0 copy-done.9
  7.9 0.8 %shard_map.122 = (f32[3,128,384]{2,1,0:T(8,128)S(1)}, f32[3,128,384]{2,1,0:T(8,128)S(1)}, f32[128,384]{1,0:T(8,128)S(1)}, bf16[256,192]{1,0:T(8,128)(2,1)S(1)}, ...) custom-call(f32[1,8]{1,0:T(1,128)S(1)} %bitcast.26, f32[1,8]{1,0:T(1,128)S(1)} %bitcast.28, ...), custom_call_target="tpu_custom_call" | custom-call | flops 6000000 | bytes 3000000 | tf_op jit(solution)/shard_map/pallas_call | solution.py:403
  8.7 0.0 collective-permute-done.one_ref
  8.7 0.4 collective-permute-done.1.two_ref
  9.1 0.1 shard_map.125
  9.2 6.9 %collective-permute-start.2 = (bf16[128,384]{1,0:T(8,128)(2,1)S(1)}, bf16[128,384]{1,0:T(8,128)(2,1)S(1)}, u32[]{:S(2)}, u32[]{:S(2)}) collective-permute-start(bf16[128,384]{1,0:T(8,128)(2,1)S(1)} %get-tuple-element.30), channel_id=1, source_target_pairs={{8,16},{16,8},{24,32},{32,24},{40,48},{48,40},{56,64},{64,56},{72,... | collective-permute-start | bytes 294920 | tf_op jit(solution)/shard_map/ppermute | solution.py:374
  16.1 6.4 %collective-permute-start.3 = (bf16[128,384]{1,0:T(8,128)(2,1)S(1)}, bf16[128,384]{1,0:T(8,128)(2,1)S(1)}, u32[]{:S(2)}, u32[]{:S(2)}) collective-permute-start(bf16[128,384]{1,0:T(8,128)(2,1)S(1)} %get-tuple-element.31), channel_id=1, source_target_pairs={{0,8},{8,0},{16,24},{24,16},{32,40},{40,32},{48,56},{56,48},{64,72... | collective-permute-start | bytes 294920 | tf_op jit(solution)/shard_map/ppermute | solution.py:375
  22.5 0.0 copy-start.3
  22.5 0.8 %shard_map.124 = (f32[3,128,384]{2,1,0:T(8,128)S(1)}, f32[12,8,384]{2,1,0:T(8,128)S(1)}, f32[3,64,384]{2,1,0:T(8,128)S(1)}, f32[256,128]{1,0:T(8,128)S(1)}) custom-call(f32[1,8]{1,0:T(1,128)S(1)} %bitcast.27, f32[1,8]{1,0:T(1,128)S(1)} %bitcast.29, f32[3,128,384]{2,1,0:T(8,128)S(1)} %bitcast.16, f32[3,128,384]{2,1,0:T(8,128)S(1)} %get-tuple-element.18.base_ref, ...), custom_call_target="tpu_custom_call" | custom-call | flops 4000000 | bytes 3000000 | tf_op jit(solution)/shard_map/pallas_call | solution.py:421
  23.3 0.0 collective-permute-done.2.far_ref
  23.3 0.1 collective-permute-done.3.pair_ref
  23.4 0.2 copy-done.3
  23.6 1.0 %shard_map.126 = (f32[3,64,384]{2,1,0:T(8,128)S(1)}, bf16[64,4,128]{2,1,0:T(4,128)(2,1)S(1)}) custom-call(f32[3,128,384]{2,1,0:T(8,128)S(1)} %bitcast.17, f32[3,128,384]{2,1,0:T(8,128)S(1)} %get-tuple-element.26.once_ref, f32[3,128,384]{2,1,0:T(8,128)S(1)} %get-tuple-element.19.scaled_ref, f32[128,384]{1,0:T(8,128)S(1)} %get-tuple-element.20.coupling_ref, ...), custom_call_target="tpu_custom_call" | custom-call | tf_op jit(solution)/shard_map/pallas_call | solution.py:430
  24.6 0.0 copy-start.1
  24.6 0.0 copy-start.6
  24.7 12.8 %all_to_all.10.got_ref = bf16[64,4,128]{2,1,0:T(4,128)(2,1)S(1)} all-to-all(bf16[64,4,128]{2,1,0:T(4,128)(2,1)S(1)} %get-tuple-element.33), channel_id=1, replica_groups={{420,421,422,423,416,417,418,419,428,429,430,431,424,425,426,427,436,43..., dimensions={0} | all-to-all | bytes 131072 | tf_op jit(solution)/shard_map/all_to_all | solution.py:440
  37.4 0.7 %shard_map.129 = bf16[12,8,128]{2,1,0:T(8,128)(2,1)} custom-call(bf16[64,4,128]{2,1,0:T(4,128)(2,1)S(1)} %all_to_all.10.got_ref), custom_call_target="tpu_custom_call" | custom-call | tf_op jit(solution)/shard_map/pallas_call | solution.py:441
  38.1 19.7 %all-to-all-start.1 = ((bf16[12,8,128]{2,1,0:T(8,128)(2,1)}), bf16[12,8,128]{2,1,0:T(8,128)(2,1)S(1)}, u32[]{:S(2)}, u32[]{:S(2)}) async-start(bf16[12,8,128]{2,1,0:T(8,128)(2,1)} %shard_map.129), calls=%async_computation.1 | async-start | bytes 49152 | tf_op jit(solution)/shard_map/all_to_all | solution.py:448
  58.4 0.0 copy-start.5
  58.4 0.9 %shard_map.127 = f32[3,128,384]{2,1,0:T(8,128)} custom-call(f32[3,64,384]{2,1,0:T(8,128)S(1)} %get-tuple-element.25.inner_ref, f32[3,64,384]{2,1,0:T(8,128)S(1)} %get-tuple-element.32.edges_ref), custom_call_target="tpu_custom_call" | custom-call | bytes 600000 | tf_op jit(solution)/shard_map/pallas_call | solution.py:449
  59.3 0.0 copy-done.1
  59.3 0.0 copy-done.6
  59.4 0.4 shard_map.128.part_ref
  59.7 0.0 all-to-all-done.1.relay_ref
  59.8 0.1 copy-done.5
  59.8 0.9 %shard_map.130 = f32[1,256]{1,0:T(1,128)} custom-call(s32[1,9]{1,0:T(1,128)S(1)} %bitcast.25, s32[1,1]{1,0:T(1,128)} %bitcast.13.rank_ref, f32[1,256]{1,0:T(1,128)S(1)} %shard_map.128.part_ref, bf16[12,8,128]{2,1,0:T(8,128)(2,1)S(1)} %all-to-all-done.1.relay_ref, bf16[2304,256]{1,0:T(8,128)(2,1)S(1)} %bitcast.19, bf16[16,256]{1,0:T(8,128)(2,1)S(1)} %bitcast.23), custom_call_target="tpu_custom_call" | custom-call | tf_op jit(solution)/shard_map/pallas_call | solution.py:468
Async XLA Ops:
  0.6 7.2 %copy-start = (f32[3,8,16,384]{3,2,1,0:T(8,128)S(1)}, f32[3,8,16,384]{3,2,1,0:T(8,128)}, u32[]{:S(2)}) copy-start(f32[3,8,16,384]{3,2,1,0:T(8,128)} %field_hbm.1) | copy-start | bytes 1769476
  0.6 7.2 %copy-start.2 = (f32[3,8,16,384]{3,2,1,0:T(8,128)S(1)}, f32[3,8,16,384]{3,2,1,0:T(8,128)}, u32[]{:S(2)}) copy-start(f32[3,8,16,384]{3,2,1,0:T(8,128)} %source_hbm.1) | copy-start | bytes 1769476
  0.7 7.2 %copy-start.4 = (s32[8,16,384]{2,1,0:T(8,128)S(1)}, s32[8,16,384]{2,1,0:T(8,128)}, u32[]{:S(2)}) copy-start(s32[8,16,384]{2,1,0:T(8,128)} %material_hbm.1) | copy-start | bytes 589828
  0.7 7.2 %copy-start.7 = (f32[8]{0:T(128)S(1)}, f32[8]{0:T(128)}, u32[]{:S(2)}) copy-start(f32[8]{0:T(128)} %param.14) | copy-start | bytes 100
  0.7 7.2 %copy-start.8 = (f32[8]{0:T(128)S(1)}, f32[8]{0:T(128)}, u32[]{:S(2)}) copy-start(f32[8]{0:T(128)} %param.15) | copy-start | bytes 100
  0.7 7.2 %copy-start.9 = (s32[1,1,256]{2,1,0:T(1,128)S(1)}, s32[1,1,256]{2,1,0:T(1,128)}, u32[]{:S(2)}) copy-start(s32[1,1,256]{2,1,0:T(1,128)} %param.16) | copy-start | bytes 3076
  1.9 6.8 %collective-permute-start = (bf16[80,384]{1,0:T(8,128)(2,1)S(1)}, bf16[80,384]{1,0:T(8,128)(2,1)S(1)}, u32[]{:S(2)}, u32[]{:S(2)}) collective-permute-start(bf16[80,384]{1,0:T(8,128)(2,1)S(1)} %get-tuple-element.21), channel_id=1, source_target_pairs={{0,1},{1,2},{2,3},{3,4},{4,5},{5,6},{6,7},{9,8},{10,9},{11,10},{12... | collective-permute-start | bytes 184328 | tf_op jit(solution)/shard_map/ppermute | solution.py:368
  3.2 5.9 %collective-permute-start.1 = (bf16[80,384]{1,0:T(8,128)(2,1)S(1)}, bf16[80,384]{1,0:T(8,128)(2,1)S(1)}, u32[]{:S(2)}, u32[]{:S(2)}) collective-permute-start(bf16[80,384]{1,0:T(8,128)(2,1)S(1)} %get-tuple-element.22), channel_id=1, source_target_pairs={{1,0},{2,1},{3,2},{4,3},{5,4},{6,5},{7,6},{8,9},{9,10},{10,11},{11... | collective-permute-start | bytes 184328 | tf_op jit(solution)/shard_map/ppermute | solution.py:368
  9.2 14.1 %collective-permute-start.2 = (bf16[128,384]{1,0:T(8,128)(2,1)S(1)}, bf16[128,384]{1,0:T(8,128)(2,1)S(1)}, u32[]{:S(2)}, u32[]{:S(2)}) collective-permute-start(bf16[128,384]{1,0:T(8,128)(2,1)S(1)} %get-tuple-element.30), channel_id=1, source_target_pairs={{8,16},{16,8},{24,32},{32,24},{40,48},{48,40},{56,64},{64,56},{72,... | collective-permute-start | bytes 294920 | tf_op jit(solution)/shard_map/ppermute | solution.py:374
  16.1 7.3 %collective-permute-start.3 = (bf16[128,384]{1,0:T(8,128)(2,1)S(1)}, bf16[128,384]{1,0:T(8,128)(2,1)S(1)}, u32[]{:S(2)}, u32[]{:S(2)}) collective-permute-start(bf16[128,384]{1,0:T(8,128)(2,1)S(1)} %get-tuple-element.31), channel_id=1, source_target_pairs={{0,8},{8,0},{16,24},{24,16},{32,40},{40,32},{48,56},{56,48},{64,72... | collective-permute-start | bytes 294920 | tf_op jit(solution)/shard_map/ppermute | solution.py:375
  22.5 1.1 %copy-start.3 = (bf16[16,96,1,1,256]{4,1,3,2,0:T(8,128)(2,1)S(1)}, bf16[16,96,1,1,256]{4,1,3,2,0:T(8,128)(2,1)}, u32[]{:S(2)}) copy-start(bf16[16,96,1,1,256]{4,1,3,2,0:T(8,128)(2,1)} %param.20) | copy-start | bytes 2359300
  24.6 34.7 %copy-start.1 = (bf16[1,1,9,256,256]{4,3,2,1,0:T(8,128)(2,1)S(1)}, bf16[1,1,9,256,256]{4,3,2,1,0:T(8,128)(2,1)}, u32[]{:S(2)}) copy-start(bf16[1,1,9,256,256]{4,3,2,1,0:T(8,128)(2,1)} %param.17) | copy-start | bytes 3538948
  24.6 34.7 %copy-start.6 = (s32[1,1,9]{2,1,0:T(1,128)S(1)}, s32[1,1,9]{2,1,0:T(1,128)}, u32[]{:S(2)}) copy-start(s32[1,1,9]{2,1,0:T(1,128)} %param.18) | copy-start | bytes 112
  38.1 21.6 %all-to-all-start.1 = ((bf16[12,8,128]{2,1,0:T(8,128)(2,1)}), bf16[12,8,128]{2,1,0:T(8,128)(2,1)S(1)}, u32[]{:S(2)}, u32[]{:S(2)}) async-start(bf16[12,8,128]{2,1,0:T(8,128)(2,1)} %shard_map.129), calls=%async_computation.1 | async-start | bytes 49152 | tf_op jit(solution)/shard_map/all_to_all | solution.py:448
  58.4 1.4 %copy-start.5 = (bf16[16,1,1,256]{3,0,2,1:T(8,128)(2,1)S(1)}, bf16[16,1,1,256]{3,0,2,1:T(8,128)(2,1)}, u32[]{:S(2)}) copy-start(bf16[16,1,1,256]{3,0,2,1:T(8,128)(2,1)} %param.19) | copy-start | bytes 24580

commit v10 on v7

--- a/solution.py
+++ b/solution.py
@@ -253,7 +253,7 @@
     for to in range(PLANE):
         packet = stacked([parts[0][to:to + 1, :], parts[1][to:to + 1, :]] + traces, 4).astype(BF16)
         for tile in range(tiles):
-            send_ref[seat(to, PLANE) * tiles + seat(tile, tiles)] = packet
+            send_ref[to * tiles + seat(tile, tiles)] = packet
 
 
 def assemble(inner_ref, edges_ref, out_hbm, sems):
@@ -276,7 +276,7 @@
     for b in range(3):
         wanted = tile + b - 1
         inside = (wanted >= 0) & (wanted < tiles)
-        packet = got_ref[seated(other, PLANE) * tiles + seated(wanted, tiles)].astype(F32)
+        packet = got_ref[other * tiles + seated(wanted, tiles)].astype(F32)
         packet = jnp.where(inside, packet, 0.0)
         relay += [packet[2:3, :], packet[3:4, :]]
     high = total.astype(BF16).astype(F32)
@@ -308,7 +308,7 @@
         for b in range(-1, 2):
             up, beside = across + a, tile + b
             inside = (up >= 0) & (up < PLANE) & (beside >= 0) & (beside < tiles)
-            packet = got_ref[seated(up, PLANE) * tiles + seated(beside, tiles)].astype(F32)
+            packet = got_ref[jnp.clip(up, 0, PLANE - 1) * tiles + seated(beside, tiles)].astype(F32)
             packet = jnp.where(inside, packet, 0.0)
             rows.append((packet[2:3, :], packet[3:4, :]))
     out_ref[...] = products(masked_rows(rows, [mask_ref[0:1, q:q + 1] for q in range(9)]), near_ref[...], 9)
@@ -421,7 +421,7 @@
         compiler_params=params,
     )(field, once, scaled, coupling, rim, edge, place, spread, far, pair, far_right.reshape(-1, 256))
     ids = np.arange(slabs * tiles).reshape(planes, PLANE, tiles)
-    ids = np.roll(ids, (-(planes // 2), -(PLANE // 2), -(tiles // 2)), axis=(0, 1, 2)).reshape(planes, members)
+    ids = np.roll(ids, (-(planes // 2), -(tiles // 2)), axis=(0, 2)).reshape(planes, members)
     got = lax.all_to_all(send, BOTH, 0, 0, axis_index_groups=ids.tolist(), tiled=True)
     send = pl.pallas_call(
         functools.partial(middle, tiles),

time: 61.2 us -> 61.7 us (level)
  blocking collectives: 12.8 us -> 14.2 us
  starting transfers between devices: 36.5 us -> 35.7 us
    all_to_all x1, blocking collectives: 12.8 us -> 14.2 us  [local(): lax.all_to_all(send, BOTH, 0, 0, axis_index_groups=ids.tolist(), tiled=True)]
    all_to_all x1, starting transfers between devices: 19.7 us -> 18.9 us  [local(): lax.all_to_all(send, BOTH, 0, 0, axis_index_groups=ids.T.tolist(), tiled=...]
where the time goes in v10:
time: 61.7 us; the launch traced here: 61.3 us
  starting transfers between devices  35.7 us (58%)
  blocking collectives  14.2 us (23%)
  Pallas kernels  6.67 us (11%)
  waiting for transfers between devices  2.93 us (5%)
  between operations  1.53 us (2%)
    all_to_all x1, starting transfers between devices, local(): lax.all_to_all(send, BOTH, 0, 0, axis_index_groups=ids.T.tolist(), tiled=...  18.9 us
    all_to_all x1, blocking collectives, local(): lax.all_to_all(send, BOTH, 0, 0, axis_index_groups=ids.tolist(), tiled=True)  14.2 us
    ppermute x1, starting transfers between devices, swap(): return (far, lax.ppermute(pair, axis, [(i, i ^ 1) for i in range(devices)]))  6.39 us
    ppermute x2, starting transfers between devices, exchange(): return (lax.ppermute(last, axis, up), lax.ppermute(first, axis, down))  5.33 us
    ppermute x1, starting transfers between devices, swap(): lax.ppermute(far, axis, [(i, i + 1 if i % 2 else i - 1) for i in range(1,...  5.11 us
    ppermute x2, waiting for transfers between devices, exchange(): return (lax.ppermute(last, axis, up), lax.ppermute(first, axis, down))  2.8 us
  transfers between devices with their start and end apart: 5, of which 2 were waited for; matrix products, arithmetic and copies ran while one was open for 0% of the time, Pallas kernels for 5%

profile of v10, /device:TPU:1, one launch (start us, length us, event | category | flops | bytes accessed | tf_op | source)
XLA Modules:
  0.0 61.3 jit_solution(1584370323281629712)
XLA Ops:
  0.6 0.0 copy-start
  0.6 0.0 copy-start.2
  0.7 0.0 copy-start.4
  0.7 0.0 copy-start.7
  0.7 0.0 copy-start.8
  0.7 0.0 copy-start.9
  0.7 1.2 %shard_map.123 = (bf16[80,384]{1,0:T(8,128)(2,1)S(1)}, bf16[80,384]{1,0:T(8,128)(2,1)S(1)}) custom-call(f32[3,8,16,384]{3,2,1,0:T(8,128)} %field_hbm.1, f32[3,8,16,384]{3,2,1,0:T(8,128)} %source_hbm.1, s32[8,16,384]{2,1,0:T(8,128)} %material_hbm.1), custom_call_target="tpu_custom_call" | custom-call | tf_op jit(solution)/shard_map/pallas_call | solution.py:370
  1.9 4.0 %collective-permute-start = (bf16[80,384]{1,0:T(8,128)(2,1)S(1)}, bf16[80,384]{1,0:T(8,128)(2,1)S(1)}, u32[]{:S(2)}, u32[]{:S(2)}) collective-permute-start(bf16[80,384]{1,0:T(8,128)(2,1)S(1)} %get-tuple-element.21), channel_id=1, source_target_pairs={{0,1},{1,2},{2,3},{3,4},{4,5},{5,6},{6,7},{8,9},{9,10},{10,11},{11... | collective-permute-start | bytes 184328 | tf_op jit(solution)/shard_map/ppermute | solution.py:354
  5.9 1.3 %collective-permute-start.1 = (bf16[80,384]{1,0:T(8,128)(2,1)S(1)}, bf16[80,384]{1,0:T(8,128)(2,1)S(1)}, u32[]{:S(2)}, u32[]{:S(2)}) collective-permute-start(bf16[80,384]{1,0:T(8,128)(2,1)S(1)} %get-tuple-element.22), channel_id=1, source_target_pairs={{1,0},{2,1},{3,2},{4,3},{5,4},{6,5},{7,6},{9,8},{10,9},{11,10},{12... | collective-permute-start | bytes 184328 | tf_op jit(solution)/shard_map/ppermute | solution.py:354
  7.2 0.0 copy-done
  7.2 0.0 copy-done.2
  7.2 0.0 copy-done.4
  7.2 0.0 copy-done.7
  7.3 0.0 copy-done.8
  7.3 0.0 copy-done.9
  7.3 0.8 %shard_map.122 = (f32[3,128,384]{2,1,0:T(8,128)S(1)}, f32[3,128,384]{2,1,0:T(8,128)S(1)}, f32[128,384]{1,0:T(8,128)S(1)}, bf16[256,192]{1,0:T(8,128)(2,1)S(1)}, ...) custom-call(f32[1,8]{1,0:T(1,128)S(1)} %bitcast.26, f32[1,8]{1,0:T(1,128)S(1)} %bitcast.28, ...), custom_call_target="tpu_custom_call" | custom-call | flops 6000000 | bytes 3000000 | tf_op jit(solution)/shard_map/pallas_call | solution.py:388
  8.1 0.0 collective-permute-done.before_ref
  8.1 2.8 %collective-permute-done.1.after_ref = bf16[80,384]{1,0:T(8,128)(2,1)S(1)} collective-permute-done((bf16[80,384]{1,0:T(8,128)(2,1)S(1)}, bf16[80,384]{1,0:T(8,128)(2,1)S(1)}, u32[]{:S(2)}, u32[]{:S(2)}) %collective-permute-start.1) | collective-permute-done | bytes 61472 | tf_op jit(solution)/shard_map/ppermute | solution.py:354
  10.9 0.1 shard_map.125
  10.9 5.1 %collective-permute-start.2 = (bf16[128,384]{1,0:T(8,128)(2,1)S(1)}, bf16[128,384]{1,0:T(8,128)(2,1)S(1)}, u32[]{:S(2)}, u32[]{:S(2)}) collective-permute-start(bf16[128,384]{1,0:T(8,128)(2,1)S(1)} %get-tuple-element.30), channel_id=1, source_target_pairs={{8,16},{16,8},{24,32},{32,24},{40,48},{48,40},{56,64},{64,56},{72,... | collective-permute-start | bytes 294920 | tf_op jit(solution)/shard_map/ppermute | solution.py:359
  16.1 6.4 %collective-permute-start.3 = (bf16[128,384]{1,0:T(8,128)(2,1)S(1)}, bf16[128,384]{1,0:T(8,128)(2,1)S(1)}, u32[]{:S(2)}, u32[]{:S(2)}) collective-permute-start(bf16[128,384]{1,0:T(8,128)(2,1)S(1)} %get-tuple-element.31), channel_id=1, source_target_pairs={{0,8},{8,0},{16,24},{24,16},{32,40},{40,32},{48,56},{56,48},{64,72... | collective-permute-start | bytes 294920 | tf_op jit(solution)/shard_map/ppermute | solution.py:360
  22.5 0.0 copy-start.3
  22.5 0.8 %shard_map.124 = (f32[3,128,384]{2,1,0:T(8,128)S(1)}, f32[12,8,384]{2,1,0:T(8,128)S(1)}, f32[3,64,384]{2,1,0:T(8,128)S(1)}, f32[256,128]{1,0:T(8,128)S(1)}) custom-call(f32[1,8]{1,0:T(1,128)S(1)} %bitcast.27, f32[1,8]{1,0:T(1,128)S(1)} %bitcast.29, f32[3,128,384]{2,1,0:T(8,128)S(1)} %bitcast.16, f32[3,128,384]{2,1,0:T(8,128)S(1)} %get-tuple-element.18.base_ref, ...), custom_call_target="tpu_custom_call" | custom-call | flops 4000000 | bytes 3000000 | tf_op jit(solution)/shard_map/pallas_call | solution.py:406
  23.3 0.0 collective-permute-done.2.far_ref
  23.3 0.1 collective-permute-done.3.pair_ref
  23.4 0.2 copy-done.3
  23.6 1.0 %shard_map.126 = (f32[3,64,384]{2,1,0:T(8,128)S(1)}, bf16[64,4,128]{2,1,0:T(4,128)(2,1)S(1)}) custom-call(f32[3,128,384]{2,1,0:T(8,128)S(1)} %bitcast.17, f32[3,128,384]{2,1,0:T(8,128)S(1)} %get-tuple-element.26.once_ref, f32[3,128,384]{2,1,0:T(8,128)S(1)} %get-tuple-element.19.scaled_ref, f32[128,384]{1,0:T(8,128)S(1)} %get-tuple-element.20.coupling_ref, ...), custom_call_target="tpu_custom_call" | custom-call | tf_op jit(solution)/shard_map/pallas_call | solution.py:415
  24.6 0.0 copy-start.1
  24.6 0.0 copy-start.6
  24.6 14.2 %all_to_all.10.got_ref = bf16[64,4,128]{2,1,0:T(4,128)(2,1)S(1)} all-to-all(bf16[64,4,128]{2,1,0:T(4,128)(2,1)S(1)} %get-tuple-element.33), channel_id=1, replica_groups={{388,389,390,391,384,385,386,387,396,397,398,399,392,393,394,395,404,40..., dimensions={0} | all-to-all | bytes 131072 | tf_op jit(solution)/shard_map/all_to_all | solution.py:425
  38.8 0.7 %shard_map.129 = bf16[12,8,128]{2,1,0:T(8,128)(2,1)} custom-call(bf16[64,4,128]{2,1,0:T(4,128)(2,1)S(1)} %all_to_all.10.got_ref), custom_call_target="tpu_custom_call" | custom-call | tf_op jit(solution)/shard_map/pallas_call | solution.py:426
  39.5 18.9 %all-to-all-start.1 = ((bf16[12,8,128]{2,1,0:T(8,128)(2,1)}), bf16[12,8,128]{2,1,0:T(8,128)(2,1)S(1)}, u32[]{:S(2)}, u32[]{:S(2)}) async-start(bf16[12,8,128]{2,1,0:T(8,128)(2,1)} %shard_map.129), calls=%async_computation.1 | async-start | bytes 49152 | tf_op jit(solution)/shard_map/all_to_all | solution.py:433
  59.0 0.0 copy-start.5
  59.1 0.9 %shard_map.127 = f32[3,128,384]{2,1,0:T(8,128)} custom-call(f32[3,64,384]{2,1,0:T(8,128)S(1)} %get-tuple-element.25.inner_ref, f32[3,64,384]{2,1,0:T(8,128)S(1)} %get-tuple-element.32.edges_ref), custom_call_target="tpu_custom_call" | custom-call | bytes 600000 | tf_op jit(solution)/shard_map/pallas_call | solution.py:434
  59.9 0.0 copy-done.1
  59.9 0.0 copy-done.6
  60.0 0.4 shard_map.128.part_ref
  60.4 0.0 all-to-all-done.1.relay_ref
  60.4 0.1 copy-done.5
  60.4 0.9 %shard_map.130 = f32[1,256]{1,0:T(1,128)} custom-call(s32[1,9]{1,0:T(1,128)S(1)} %bitcast.25, s32[1,1]{1,0:T(1,128)} %bitcast.13.rank_ref, f32[1,256]{1,0:T(1,128)S(1)} %shard_map.128.part_ref, bf16[12,8,128]{2,1,0:T(8,128)(2,1)S(1)} %all-to-all-done.1.relay_ref, bf16[2304,256]{1,0:T(8,128)(2,1)S(1)} %bitcast.19, bf16[16,256]{1,0:T(8,128)(2,1)S(1)} %bitcast.23), custom_call_target="tpu_custom_call" | custom-call | tf_op jit(solution)/shard_map/pallas_call | solution.py:453
Async XLA Ops:
  0.6 6.6 %copy-start = (f32[3,8,16,384]{3,2,1,0:T(8,128)S(1)}, f32[3,8,16,384]{3,2,1,0:T(8,128)}, u32[]{:S(2)}) copy-start(f32[3,8,16,384]{3,2,1,0:T(8,128)} %field_hbm.1) | copy-start | bytes 1769476
  0.6 6.6 %copy-start.2 = (f32[3,8,16,384]{3,2,1,0:T(8,128)S(1)}, f32[3,8,16,384]{3,2,1,0:T(8,128)}, u32[]{:S(2)}) copy-start(f32[3,8,16,384]{3,2,1,0:T(8,128)} %source_hbm.1) | copy-start | bytes 1769476
  0.7 6.6 %copy-start.4 = (s32[8,16,384]{2,1,0:T(8,128)S(1)}, s32[8,16,384]{2,1,0:T(8,128)}, u32[]{:S(2)}) copy-start(s32[8,16,384]{2,1,0:T(8,128)} %material_hbm.1) | copy-start | bytes 589828
  0.7 6.6 %copy-start.7 = (f32[8]{0:T(128)S(1)}, f32[8]{0:T(128)}, u32[]{:S(2)}) copy-start(f32[8]{0:T(128)} %param.14) | copy-start | bytes 100
  0.7 6.6 %copy-start.8 = (f32[8]{0:T(128)S(1)}, f32[8]{0:T(128)}, u32[]{:S(2)}) copy-start(f32[8]{0:T(128)} %param.15) | copy-start | bytes 100
  0.7 6.6 %copy-start.9 = (s32[1,1,256]{2,1,0:T(1,128)S(1)}, s32[1,1,256]{2,1,0:T(1,128)}, u32[]{:S(2)}) copy-start(s32[1,1,256]{2,1,0:T(1,128)} %param.16) | copy-start | bytes 3076
  1.9 6.2 %collective-permute-start = (bf16[80,384]{1,0:T(8,128)(2,1)S(1)}, bf16[80,384]{1,0:T(8,128)(2,1)S(1)}, u32[]{:S(2)}, u32[]{:S(2)}) collective-permute-start(bf16[80,384]{1,0:T(8,128)(2,1)S(1)} %get-tuple-element.21), channel_id=1, source_target_pairs={{0,1},{1,2},{2,3},{3,4},{4,5},{5,6},{6,7},{8,9},{9,10},{10,11},{11... | collective-permute-start | bytes 184328 | tf_op jit(solution)/shard_map/ppermute | solution.py:354
  5.9 5.0 %collective-permute-start.1 = (bf16[80,384]{1,0:T(8,128)(2,1)S(1)}, bf16[80,384]{1,0:T(8,128)(2,1)S(1)}, u32[]{:S(2)}, u32[]{:S(2)}) collective-permute-start(bf16[80,384]{1,0:T(8,128)(2,1)S(1)} %get-tuple-element.22), channel_id=1, source_target_pairs={{1,0},{2,1},{3,2},{4,3},{5,4},{6,5},{7,6},{9,8},{10,9},{11,10},{12... | collective-permute-start | bytes 184328 | tf_op jit(solution)/shard_map/ppermute | solution.py:354
  10.9 12.3 %collective-permute-start.2 = (bf16[128,384]{1,0:T(8,128)(2,1)S(1)}, bf16[128,384]{1,0:T(8,128)(2,1)S(1)}, u32[]{:S(2)}, u32[]{:S(2)}) collective-permute-start(bf16[128,384]{1,0:T(8,128)(2,1)S(1)} %get-tuple-element.30), channel_id=1, source_target_pairs={{8,16},{16,8},{24,32},{32,24},{40,48},{48,40},{56,64},{64,56},{72,... | collective-permute-start | bytes 294920 | tf_op jit(solution)/shard_map/ppermute | solution.py:359
  16.1 7.3 %collective-permute-start.3 = (bf16[128,384]{1,0:T(8,128)(2,1)S(1)}, bf16[128,384]{1,0:T(8,128)(2,1)S(1)}, u32[]{:S(2)}, u32[]{:S(2)}) collective-permute-start(bf16[128,384]{1,0:T(8,128)(2,1)S(1)} %get-tuple-element.31), channel_id=1, source_target_pairs={{0,8},{8,0},{16,24},{24,16},{32,40},{40,32},{48,56},{56,48},{64,72... | collective-permute-start | bytes 294920 | tf_op jit(solution)/shard_map/ppermute | solution.py:360
  22.5 1.1 %copy-start.3 = (bf16[16,96,1,1,256]{4,1,3,2,0:T(8,128)(2,1)S(1)}, bf16[16,96,1,1,256]{4,1,3,2,0:T(8,128)(2,1)}, u32[]{:S(2)}) copy-start(bf16[16,96,1,1,256]{4,1,3,2,0:T(8,128)(2,1)} %param.20) | copy-start | bytes 2359300
  24.6 35.3 %copy-start.1 = (bf16[1,1,9,256,256]{4,3,2,1,0:T(8,128)(2,1)S(1)}, bf16[1,1,9,256,256]{4,3,2,1,0:T(8,128)(2,1)}, u32[]{:S(2)}) copy-start(bf16[1,1,9,256,256]{4,3,2,1,0:T(8,128)(2,1)} %param.17) | copy-start | bytes 3538948
  24.6 35.3 %copy-start.6 = (s32[1,1,9]{2,1,0:T(1,128)S(1)}, s32[1,1,9]{2,1,0:T(1,128)}, u32[]{:S(2)}) copy-start(s32[1,1,9]{2,1,0:T(1,128)} %param.18) | copy-start | bytes 112
  39.5 20.8 %all-to-all-start.1 = ((bf16[12,8,128]{2,1,0:T(8,128)(2,1)}), bf16[12,8,128]{2,1,0:T(8,128)(2,1)S(1)}, u32[]{:S(2)}, u32[]{:S(2)}) async-start(bf16[12,8,128]{2,1,0:T(8,128)(2,1)} %shard_map.129), calls=%async_computation.1 | async-start | bytes 49152 | tf_op jit(solution)/shard_map/all_to_all | solution.py:433
  59.0 1.4 %copy-start.5 = (bf16[16,1,1,256]{3,0,2,1:T(8,128)(2,1)S(1)}, bf16[16,1,1,256]{3,0,2,1:T(8,128)(2,1)}, u32[]{:S(2)}) copy-start(bf16[16,1,1,256]{3,0,2,1:T(8,128)(2,1)} %param.19) | copy-start | bytes 24580

commit v11 on v7

--- a/solution.py
+++ b/solution.py
@@ -284,7 +284,7 @@
     for half in range(2):
         packet = stacked([high[half:half + 1, :], low[half:half + 1, :]] + relay, 8).astype(BF16)
         for z in range(8 * half, min(8 * half + 8, send_ref.shape[0])):
-            send_ref[seat(z, send_ref.shape[0])] = packet
+            send_ref[seat(z - 1, send_ref.shape[0])] = packet
 
 
 def masked_rows(rows, factors):
@@ -321,7 +321,7 @@
     upward = across == PLANE - 1
     start = jnp.where(upward, plane + 1, plane - 1)
     edge = ((across == 0) | upward) & (start >= 0) & (start < planes)
-    packet = jnp.where(edge, relay_ref[seated(start, planes)].astype(F32), 0.0)
+    packet = jnp.where(edge, relay_ref[lax.rem(seated(start, planes) + planes - 1, planes)].astype(F32), 0.0)
     rows = [(packet[2 + 2 * b:3 + 2 * b, :], packet[3 + 2 * b:4 + 2 * b, :]) for b in range(3)]
     first = jnp.where(upward, 6, 0)
     blocks = near_ref[pl.ds(pl.multiple_of(256 * first, 256), 768), :]
@@ -421,7 +421,7 @@
         compiler_params=params,
     )(field, once, scaled, coupling, rim, edge, place, spread, far, pair, far_right.reshape(-1, 256))
     ids = np.arange(slabs * tiles).reshape(planes, PLANE, tiles)
-    ids = np.roll(ids, (-(planes // 2), -(PLANE // 2), -(tiles // 2)), axis=(0, 1, 2)).reshape(planes, members)
+    ids = np.roll(ids, (-(planes // 2) - 1, -(PLANE // 2), -(tiles // 2)), axis=(0, 1, 2)).reshape(planes, members)
     got = lax.all_to_all(send, BOTH, 0, 0, axis_index_groups=ids.tolist(), tiled=True)
     send = pl.pallas_call(
         functools.partial(middle, tiles),

time: 61.2 us -> 61 us (level)
  starting transfers between devices: 36.5 us -> 35.6 us
    all_to_all x1, starting transfers between devices: 19.7 us -> 18.8 us  [local(): lax.all_to_all(send, BOTH, 0, 0, axis_index_groups=ids.T.tolist(), tiled=...]
  transfers between devices with their start and end apart: 5 -> 5, of which waited for: 2 -> 3; matrix products, arithmetic and copies ran while one was open for 0% -> 0% of each run, Pallas kernels for 5% -> 5%
where the time goes in v11:
time: 61 us; the launch traced here: 60.3 us
  starting transfers between devices  35.6 us (58%)
  blocking collectives  12.8 us (21%)
  Pallas kernels  6.67 us (11%)
  waiting for transfers between devices  3.43 us (6%)
  between operations  1.52 us (2%)
    all_to_all x1, starting transfers between devices, local(): lax.all_to_all(send, BOTH, 0, 0, axis_index_groups=ids.T.tolist(), tiled=...  18.8 us
    all_to_all x1, blocking collectives, local(): lax.all_to_all(send, BOTH, 0, 0, axis_index_groups=ids.tolist(), tiled=True)  12.8 us
    ppermute x1, starting transfers between devices, swap(): return (far, lax.ppermute(pair, axis, [(i, i ^ 1) for i in range(devices)]))  6.39 us
    ppermute x2, starting transfers between devices, exchange(): return (lax.ppermute(last, axis, up), lax.ppermute(first, axis, down))  5.33 us
    ppermute x1, starting transfers between devices, swap(): lax.ppermute(far, axis, [(i, i + 1 if i % 2 else i - 1) for i in range(1,...  5.11 us
    ppermute x2, waiting for transfers between devices, exchange(): return (lax.ppermute(last, axis, up), lax.ppermute(first, axis, down))  2.8 us
  transfers between devices with their start and end apart: 5, of which 3 were waited for; matrix products, arithmetic and copies ran while one was open for 0% of the time, Pallas kernels for 5%

profile of v11, /device:TPU:1, one launch (start us, length us, event | category | flops | bytes accessed | tf_op | source)
XLA Modules:
  0.0 60.3 jit_solution(3388343227625154423)
XLA Ops:
  0.6 0.0 copy-start
  0.6 0.0 copy-start.2
  0.7 0.0 copy-start.4
  0.7 0.0 copy-start.7
  0.7 0.0 copy-start.8
  0.7 0.0 copy-start.9
  0.7 1.2 %shard_map.123 = (bf16[80,384]{1,0:T(8,128)(2,1)S(1)}, bf16[80,384]{1,0:T(8,128)(2,1)S(1)}) custom-call(f32[3,8,16,384]{3,2,1,0:T(8,128)} %field_hbm.1, f32[3,8,16,384]{3,2,1,0:T(8,128)} %source_hbm.1, s32[8,16,384]{2,1,0:T(8,128)} %material_hbm.1), custom_call_target="tpu_custom_call" | custom-call | tf_op jit(solution)/shard_map/pallas_call | solution.py:370
  1.9 4.0 %collective-permute-start = (bf16[80,384]{1,0:T(8,128)(2,1)S(1)}, bf16[80,384]{1,0:T(8,128)(2,1)S(1)}, u32[]{:S(2)}, u32[]{:S(2)}) collective-permute-start(bf16[80,384]{1,0:T(8,128)(2,1)S(1)} %get-tuple-element.21), channel_id=1, source_target_pairs={{0,1},{1,2},{2,3},{3,4},{4,5},{5,6},{6,7},{8,9},{9,10},{10,11},{11... | collective-permute-start | bytes 184328 | tf_op jit(solution)/shard_map/ppermute | solution.py:354
  5.9 1.3 %collective-permute-start.1 = (bf16[80,384]{1,0:T(8,128)(2,1)S(1)}, bf16[80,384]{1,0:T(8,128)(2,1)S(1)}, u32[]{:S(2)}, u32[]{:S(2)}) collective-permute-start(bf16[80,384]{1,0:T(8,128)(2,1)S(1)} %get-tuple-element.22), channel_id=1, source_target_pairs={{1,0},{2,1},{3,2},{4,3},{5,4},{6,5},{7,6},{9,8},{10,9},{11,10},{12... | collective-permute-start | bytes 184328 | tf_op jit(solution)/shard_map/ppermute | solution.py:354
  7.2 0.0 copy-done
  7.2 0.0 copy-done.2
  7.2 0.0 copy-done.4
  7.2 0.0 copy-done.7
  7.3 0.0 copy-done.8
  7.3 0.0 copy-done.9
  7.3 0.8 %shard_map.122 = (f32[3,128,384]{2,1,0:T(8,128)S(1)}, f32[3,128,384]{2,1,0:T(8,128)S(1)}, f32[128,384]{1,0:T(8,128)S(1)}, bf16[256,192]{1,0:T(8,128)(2,1)S(1)}, ...) custom-call(f32[1,8]{1,0:T(1,128)S(1)} %bitcast.26, f32[1,8]{1,0:T(1,128)S(1)} %bitcast.28, ...), custom_call_target="tpu_custom_call" | custom-call | flops 6000000 | bytes 3000000 | tf_op jit(solution)/shard_map/pallas_call | solution.py:388
  8.1 0.0 collective-permute-done.before_ref
  8.1 2.8 %collective-permute-done.1.after_ref = bf16[80,384]{1,0:T(8,128)(2,1)S(1)} collective-permute-done((bf16[80,384]{1,0:T(8,128)(2,1)S(1)}, bf16[80,384]{1,0:T(8,128)(2,1)S(1)}, u32[]{:S(2)}, u32[]{:S(2)}) %collective-permute-start.1) | collective-permute-done | bytes 61472 | tf_op jit(solution)/shard_map/ppermute | solution.py:354
  10.9 0.1 shard_map.125
  10.9 5.1 %collective-permute-start.2 = (bf16[128,384]{1,0:T(8,128)(2,1)S(1)}, bf16[128,384]{1,0:T(8,128)(2,1)S(1)}, u32[]{:S(2)}, u32[]{:S(2)}) collective-permute-start(bf16[128,384]{1,0:T(8,128)(2,1)S(1)} %get-tuple-element.30), channel_id=1, source_target_pairs={{8,16},{16,8},{24,32},{32,24},{40,48},{48,40},{56,64},{64,56},{72,... | collective-permute-start | bytes 294920 | tf_op jit(solution)/shard_map/ppermute | solution.py:359
  16.1 6.4 %collective-permute-start.3 = (bf16[128,384]{1,0:T(8,128)(2,1)S(1)}, bf16[128,384]{1,0:T(8,128)(2,1)S(1)}, u32[]{:S(2)}, u32[]{:S(2)}) collective-permute-start(bf16[128,384]{1,0:T(8,128)(2,1)S(1)} %get-tuple-element.31), channel_id=1, source_target_pairs={{0,8},{8,0},{16,24},{24,16},{32,40},{40,32},{48,56},{56,48},{64,72... | collective-permute-start | bytes 294920 | tf_op jit(solution)/shard_map/ppermute | solution.py:360
  22.5 0.0 copy-start.3
  22.5 0.8 %shard_map.124 = (f32[3,128,384]{2,1,0:T(8,128)S(1)}, f32[12,8,384]{2,1,0:T(8,128)S(1)}, f32[3,64,384]{2,1,0:T(8,128)S(1)}, f32[256,128]{1,0:T(8,128)S(1)}) custom-call(f32[1,8]{1,0:T(1,128)S(1)} %bitcast.27, f32[1,8]{1,0:T(1,128)S(1)} %bitcast.29, f32[3,128,384]{2,1,0:T(8,128)S(1)} %bitcast.16, f32[3,128,384]{2,1,0:T(8,128)S(1)} %get-tuple-element.18.base_ref, ...), custom_call_target="tpu_custom_call" | custom-call | flops 4000000 | bytes 3000000 | tf_op jit(solution)/shard_map/pallas_call | solution.py:406
  23.3 0.0 collective-permute-done.2.far_ref
  23.3 0.1 collective-permute-done.3.pair_ref
  23.4 0.2 copy-done.3
  23.6 1.0 %shard_map.126 = (f32[3,64,384]{2,1,0:T(8,128)S(1)}, bf16[64,4,128]{2,1,0:T(4,128)(2,1)S(1)}) custom-call(f32[3,128,384]{2,1,0:T(8,128)S(1)} %bitcast.17, f32[3,128,384]{2,1,0:T(8,128)S(1)} %get-tuple-element.26.once_ref, f32[3,128,384]{2,1,0:T(8,128)S(1)} %get-tuple-element.19.scaled_ref, f32[128,384]{1,0:T(8,128)S(1)} %get-tuple-element.20.coupling_ref, ...), custom_call_target="tpu_custom_call" | custom-call | tf_op jit(solution)/shard_map/pallas_call | solution.py:415
  24.6 0.0 copy-start.1
  24.6 0.0 copy-start.6
  24.6 12.8 %all_to_all.10.got_ref = bf16[64,4,128]{2,1,0:T(4,128)(2,1)S(1)} all-to-all(bf16[64,4,128]{2,1,0:T(4,128)(2,1)S(1)} %get-tuple-element.33), channel_id=1, replica_groups={{484,485,486,487,480,481,482,483,492,493,494,495,488,489,490,491,500,50..., dimensions={0} | all-to-all | bytes 131072 | tf_op jit(solution)/shard_map/all_to_all | solution.py:425
  37.4 0.7 %shard_map.129 = bf16[12,8,128]{2,1,0:T(8,128)(2,1)} custom-call(bf16[64,4,128]{2,1,0:T(4,128)(2,1)S(1)} %all_to_all.10.got_ref), custom_call_target="tpu_custom_call" | custom-call | tf_op jit(solution)/shard_map/pallas_call | solution.py:426
  38.1 18.8 %all-to-all-start.1 = ((bf16[12,8,128]{2,1,0:T(8,128)(2,1)}), bf16[12,8,128]{2,1,0:T(8,128)(2,1)S(1)}, u32[]{:S(2)}, u32[]{:S(2)}) async-start(bf16[12,8,128]{2,1,0:T(8,128)(2,1)} %shard_map.129), calls=%async_computation.1 | async-start | bytes 49152 | tf_op jit(solution)/shard_map/all_to_all | solution.py:433
  57.5 0.0 copy-start.5
  57.5 0.9 %shard_map.127 = f32[3,128,384]{2,1,0:T(8,128)} custom-call(f32[3,64,384]{2,1,0:T(8,128)S(1)} %get-tuple-element.25.inner_ref, f32[3,64,384]{2,1,0:T(8,128)S(1)} %get-tuple-element.32.edges_ref), custom_call_target="tpu_custom_call" | custom-call | bytes 600000 | tf_op jit(solution)/shard_map/pallas_call | solution.py:434
  58.4 0.0 copy-done.1
  58.4 0.0 copy-done.6
  58.4 0.4 shard_map.128.part_ref
  58.8 0.5 all-to-all-done.1.relay_ref
  59.4 0.0 copy-done.5
  59.4 0.9 %shard_map.130 = f32[1,256]{1,0:T(1,128)} custom-call(s32[1,9]{1,0:T(1,128)S(1)} %bitcast.25, s32[1,1]{1,0:T(1,128)} %bitcast.13.rank_ref, f32[1,256]{1,0:T(1,128)S(1)} %shard_map.128.part_ref, bf16[12,8,128]{2,1,0:T(8,128)(2,1)S(1)} %all-to-all-done.1.relay_ref, bf16[2304,256]{1,0:T(8,128)(2,1)S(1)} %bitcast.19, bf16[16,256]{1,0:T(8,128)(2,1)S(1)} %bitcast.23), custom_call_target="tpu_custom_call" | custom-call | tf_op jit(solution)/shard_map/pallas_call | solution.py:453
Async XLA Ops:
  0.6 6.6 %copy-start = (f32[3,8,16,384]{3,2,1,0:T(8,128)S(1)}, f32[3,8,16,384]{3,2,1,0:T(8,128)}, u32[]{:S(2)}) copy-start(f32[3,8,16,384]{3,2,1,0:T(8,128)} %field_hbm.1) | copy-start | bytes 1769476
  0.6 6.6 %copy-start.2 = (f32[3,8,16,384]{3,2,1,0:T(8,128)S(1)}, f32[3,8,16,384]{3,2,1,0:T(8,128)}, u32[]{:S(2)}) copy-start(f32[3,8,16,384]{3,2,1,0:T(8,128)} %source_hbm.1) | copy-start | bytes 1769476
  0.7 6.6 %copy-start.4 = (s32[8,16,384]{2,1,0:T(8,128)S(1)}, s32[8,16,384]{2,1,0:T(8,128)}, u32[]{:S(2)}) copy-start(s32[8,16,384]{2,1,0:T(8,128)} %material_hbm.1) | copy-start | bytes 589828
  0.7 6.6 %copy-start.7 = (f32[8]{0:T(128)S(1)}, f32[8]{0:T(128)}, u32[]{:S(2)}) copy-start(f32[8]{0:T(128)} %param.14) | copy-start | bytes 100
  0.7 6.6 %copy-start.8 = (f32[8]{0:T(128)S(1)}, f32[8]{0:T(128)}, u32[]{:S(2)}) copy-start(f32[8]{0:T(128)} %param.15) | copy-start | bytes 100
  0.7 6.6 %copy-start.9 = (s32[1,1,256]{2,1,0:T(1,128)S(1)}, s32[1,1,256]{2,1,0:T(1,128)}, u32[]{:S(2)}) copy-start(s32[1,1,256]{2,1,0:T(1,128)} %param.16) | copy-start | bytes 3076
  1.9 6.2 %collective-permute-start = (bf16[80,384]{1,0:T(8,128)(2,1)S(1)}, bf16[80,384]{1,0:T(8,128)(2,1)S(1)}, u32[]{:S(2)}, u32[]{:S(2)}) collective-permute-start(bf16[80,384]{1,0:T(8,128)(2,1)S(1)} %get-tuple-element.21), channel_id=1, source_target_pairs={{0,1},{1,2},{2,3},{3,4},{4,5},{5,6},{6,7},{8,9},{9,10},{10,11},{11... | collective-permute-start | bytes 184328 | tf_op jit(solution)/shard_map/ppermute | solution.py:354
  5.9 5.0 %collective-permute-start.1 = (bf16[80,384]{1,0:T(8,128)(2,1)S(1)}, bf16[80,384]{1,0:T(8,128)(2,1)S(1)}, u32[]{:S(2)}, u32[]{:S(2)}) collective-permute-start(bf16[80,384]{1,0:T(8,128)(2,1)S(1)} %get-tuple-element.22), channel_id=1, source_target_pairs={{1,0},{2,1},{3,2},{4,3},{5,4},{6,5},{7,6},{9,8},{10,9},{11,10},{12... | collective-permute-start | bytes 184328 | tf_op jit(solution)/shard_map/ppermute | solution.py:354
  10.9 12.3 %collective-permute-start.2 = (bf16[128,384]{1,0:T(8,128)(2,1)S(1)}, bf16[128,384]{1,0:T(8,128)(2,1)S(1)}, u32[]{:S(2)}, u32[]{:S(2)}) collective-permute-start(bf16[128,384]{1,0:T(8,128)(2,1)S(1)} %get-tuple-element.30), channel_id=1, source_target_pairs={{8,16},{16,8},{24,32},{32,24},{40,48},{48,40},{56,64},{64,56},{72,... | collective-permute-start | bytes 294920 | tf_op jit(solution)/shard_map/ppermute | solution.py:359
  16.1 7.3 %collective-permute-start.3 = (bf16[128,384]{1,0:T(8,128)(2,1)S(1)}, bf16[128,384]{1,0:T(8,128)(2,1)S(1)}, u32[]{:S(2)}, u32[]{:S(2)}) collective-permute-start(bf16[128,384]{1,0:T(8,128)(2,1)S(1)} %get-tuple-element.31), channel_id=1, source_target_pairs={{0,8},{8,0},{16,24},{24,16},{32,40},{40,32},{48,56},{56,48},{64,72... | collective-permute-start | bytes 294920 | tf_op jit(solution)/shard_map/ppermute | solution.py:360
  22.5 1.1 %copy-start.3 = (bf16[16,96,1,1,256]{4,1,3,2,0:T(8,128)(2,1)S(1)}, bf16[16,96,1,1,256]{4,1,3,2,0:T(8,128)(2,1)}, u32[]{:S(2)}) copy-start(bf16[16,96,1,1,256]{4,1,3,2,0:T(8,128)(2,1)} %param.20) | copy-start | bytes 2359300
  24.6 33.8 %copy-start.1 = (bf16[1,1,9,256,256]{4,3,2,1,0:T(8,128)(2,1)S(1)}, bf16[1,1,9,256,256]{4,3,2,1,0:T(8,128)(2,1)}, u32[]{:S(2)}) copy-start(bf16[1,1,9,256,256]{4,3,2,1,0:T(8,128)(2,1)} %param.17) | copy-start | bytes 3538948
  24.6 33.8 %copy-start.6 = (s32[1,1,9]{2,1,0:T(1,128)S(1)}, s32[1,1,9]{2,1,0:T(1,128)}, u32[]{:S(2)}) copy-start(s32[1,1,9]{2,1,0:T(1,128)} %param.18) | copy-start | bytes 112
  38.1 21.2 %all-to-all-start.1 = ((bf16[12,8,128]{2,1,0:T(8,128)(2,1)}), bf16[12,8,128]{2,1,0:T(8,128)(2,1)S(1)}, u32[]{:S(2)}, u32[]{:S(2)}) async-start(bf16[12,8,128]{2,1,0:T(8,128)(2,1)} %shard_map.129), calls=%async_computation.1 | async-start | bytes 49152 | tf_op jit(solution)/shard_map/all_to_all | solution.py:433
  57.5 1.8 %copy-start.5 = (bf16[16,1,1,256]{3,0,2,1:T(8,128)(2,1)S(1)}, bf16[16,1,1,256]{3,0,2,1:T(8,128)(2,1)}, u32[]{:S(2)}) copy-start(bf16[16,1,1,256]{3,0,2,1:T(8,128)(2,1)} %param.19) | copy-start | bytes 24580

commit v12 on v11

--- a/solution.py
+++ b/solution.py
@@ -284,7 +284,7 @@
     for half in range(2):
         packet = stacked([high[half:half + 1, :], low[half:half + 1, :]] + relay, 8).astype(BF16)
         for z in range(8 * half, min(8 * half + 8, send_ref.shape[0])):
-            send_ref[seat(z - 1, send_ref.shape[0])] = packet
+            send_ref[seat(z - 2, send_ref.shape[0])] = packet
 
 
 def masked_rows(rows, factors):
@@ -321,7 +321,7 @@
     upward = across == PLANE - 1
     start = jnp.where(upward, plane + 1, plane - 1)
     edge = ((across == 0) | upward) & (start >= 0) & (start < planes)
-    packet = jnp.where(edge, relay_ref[lax.rem(seated(start, planes) + planes - 1, planes)].astype(F32), 0.0)
+    packet = jnp.where(edge, relay_ref[lax.rem(seated(start, planes) + planes - 2, planes)].astype(F32), 0.0)
     rows = [(packet[2 + 2 * b:3 + 2 * b, :], packet[3 + 2 * b:4 + 2 * b, :]) for b in range(3)]
     first = jnp.where(upward, 6, 0)
     blocks = near_ref[pl.ds(pl.multiple_of(256 * first, 256), 768), :]
@@ -421,7 +421,7 @@
         compiler_params=params,
     )(field, once, scaled, coupling, rim, edge, place, spread, far, pair, far_right.reshape(-1, 256))
     ids = np.arange(slabs * tiles).reshape(planes, PLANE, tiles)
-    ids = np.roll(ids, (-(planes // 2) - 1, -(PLANE // 2), -(tiles // 2)), axis=(0, 1, 2)).reshape(planes, members)
+    ids = np.roll(ids, (-(planes // 2) - 2, -(PLANE // 2), -(tiles // 2)), axis=(0, 1, 2)).reshape(planes, members)
     got = lax.all_to_all(send, BOTH, 0, 0, axis_index_groups=ids.tolist(), tiled=True)
     send = pl.pallas_call(
         functools.partial(middle, tiles),

time: 61 us -> 61 us (level)
  waiting for transfers between devices: 3.43 us -> 5.62 us
  starting transfers between devices: 35.6 us -> 33.8 us
    all_to_all x1, waiting for transfers between devices: 0.51 us -> 2.71 us  [local(): lax.all_to_all(send, BOTH, 0, 0, axis_index_groups=ids.T.tolist(), tiled=...]
    all_to_all x1, starting transfers between devices: 18.8 us -> 16.9 us  [local(): lax.all_to_all(send, BOTH, 0, 0, axis_index_groups=ids.T.tolist(), tiled=...]
where the time goes in v12:
time: 61 us; the launch traced here: 60.6 us
  starting transfers between devices  33.8 us (55%)
  blocking collectives  12.8 us (21%)
  Pallas kernels  6.67 us (11%)
  waiting for transfers between devices  5.62 us (9%)
  between operations  1.52 us (2%)
    all_to_all x1, starting transfers between devices, local(): lax.all_to_all(send, BOTH, 0, 0, axis_index_groups=ids.T.tolist(), tiled=...  16.9 us
    all_to_all x1, blocking collectives, local(): lax.all_to_all(send, BOTH, 0, 0, axis_index_groups=ids.tolist(), tiled=True)  12.8 us
    ppermute x1, starting transfers between devices, swap(): return (far, lax.ppermute(pair, axis, [(i, i ^ 1) for i in range(devices)]))  6.39 us
    ppermute x2, starting transfers between devices, exchange(): return (lax.ppermute(last, axis, up), lax.ppermute(first, axis, down))  5.33 us
    ppermute x1, starting transfers between devices, swap(): lax.ppermute(far, axis, [(i, i + 1 if i % 2 else i - 1) for i in range(1,...  5.11 us
    ppermute x2, waiting for transfers between devices, exchange(): return (lax.ppermute(last, axis, up), lax.ppermute(first, axis, down))  2.8 us
    all_to_all x1, waiting for transfers between devices, local(): lax.all_to_all(send, BOTH, 0, 0, axis_index_groups=ids.T.tolist(), tiled=...  2.71 us
  transfers between devices with their start and end apart: 5, of which 3 were waited for; matrix products, arithmetic and copies ran while one was open for 0% of the time, Pallas kernels for 5%

profile of v12, /device:TPU:1, one launch (start us, length us, event | category | flops | bytes accessed | tf_op | source)
XLA Modules:
  0.0 60.6 jit_solution(7441466300888194358)
XLA Ops:
  0.6 0.0 copy-start
  0.6 0.0 copy-start.2
  0.7 0.0 copy-start.4
  0.7 0.0 copy-start.7
  0.7 0.0 copy-start.8
  0.7 0.0 copy-start.9
  0.7 1.2 %shard_map.123 = (bf16[80,384]{1,0:T(8,128)(2,1)S(1)}, bf16[80,384]{1,0:T(8,128)(2,1)S(1)}) custom-call(f32[3,8,16,384]{3,2,1,0:T(8,128)} %field_hbm.1, f32[3,8,16,384]{3,2,1,0:T(8,128)} %source_hbm.1, s32[8,16,384]{2,1,0:T(8,128)} %material_hbm.1), custom_call_target="tpu_custom_call" | custom-call | tf_op jit(solution)/shard_map/pallas_call | solution.py:370
  1.9 4.0 %collective-permute-start = (bf16[80,384]{1,0:T(8,128)(2,1)S(1)}, bf16[80,384]{1,0:T(8,128)(2,1)S(1)}, u32[]{:S(2)}, u32[]{:S(2)}) collective-permute-start(bf16[80,384]{1,0:T(8,128)(2,1)S(1)} %get-tuple-element.21), channel_id=1, source_target_pairs={{0,1},{1,2},{2,3},{3,4},{4,5},{5,6},{6,7},{8,9},{9,10},{10,11},{11... | collective-permute-start | bytes 184328 | tf_op jit(solution)/shard_map/ppermute | solution.py:354
  5.9 1.3 %collective-permute-start.1 = (bf16[80,384]{1,0:T(8,128)(2,1)S(1)}, bf16[80,384]{1,0:T(8,128)(2,1)S(1)}, u32[]{:S(2)}, u32[]{:S(2)}) collective-permute-start(bf16[80,384]{1,0:T(8,128)(2,1)S(1)} %get-tuple-element.22), channel_id=1, source_target_pairs={{1,0},{2,1},{3,2},{4,3},{5,4},{6,5},{7,6},{9,8},{10,9},{11,10},{12... | collective-permute-start | bytes 184328 | tf_op jit(solution)/shard_map/ppermute | solution.py:354
  7.2 0.0 copy-done
  7.2 0.0 copy-done.2
  7.2 0.0 copy-done.4
  7.2 0.0 copy-done.7
  7.3 0.0 copy-done.8
  7.3 0.0 copy-done.9
  7.3 0.8 %shard_map.122 = (f32[3,128,384]{2,1,0:T(8,128)S(1)}, f32[3,128,384]{2,1,0:T(8,128)S(1)}, f32[128,384]{1,0:T(8,128)S(1)}, bf16[256,192]{1,0:T(8,128)(2,1)S(1)}, ...) custom-call(f32[1,8]{1,0:T(1,128)S(1)} %bitcast.26, f32[1,8]{1,0:T(1,128)S(1)} %bitcast.28, ...), custom_call_target="tpu_custom_call" | custom-call | flops 6000000 | bytes 3000000 | tf_op jit(solution)/shard_map/pallas_call | solution.py:388
  8.1 0.0 collective-permute-done.before_ref
  8.1 2.8 %collective-permute-done.1.after_ref = bf16[80,384]{1,0:T(8,128)(2,1)S(1)} collective-permute-done((bf16[80,384]{1,0:T(8,128)(2,1)S(1)}, bf16[80,384]{1,0:T(8,128)(2,1)S(1)}, u32[]{:S(2)}, u32[]{:S(2)}) %collective-permute-start.1) | collective-permute-done | bytes 61472 | tf_op jit(solution)/shard_map/ppermute | solution.py:354
  10.9 0.1 shard_map.125
  10.9 5.1 %collective-permute-start.2 = (bf16[128,384]{1,0:T(8,128)(2,1)S(1)}, bf16[128,384]{1,0:T(8,128)(2,1)S(1)}, u32[]{:S(2)}, u32[]{:S(2)}) collective-permute-start(bf16[128,384]{1,0:T(8,128)(2,1)S(1)} %get-tuple-element.30), channel_id=1, source_target_pairs={{8,16},{16,8},{24,32},{32,24},{40,48},{48,40},{56,64},{64,56},{72,... | collective-permute-start | bytes 294920 | tf_op jit(solution)/shard_map/ppermute | solution.py:359
  16.1 6.4 %collective-permute-start.3 = (bf16[128,384]{1,0:T(8,128)(2,1)S(1)}, bf16[128,384]{1,0:T(8,128)(2,1)S(1)}, u32[]{:S(2)}, u32[]{:S(2)}) collective-permute-start(bf16[128,384]{1,0:T(8,128)(2,1)S(1)} %get-tuple-element.31), channel_id=1, source_target_pairs={{0,8},{8,0},{16,24},{24,16},{32,40},{40,32},{48,56},{56,48},{64,72... | collective-permute-start | bytes 294920 | tf_op jit(solution)/shard_map/ppermute | solution.py:360
  22.5 0.0 copy-start.3
  22.5 0.8 %shard_map.124 = (f32[3,128,384]{2,1,0:T(8,128)S(1)}, f32[12,8,384]{2,1,0:T(8,128)S(1)}, f32[3,64,384]{2,1,0:T(8,128)S(1)}, f32[256,128]{1,0:T(8,128)S(1)}) custom-call(f32[1,8]{1,0:T(1,128)S(1)} %bitcast.27, f32[1,8]{1,0:T(1,128)S(1)} %bitcast.29, f32[3,128,384]{2,1,0:T(8,128)S(1)} %bitcast.16, f32[3,128,384]{2,1,0:T(8,128)S(1)} %get-tuple-element.18.base_ref, ...), custom_call_target="tpu_custom_call" | custom-call | flops 4000000 | bytes 3000000 | tf_op jit(solution)/shard_map/pallas_call | solution.py:406
  23.3 0.0 collective-permute-done.2.far_ref
  23.3 0.1 collective-permute-done.3.pair_ref
  23.4 0.2 copy-done.3
  23.6 1.0 %shard_map.126 = (f32[3,64,384]{2,1,0:T(8,128)S(1)}, bf16[64,4,128]{2,1,0:T(4,128)(2,1)S(1)}) custom-call(f32[3,128,384]{2,1,0:T(8,128)S(1)} %bitcast.17, f32[3,128,384]{2,1,0:T(8,128)S(1)} %get-tuple-element.26.once_ref, f32[3,128,384]{2,1,0:T(8,128)S(1)} %get-tuple-element.19.scaled_ref, f32[128,384]{1,0:T(8,128)S(1)} %get-tuple-element.20.coupling_ref, ...), custom_call_target="tpu_custom_call" | custom-call | tf_op jit(solution)/shard_map/pallas_call | solution.py:415
  24.6 0.0 copy-start.1
  24.6 0.0 copy-start.6
  24.6 12.8 %all_to_all.10.got_ref = bf16[64,4,128]{2,1,0:T(4,128)(2,1)S(1)} all-to-all(bf16[64,4,128]{2,1,0:T(4,128)(2,1)S(1)} %get-tuple-element.33), channel_id=1, replica_groups={{548,549,550,551,544,545,546,547,556,557,558,559,552,553,554,555,564,56..., dimensions={0} | all-to-all | bytes 131072 | tf_op jit(solution)/shard_map/all_to_all | solution.py:425
  37.4 0.7 %shard_map.129 = bf16[12,8,128]{2,1,0:T(8,128)(2,1)} custom-call(bf16[64,4,128]{2,1,0:T(4,128)(2,1)S(1)} %all_to_all.10.got_ref), custom_call_target="tpu_custom_call" | custom-call | tf_op jit(solution)/shard_map/pallas_call | solution.py:426
  38.1 16.9 %all-to-all-start.1 = ((bf16[12,8,128]{2,1,0:T(8,128)(2,1)}), bf16[12,8,128]{2,1,0:T(8,128)(2,1)S(1)}, u32[]{:S(2)}, u32[]{:S(2)}) async-start(bf16[12,8,128]{2,1,0:T(8,128)(2,1)} %shard_map.129), calls=%async_computation.1 | async-start | bytes 49152 | tf_op jit(solution)/shard_map/all_to_all | solution.py:433
  55.7 0.0 copy-start.5
  55.7 0.9 %shard_map.127 = f32[3,128,384]{2,1,0:T(8,128)} custom-call(f32[3,64,384]{2,1,0:T(8,128)S(1)} %get-tuple-element.25.inner_ref, f32[3,64,384]{2,1,0:T(8,128)S(1)} %get-tuple-element.32.edges_ref), custom_call_target="tpu_custom_call" | custom-call | bytes 600000 | tf_op jit(solution)/shard_map/pallas_call | solution.py:434
  56.6 0.0 copy-done.1
  56.6 0.0 copy-done.6
  56.6 0.4 shard_map.128.part_ref
  57.0 2.7 %all-to-all-done.1.relay_ref = bf16[12,8,128]{2,1,0:T(8,128)(2,1)S(1)} async-done(((bf16[12,8,128]{2,1,0:T(8,128)(2,1)}), bf16[12,8,128]{2,1,0:T(8,128)(2,1)S(1)}, u32[]{:S(2)}, u32[]{:S(2)}) %all-to-all-start.1) | async-done | bytes 24608 | tf_op jit(solution)/shard_map/all_to_all | solution.py:433
  59.7 0.0 copy-done.5
  59.7 0.9 %shard_map.130 = f32[1,256]{1,0:T(1,128)} custom-call(s32[1,9]{1,0:T(1,128)S(1)} %bitcast.25, s32[1,1]{1,0:T(1,128)} %bitcast.13.rank_ref, f32[1,256]{1,0:T(1,128)S(1)} %shard_map.128.part_ref, bf16[12,8,128]{2,1,0:T(8,128)(2,1)S(1)} %all-to-all-done.1.relay_ref, bf16[2304,256]{1,0:T(8,128)(2,1)S(1)} %bitcast.19, bf16[16,256]{1,0:T(8,128)(2,1)S(1)} %bitcast.23), custom_call_target="tpu_custom_call" | custom-call | tf_op jit(solution)/shard_map/pallas_call | solution.py:453
Async XLA Ops:
  0.6 6.6 %copy-start = (f32[3,8,16,384]{3,2,1,0:T(8,128)S(1)}, f32[3,8,16,384]{3,2,1,0:T(8,128)}, u32[]{:S(2)}) copy-start(f32[3,8,16,384]{3,2,1,0:T(8,128)} %field_hbm.1) | copy-start | bytes 1769476
  0.6 6.6 %copy-start.2 = (f32[3,8,16,384]{3,2,1,0:T(8,128)S(1)}, f32[3,8,16,384]{3,2,1,0:T(8,128)}, u32[]{:S(2)}) copy-start(f32[3,8,16,384]{3,2,1,0:T(8,128)} %source_hbm.1) | copy-start | bytes 1769476
  0.7 6.6 %copy-start.4 = (s32[8,16,384]{2,1,0:T(8,128)S(1)}, s32[8,16,384]{2,1,0:T(8,128)}, u32[]{:S(2)}) copy-start(s32[8,16,384]{2,1,0:T(8,128)} %material_hbm.1) | copy-start | bytes 589828
  0.7 6.6 %copy-start.7 = (f32[8]{0:T(128)S(1)}, f32[8]{0:T(128)}, u32[]{:S(2)}) copy-start(f32[8]{0:T(128)} %param.14) | copy-start | bytes 100
  0.7 6.6 %copy-start.8 = (f32[8]{0:T(128)S(1)}, f32[8]{0:T(128)}, u32[]{:S(2)}) copy-start(f32[8]{0:T(128)} %param.15) | copy-start | bytes 100
  0.7 6.6 %copy-start.9 = (s32[1,1,256]{2,1,0:T(1,128)S(1)}, s32[1,1,256]{2,1,0:T(1,128)}, u32[]{:S(2)}) copy-start(s32[1,1,256]{2,1,0:T(1,128)} %param.16) | copy-start | bytes 3076
  1.9 6.2 %collective-permute-start = (bf16[80,384]{1,0:T(8,128)(2,1)S(1)}, bf16[80,384]{1,0:T(8,128)(2,1)S(1)}, u32[]{:S(2)}, u32[]{:S(2)}) collective-permute-start(bf16[80,384]{1,0:T(8,128)(2,1)S(1)} %get-tuple-element.21), channel_id=1, source_target_pairs={{0,1},{1,2},{2,3},{3,4},{4,5},{5,6},{6,7},{8,9},{9,10},{10,11},{11... | collective-permute-start | bytes 184328 | tf_op jit(solution)/shard_map/ppermute | solution.py:354
  5.9 5.0 %collective-permute-start.1 = (bf16[80,384]{1,0:T(8,128)(2,1)S(1)}, bf16[80,384]{1,0:T(8,128)(2,1)S(1)}, u32[]{:S(2)}, u32[]{:S(2)}) collective-permute-start(bf16[80,384]{1,0:T(8,128)(2,1)S(1)} %get-tuple-element.22), channel_id=1, source_target_pairs={{1,0},{2,1},{3,2},{4,3},{5,4},{6,5},{7,6},{9,8},{10,9},{11,10},{12... | collective-permute-start | bytes 184328 | tf_op jit(solution)/shard_map/ppermute | solution.py:354
  10.9 12.3 %collective-permute-start.2 = (bf16[128,384]{1,0:T(8,128)(2,1)S(1)}, bf16[128,384]{1,0:T(8,128)(2,1)S(1)}, u32[]{:S(2)}, u32[]{:S(2)}) collective-permute-start(bf16[128,384]{1,0:T(8,128)(2,1)S(1)} %get-tuple-element.30), channel_id=1, source_target_pairs={{8,16},{16,8},{24,32},{32,24},{40,48},{48,40},{56,64},{64,56},{72,... | collective-permute-start | bytes 294920 | tf_op jit(solution)/shard_map/ppermute | solution.py:359
  16.1 7.3 %collective-permute-start.3 = (bf16[128,384]{1,0:T(8,128)(2,1)S(1)}, bf16[128,384]{1,0:T(8,128)(2,1)S(1)}, u32[]{:S(2)}, u32[]{:S(2)}) collective-permute-start(bf16[128,384]{1,0:T(8,128)(2,1)S(1)} %get-tuple-element.31), channel_id=1, source_target_pairs={{0,8},{8,0},{16,24},{24,16},{32,40},{40,32},{48,56},{56,48},{64,72... | collective-permute-start | bytes 294920 | tf_op jit(solution)/shard_map/ppermute | solution.py:360
  22.5 1.1 %copy-start.3 = (bf16[16,96,1,1,256]{4,1,3,2,0:T(8,128)(2,1)S(1)}, bf16[16,96,1,1,256]{4,1,3,2,0:T(8,128)(2,1)}, u32[]{:S(2)}) copy-start(bf16[16,96,1,1,256]{4,1,3,2,0:T(8,128)(2,1)} %param.20) | copy-start | bytes 2359300
  24.6 32.0 %copy-start.1 = (bf16[1,1,9,256,256]{4,3,2,1,0:T(8,128)(2,1)S(1)}, bf16[1,1,9,256,256]{4,3,2,1,0:T(8,128)(2,1)}, u32[]{:S(2)}) copy-start(bf16[1,1,9,256,256]{4,3,2,1,0:T(8,128)(2,1)} %param.17) | copy-start | bytes 3538948
  24.6 32.0 %copy-start.6 = (s32[1,1,9]{2,1,0:T(1,128)S(1)}, s32[1,1,9]{2,1,0:T(1,128)}, u32[]{:S(2)}) copy-start(s32[1,1,9]{2,1,0:T(1,128)} %param.18) | copy-start | bytes 112
  38.1 21.6 %all-to-all-start.1 = ((bf16[12,8,128]{2,1,0:T(8,128)(2,1)}), bf16[12,8,128]{2,1,0:T(8,128)(2,1)S(1)}, u32[]{:S(2)}, u32[]{:S(2)}) async-start(bf16[12,8,128]{2,1,0:T(8,128)(2,1)} %shard_map.129), calls=%async_computation.1 | async-start | bytes 49152 | tf_op jit(solution)/shard_map/all_to_all | solution.py:433
  55.7 4.0 %copy-start.5 = (bf16[16,1,1,256]{3,0,2,1:T(8,128)(2,1)S(1)}, bf16[16,1,1,256]{3,0,2,1:T(8,128)(2,1)}, u32[]{:S(2)}) copy-start(bf16[16,1,1,256]{3,0,2,1:T(8,128)(2,1)} %param.19) | copy-start | bytes 24580
